TPU v7x, 32 devices: a whole 2x2x4 slice. The times are simulated.
32 devices in a mesh: dp: 8 (over y, x, core), tensor: 4 (over z).
Axes of the slice: x: 2, y: 2, z: 4, core: 2. Of those that a mesh axis runs over, the one named last changes fastest.
Arguments:
- tokens_in: bfloat16 [8192, 1024], P(('dp', 'tensor')), may hold values from -6 to 6
- out_grad: bfloat16 [8192, 1024], P(('dp', 'tensor')), may hold values from -6 to 6
- attn_gain: bfloat16 [1024], P('dp'), may hold values from 0.5 to 1.5
- w_query: bfloat16 [1024, 1024], P('dp', 'tensor'), may hold values from -0.1875 to 0.1875
- w_key: bfloat16 [1024, 1024], P('dp', 'tensor'), may hold values from -0.1875 to 0.1875
- w_value: bfloat16 [1024, 1024], P('dp', 'tensor'), may hold values from -0.1875 to 0.1875
- w_output: bfloat16 [1024, 1024], P('tensor', 'dp'), may hold values from -0.75 to 0.75
- rel_table: float32 [16, 32], P('tensor'), may hold values from -4 to 4
- moe_gain: bfloat16 [1024], P('dp'), may hold values from 0.5 to 1.5
- w_router: bfloat16 [1024, 4], P('dp'), may hold values from -0.125 to 0.125
- w_gate: bfloat16 [4, 1024, 2816], P(None, 'dp', 'tensor'), may hold values from -0.1875 to 0.1875
- w_up: bfloat16 [4, 1024, 2816], P(None, 'dp', 'tensor'), may hold values from -0.1875 to 0.1875
- down_weight: bfloat16 [4, 2816, 1024], P(None, 'tensor', 'dp'), may hold values from -0.3125 to 0.3125
- expert_ids: int32 [8192, 2], P('dp'), may hold values from 0 to 3, as said below
- piece_starts: int32 [8, 2], P('dp'), may hold values from 0 to 768, as said below
Outputs:
- out_rows: bfloat16 [8192, 1024], P(('dp', 'tensor'))
- in_grad: float32 [8192, 1024], P(('dp', 'tensor'))
- grad_attn_gain: float32 [1024], P(('dp', 'tensor'))
- grad_w_query: float32 [1024, 1024], P('dp', 'tensor')
- grad_w_key: float32 [1024, 1024], P('dp', 'tensor')
- grad_w_value: float32 [1024, 1024], P('dp', 'tensor')
- grad_w_output: float32 [1024, 1024], P('tensor', 'dp')
- grad_rel_table: float32 [16, 32], P('tensor')
- grad_moe_gain: float32 [1024], P(('dp', 'tensor'))
- grad_w_router: float32 [1024, 4], P(('dp', 'tensor'))
- gate_weight_gradient: float32 [4, 1024, 2816], P(None, 'dp', 'tensor')
- grad_w_up: float32 [4, 1024, 2816], P(None, 'dp', 'tensor')
- grad_w_down: float32 [4, 2816, 1024], P(None, 'tensor', 'dp')
Inputs may be any that keep to these rules, and one draw needn't show every extreme that they name: `expert_ids`: the two experts of a token differ. Within the tokens of each index of dp, one expert, which one drawn from the seed, is among the two choices of exactly 768 tokens. `piece_starts`: in each sequence the k-th of the 2 pieces lies wholly inside the k-th of 2 equal parts of the sequence; positions count from the sequence's start. Some sequence's first piece starts at position 0 and some sequence's last piece ends at the sequence's end.
All inputs are finite; a program needn't handle non-finite values.
Results may differ from a plain program's by a relative error of at most 0.02.
Values may be sent and summed in bfloat16 or wider, within the bound.
No kernel may reach another device: no remote copies, remote signals or barrier semaphores. Data moves between devices by JAX's collectives and lax.ppermute only.
A program may use at most 256 MiB of HBM per device.

v0:
```python
import functools

import jax
import jax.numpy as jnp
import numpy as np
from jax import lax
from jax.experimental import pallas as pl
from jax.experimental.pallas import tpu as pltpu
from jax.sharding import PartitionSpec as P

EXPERTS = 4
PIECE = 256
CAP = 640
BUCKETS = 32
EPSILON = 1e-06
PRECISE = lax.Precision.HIGHEST
LIMITS = (12, 16, 23, 32, 46, 64, 91)
MASKED = -1e30
BF = jnp.bfloat16
F32 = jnp.float32
BLOCK = 256
VMEM_LIMIT = 56 * 1024 * 1024


def params(semantics=None):
    return pltpu.CompilerParams(dimension_semantics=semantics, vmem_limit_bytes=VMEM_LIMIT)


def dot_nn(a, b):
    return lax.dot_general(a, b, (((1,), (0,)), ((), ())), preferred_element_type=F32)


def dot_nt(a, b):
    return lax.dot_general(a, b, (((1,), (1,)), ((), ())), preferred_element_type=F32)


def dot_tn(a, b):
    return lax.dot_general(a, b, (((0,), (0,)), ((), ())), preferred_element_type=F32)


def bucket_of(offsets):
    distance = np.abs(offsets)
    far = np.full_like(distance, 8)
    for bound in LIMITS:
        far = far + (distance >= bound)
    return np.where(distance < 8, distance, far) + np.where(offsets > 0, 16, 0)


def onehot_of(offsets):
    return (bucket_of(offsets)[..., None] == np.arange(BUCKETS)).astype(np.float32)


def cost(flops, nbytes):
    return pl.CostEstimate(flops=int(flops), bytes_accessed=int(nbytes), transcendentals=0)


def vspec():
    return pl.BlockSpec(memory_space=pltpu.VMEM)


def sspec():
    return pl.BlockSpec(memory_space=pltpu.SMEM)


def z_swap(x, mask, size):
    return lax.ppermute(x, "tensor", [(i, i ^ mask) for i in range(size)])


def z_gather(x, size):
    near = z_swap(x, 1, size)
    far = z_swap(x, 2, size)
    return [x, near, far, z_swap(far, 1, size)]


def z_direct(parts, size):
    return [parts[0]] + [z_swap(parts[mask], mask, size) for mask in range(1, size)]


def z_reduce(parts, size):
    passed = z_swap(parts[3], 1, size)
    far = z_swap((parts[2].astype(F32) + passed.astype(F32)).astype(BF), 2, size)
    return [parts[0], z_swap(parts[1], 1, size), far]


def after(x, *others):
    return lax.optimization_barrier((x,) + others)[0]


def dp_slots(ranks):
    return ((ranks >> 1) & 3) | ((ranks & 1) << 2)


def dp_step(x, bit):
    other = lax.ppermute(x, "dp", [(i, i ^ bit) for i in range(8)])
    return jnp.concatenate([x, other], 0)


def dp_fold(keep, send, bit):
    other = lax.ppermute(send, "dp", [(i, i ^ bit) for i in range(8)])
    return (keep.astype(F32) + other.astype(F32)).astype(keep.dtype)


def halves(x):
    return x[: x.shape[0] // 2], x[x.shape[0] // 2 :]


def dp_scatter_slots(ranks):
    return ((ranks >> 2) & 1) | (((ranks >> 1) & 1) << 1) | ((ranks & 1) << 2)


def parted(keep_ref, send_ref, order_ref):
    half = keep_ref.shape[0]
    for j in range(2 * half if half > 1 else 1):
        yield (keep_ref if j < half else send_ref), j % half, order_ref[j]


def join_rows(ref, index_ref, count, rows):
    if count == 1:
        return ref[0, 0:rows, :]
    return jnp.concatenate([ref[index_ref[c], 0:rows, :] for c in range(count)], 0)


def qkv_body(count, chunks, rows, index_ref, place_ref, *refs):
    toks = refs[:chunks]
    pack_ref, small_ref = refs[chunks : chunks + 2]
    n1_ref, q_ref, k_ref, v_ref, kt_ref, vt_ref, gains_ref, router_ref = refs[chunks + 2 :]
    depth = n1_ref.shape[1] // count
    weights = join_rows(pack_ref, index_ref, count, depth)
    width = q_ref.shape[1]
    if count == 1:
        small = [small_ref[r : r + 1, :] for r in range(2 + EXPERTS)]
    else:
        lines = [small_ref[index_ref[d], depth : depth + 1, :].astype(F32) for d in range(count)]
        small = [
            jnp.concatenate([x[:, depth * r : depth * (r + 1)] for x in lines], 1) for r in range(2 + EXPERTS)
        ]
    small = jnp.concatenate([x.astype(F32) for x in small] + [jnp.zeros((2, depth * count), F32)], 0)
    gains_ref[...] = small
    routers = jnp.concatenate([small[2:], jnp.zeros((10, depth * count), F32)], 0)
    router_ref[...] = jnp.zeros_like(router_ref)
    router_ref[0:16, :] = routers.astype(BF)
    gain = small[0:1, :]
    for c in range(chunks):
        at = pl.ds(pl.multiple_of(place_ref[c] * rows, rows), rows)
        x = toks[c][...].astype(F32)
        scale = lax.rsqrt(jnp.mean(x * x, axis=1, keepdims=True) + EPSILON)
        normed = (x * scale * gain).astype(BF)
        n1_ref[at, :] = normed
        out = dot_nn(normed, weights)
        q_ref[at, :] = (out[:, :width].astype(BF).astype(F32) * 0.125).astype(BF)
        key = out[:, width : 2 * width]
        value = out[:, 2 * width :]
        k_ref[at, :] = key.astype(BF)
        v_ref[at, :] = value.astype(BF)
        kt_ref[:, at] = jnp.transpose(key).astype(BF)
        vt_ref[:, at] = jnp.transpose(value).astype(BF)


def qkv_call(index, place, toks, pack, small, width):
    chunks, rows, depth = len(toks), toks[0].shape[0], toks[0].shape[1]
    total = chunks * rows
    shapes = [(total, depth)] + [(total, width)] * 3 + [(width, total)] * 2
    return pl.pallas_call(
        functools.partial(qkv_body, pack.shape[0], chunks, rows),
        in_specs=[sspec(), sspec()] + [vspec()] * (chunks + 2),
        out_specs=[vspec()] * 8,
        out_shape=[jax.ShapeDtypeStruct(s, BF) for s in shapes]
        + [jax.ShapeDtypeStruct((8, depth), F32), jax.ShapeDtypeStruct((128, depth), BF)],
        compiler_params=params(),
        cost_estimate=cost(2 * total * depth * 3 * width, 8 * total * depth),
        name="norm_qkv",
    )(index, place, *toks, pack, small)


def extents(total):
    blocks = total // BLOCK
    return [(i, min(BLOCK * (i + 2), total)) for i in range(blocks)]


def fwd_body(total, chunks, starts_ref, place_ref, q_ref, k_ref, vt_ref, line_ref, p_ref, ot_ref, *refs):
    atts = refs[:chunks]
    strip_ref, mask_ref, all_ref = refs[chunks:]
    head = pl.program_id(0)
    heads = pl.num_programs(0)
    blocks = total // BLOCK
    width = q_ref.shape[1]
    dim = width // 4

    @pl.when(head == 0)
    def _():
        def label(pos):
            first = (pos >= starts_ref[0, 0]) & (pos < starts_ref[0, 0] + PIECE)
            second = (pos >= starts_ref[0, 1]) & (pos < starts_ref[0, 1] + PIECE)
            return first, second

        for i in range(blocks):
            for j in (i, i + 1):
                if j >= blocks:
                    continue
                kpos = lax.broadcasted_iota(jnp.int32, (BLOCK, BLOCK), 0) + BLOCK * j
                qpos = lax.broadcasted_iota(jnp.int32, (BLOCK, BLOCK), 1) + BLOCK * i
                k1, k2 = label(kpos)
                q1, q2 = label(qpos)
                seen = (kpos <= qpos) | (k1 & q1) | (k2 & q2)
                mask_ref[2 * i + j - i] = jnp.where(seen, 0.0, MASKED)

    for beta in range(blocks + 1):
        start = BLOCK * (blocks - beta)
        window = line_ref[0, 0:1, start : start + 2 * BLOCK]
        spread = jnp.broadcast_to(window, (BLOCK, 2 * BLOCK))
        rolled = pltpu.roll(spread, BLOCK + 1, 1, stride=1, stride_axis=0)
        strip_ref[BLOCK * beta : BLOCK * (beta + 1), :] = rolled[:, :BLOCK]

    lanes = lax.broadcasted_iota(jnp.int32, (BLOCK, width), 1)
    own = (lanes >= head * dim) & (lanes < (head + 1) * dim)
    at_head = pl.ds(pl.multiple_of(head * dim, dim), dim)
    for i, extent in extents(total):
        q_rows = q_ref[BLOCK * i : BLOCK * (i + 1), :]
        q_own = jnp.where(own, q_rows, jnp.zeros_like(q_rows))
        base = BLOCK * (blocks - 1 - i)
        scores = dot_nt(k_ref[0:extent, :], q_own) + strip_ref[base : base + extent, :]
        parts = [scores[BLOCK * j : BLOCK * (j + 1)] for j in range(extent // BLOCK)]
        for j in (i, i + 1):
            if j < blocks:
                parts[j] = parts[j] + mask_ref[2 * i + j - i]
        top = functools.reduce(jnp.maximum, parts)
        top = jnp.max(top, axis=0, keepdims=True)
        parts = [jnp.exp(part - top) for part in parts]
        total_sum = jnp.sum(functools.reduce(jnp.add, parts), axis=0, keepdims=True)
        inverse = 1.0 / total_sum
        chances = jnp.concatenate([(part * inverse).astype(BF) for part in parts], 0)
        p_ref[0, 0:extent, BLOCK * i : BLOCK * (i + 1)] = chances
        ot_ref[at_head, BLOCK * i : BLOCK * (i + 1)] = dot_nn(vt_ref[at_head, 0:extent], chances)

    @pl.when(head == heads - 1)
    def _():
        mixed = ot_ref[...]
        all_ref[...] = jnp.transpose(mixed).astype(BF)
        rows = total // chunks
        for c in range(chunks):
            at = pl.ds(pl.multiple_of(place_ref[c] * rows, rows), rows)
            atts[c][...] = all_ref[at, :]


def attn_fwd(starts, place, chunks, q, k, vt, line):
    total, width = q.shape
    heads = line.shape[0]
    blocks = total // BLOCK
    whole = lambda shape: pl.BlockSpec(shape, lambda h: (0,) * len(shape))
    return pl.pallas_call(
        functools.partial(fwd_body, total, chunks),
        grid=(heads,),
        in_specs=[
            sspec(),
            sspec(),
            whole((total, width)),
            whole((total, width)),
            whole((width, total)),
            pl.BlockSpec((1, 1, line.shape[2]), lambda h: (h, 0, 0)),
        ],
        out_specs=[
            pl.BlockSpec((1, total, total), lambda h: (h, 0, 0)),
            whole((width, total)),
        ]
        + [whole((total // chunks, width))] * chunks,
        out_shape=[
            jax.ShapeDtypeStruct((heads, total, total), BF),
            jax.ShapeDtypeStruct((width, total), F32),
        ]
        + [jax.ShapeDtypeStruct((total // chunks, width), BF)] * chunks,
        scratch_shapes=[
            pltpu.VMEM((BLOCK * (blocks + 1), BLOCK), F32),
            pltpu.VMEM((2 * blocks, BLOCK, BLOCK), F32),
            pltpu.VMEM((total, width), BF),
        ],
        compiler_params=params(("arbitrary",)),
        cost_estimate=cost(heads * 4 * total * total * width, 10 * total * total),
        name="attn_forward",
    )(starts, place, q, k, vt, line)


def diagonal_sums(acc):
    half = BLOCK // 2
    low, high = acc[:half], acc[half:]
    rows = jnp.concatenate(
        [high[:, :half], high[:, half:] + low[:, :half], low[:, half:], jnp.zeros((half, half), F32)], 1
    )
    step = half // 2
    while step >= 8:
        rows = rows[step:] + pltpu.roll(rows[:step], step, 1)
        step //= 2
    index = lax.broadcasted_iota(jnp.int32, rows.shape, 0)
    for step in (4, 2, 1):
        rows = jnp.where((index & step) == 0, pltpu.roll(rows, step, 1), rows)
    return jnp.sum(rows, axis=0, keepdims=True)


def bwd_body(total, chunks, place_ref, *refs):
    grads = refs[:chunks]
    p_ref, q_ref, k_ref, v_ref, kt_ref, ot_ref = refs[chunks : chunks + 6]
    dq_ref, dk_ref, dv_ref, diag_ref = refs[chunks + 6 : chunks + 10]
    do_ref, dot_ref, dqt_ref, dka_ref, dva_ref, ds_ref, acc_ref = refs[chunks + 10 :]
    head = pl.program_id(0)
    heads = pl.num_programs(0)
    blocks = total // BLOCK
    rows = total // chunks
    width = q_ref.shape[1]
    dim = width // 4

    @pl.when(head == 0)
    def _():
        for c in range(chunks):
            at = pl.ds(pl.multiple_of(place_ref[c] * rows, rows), rows)
            do_ref[at, :] = grads[c][...]
        dot_ref[...] = jnp.transpose(do_ref[...].astype(F32))
        dka_ref[...] = jnp.zeros_like(dka_ref)
        dva_ref[...] = jnp.zeros_like(dva_ref)

    at_head = pl.ds(pl.multiple_of(head * dim, dim), dim)
    inner = jnp.sum(dot_ref[at_head, :] * ot_ref[at_head, :], axis=0, keepdims=True)
    lanes = lax.broadcasted_iota(jnp.int32, (total, width), 1)
    own = (lanes >= head * dim) & (lanes < (head + 1) * dim)
    q_own = jnp.where(own, q_ref[...], jnp.zeros_like(q_ref))
    do_own = jnp.where(own, do_ref[...], jnp.zeros_like(do_ref))
    written = 0
    for i, extent in reversed(extents(total)):
        cols = slice(BLOCK * i, BLOCK * (i + 1))
        chance_grad = dot_nt(v_ref[0:extent, :], do_own[cols, :])
        chances = p_ref[0, 0:extent, cols].astype(F32)
        score_grad = (chances * (chance_grad - inner[:, cols])).astype(BF)
        ds_ref[0:extent, cols] = score_grad
        dqt_ref[at_head, cols] = dot_nn(kt_ref[at_head, 0:extent], score_grad)
        base = BLOCK * (blocks - 1 - i)
        wide = score_grad.astype(F32)
        if i == blocks - 1:
            acc_ref[0:extent, :] = wide
            written = extent
        else:
            old = written - base
            acc_ref[base:written, :] += wide[:old]
            if base + extent > written:
                acc_ref[written : base + extent, :] = wide[old:]
                written = base + extent
    for j in range(blocks):
        first = max(0, BLOCK * (j - 1))
        keys = slice(BLOCK * j, BLOCK * (j + 1))
        dka_ref[keys, :] += dot_nn(ds_ref[keys, first:], q_own[first:, :])
        dva_ref[keys, :] += dot_nn(p_ref[0, keys, first:], do_own[first:, :])
    for beta in range(blocks + 1):
        diag_ref[0, beta : beta + 1, :] = diagonal_sums(acc_ref[BLOCK * beta : BLOCK * (beta + 1), :])

    @pl.when(head == heads - 1)
    def _():
        dq_ref[...] = (jnp.transpose(dqt_ref[...]) * 0.125).astype(BF)
        dk_ref[...] = dka_ref[...].astype(BF)
        dv_ref[...] = dva_ref[...].astype(BF)


def attn_bwd(place, grads, chances, q, k, v, kt, ot):
    total, width = q.shape
    heads = chances.shape[0]
    blocks = total // BLOCK
    chunks = len(grads)
    whole = lambda shape: pl.BlockSpec(shape, lambda h: (0,) * len(shape))
    return pl.pallas_call(
        functools.partial(bwd_body, total, chunks),
        grid=(heads,),
        in_specs=[sspec()]
        + [whole(grads[0].shape)] * chunks
        + [pl.BlockSpec((1, total, total), lambda h: (h, 0, 0))]
        + [whole((total, width))] * 3
        + [whole((width, total))] * 2,
        out_specs=[whole((total, width))] * 3 + [pl.BlockSpec((1, blocks + 1, 2 * BLOCK), lambda h: (h, 0, 0))],
        out_shape=[jax.ShapeDtypeStruct((total, width), BF)] * 3
        + [jax.ShapeDtypeStruct((heads, blocks + 1, 2 * BLOCK), F32)],
        scratch_shapes=[
            pltpu.VMEM((total, width), BF),
            pltpu.VMEM((width, total), F32),
            pltpu.VMEM((width, total), F32),
            pltpu.VMEM((total, width), F32),
            pltpu.VMEM((total, width), F32),
            pltpu.VMEM((total, total), BF),
            pltpu.VMEM((BLOCK * (blocks + 1), BLOCK), F32),
        ],
        compiler_params=params(("arbitrary",)),
        cost_estimate=cost(heads * 160 * total * total * width, 10 * total * total),
        name="attn_backward",
    )(place, *grads, chances, q, k, v, kt, ot)


def join_lanes(ref, index_ref, count, slot):
    if count == 1:
        return ref[0, slot]
    return jnp.concatenate([ref[index_ref[c], slot] for c in range(count)], 1)


def mid_body(count, chunks, index_ref, *refs):
    atts = refs[:chunks]
    w_ref, tok_ref, gain_ref, mid_ref, n2_ref = refs[chunks:]
    u = tok_ref[...].astype(F32)
    for c in range(chunks):
        u = u + dot_nn(atts[c][...], join_lanes(w_ref, index_ref, count, c))
    mid_ref[...] = u
    scale = lax.rsqrt(jnp.mean(u * u, axis=1, keepdims=True) + EPSILON)
    n2_ref[...] = (u * scale * gain_ref[1:2, :]).astype(BF)


def mid_call(index, atts, w_out, tok, gains):
    chunks = len(atts)
    return pl.pallas_call(
        functools.partial(mid_body, w_out.shape[0], chunks),
        in_specs=[sspec()] + [vspec()] * (chunks + 3),
        out_specs=[vspec()] * 2,
        out_shape=[jax.ShapeDtypeStruct(tok.shape, F32), jax.ShapeDtypeStruct(tok.shape, BF)],
        compiler_params=params(),
        cost_estimate=cost(2 * tok.shape[0] * tok.shape[1] ** 2, 4 * tok.shape[1] ** 2),
        name="out_projection_norm",
    )(index, *atts, w_out, tok, gains)


def split_dot(a, b, dot):
    high = a.astype(BF)
    low = (a - high.astype(F32)).astype(BF)
    return dot(high, b) + dot(low, b)


def joined(ref, which):
    if ref.shape[0] == 1:
        return ref[0, which]
    return jnp.concatenate([ref[d, which] for d in range(ref.shape[0])], 1)


def units_body(chunks, unit, place_ref, *refs):
    n2s = refs[:chunks]
    gs = refs[chunks : 2 * chunks]
    sel_ref, rout_ref, w_ref = refs[2 * chunks : 2 * chunks + 3]
    hg_ref, gg_ref, ug_ref, lg_ref, rpart_ref = refs[2 * chunks + 3 : 2 * chunks + 8]
    n2_ref, g_ref, gate_ref, sum_ref, prob_ref, pick_ref = refs[2 * chunks + 8 :]
    step = pl.program_id(0)
    steps = pl.num_programs(0)
    rows = n2s[0].shape[0]
    tokens = chunks * rows
    lane = lax.broadcasted_iota(jnp.int32, (tokens, 128), 1)

    @pl.when(step == 0)
    def _():
        for c in range(chunks):
            n2_ref[rows * c : rows * (c + 1), :] = n2s[c][...]
            g_ref[rows * c : rows * (c + 1), :] = gs[c][...]
        logits = dot_nt(n2_ref[...], rout_ref[...])
        logits = jnp.where(lane < EXPERTS, logits, MASKED)
        raised = jnp.exp(logits - jnp.max(logits, axis=1, keepdims=True))
        prob_ref[...] = raised / jnp.sum(raised, axis=1, keepdims=True)
        for c in range(chunks):
            at = pl.ds(pl.multiple_of(place_ref[c] * rows, rows), rows)
            pick_ref[rows * c : rows * (c + 1), :] = sel_ref[at, :]
        gates = prob_ref[...] * pick_ref[...]
        for e in range(EXPERTS):
            one = jnp.sum(jnp.where(lane == e, gates, 0.0), axis=1, keepdims=True)
            gate_ref[e] = jnp.broadcast_to(one, (tokens, 128))
        sum_ref[...] = jnp.zeros_like(sum_ref)

    wg, wu, wd = joined(w_ref, 0), joined(w_ref, 1), joined(w_ref, 2)
    pre = dot_nt(n2_ref[...], jnp.concatenate([wg, wu], 0))
    gate_pre, up_pre = pre[:, : wg.shape[0]], pre[:, wg.shape[0] :]
    raw = dot_nt(g_ref[...], wd)
    c0 = float(np.sqrt(2.0 / np.pi))
    square = gate_pre * gate_pre
    th = jnp.tanh(gate_pre * (c0 + (c0 * 0.044715) * square))
    half = 0.5 + 0.5 * th
    act = gate_pre * half
    slope = half + gate_pre * (0.5 * c0 + (1.5 * c0 * 0.044715) * square) * (1.0 - th * th)
    hidden = act * up_pre
    prod = raw * hidden
    width = hg_ref.shape[1]
    e_low = (step * width) // unit
    e_high = (step * width + width - 1) // unit
    bound = jnp.where(e_high > e_low, unit * e_high - step * width, width)
    lows, highs = [], []
    for m in range(width // 128):
        is_low = lane + 128 * m < bound
        part = slice(128 * m, 128 * (m + 1))
        gate = jnp.where(is_low, gate_ref[e_low], gate_ref[e_high])
        lows.append(jnp.where(is_low, prod[:, part], 0.0))
        highs.append(prod[:, part] - lows[m])
        hg_ref[:, part] = (gate * hidden[:, part]).astype(BF)
        hidden_grad = gate * raw[:, part]
        gg_ref[:, part] = (hidden_grad * up_pre[:, part] * slope[:, part]).astype(BF)
        ug_ref[:, part] = (hidden_grad * act[:, part]).astype(BF)
    sum_ref[e_low] += functools.reduce(jnp.add, lows)

    @pl.when(e_high > e_low)
    def _():
        sum_ref[e_high] += functools.reduce(jnp.add, highs)

    @pl.when(step == steps - 1)
    def _():
        grad = jnp.zeros((tokens, 128), F32)
        for e in range(EXPERTS):
            grad = grad + jnp.where(lane == e, jnp.sum(sum_ref[e], axis=1, keepdims=True), 0.0)
        grad = grad * pick_ref[...]
        probs = prob_ref[...]
        logit_grad = probs * (grad - jnp.sum(probs * grad, axis=1, keepdims=True))
        lg_ref[...] = logit_grad
        rpart_ref[...] = split_dot(logit_grad, n2_ref[...], dot_tn)[0:8, :]


def units_call(place, n2s, gs, sel, router, weights, unit):
    chunks, rows, depth = len(n2s), n2s[0].shape[0], n2s[0].shape[1]
    count, _, ff, part = weights.shape
    tokens = chunks * rows
    whole = lambda shape: pl.BlockSpec(shape, lambda s: (0,) * len(shape))
    return pl.pallas_call(
        functools.partial(units_body, chunks, unit),
        grid=(ff // BLOCK,),
        in_specs=[sspec()]
        + [whole((rows, depth))] * (2 * chunks)
        + [whole(sel.shape), whole(router.shape), pl.BlockSpec((count, 3, BLOCK, part), lambda s: (0, 0, s, 0))],
        out_specs=[pl.BlockSpec((tokens, BLOCK), lambda s: (0, s))] * 3 + [whole((tokens, 128)), whole((8, depth))],
        out_shape=[jax.ShapeDtypeStruct((tokens, ff), BF)] * 3
        + [jax.ShapeDtypeStruct((tokens, 128), F32), jax.ShapeDtypeStruct((8, depth), F32)],
        scratch_shapes=[
            pltpu.VMEM((tokens, depth), BF),
            pltpu.VMEM((tokens, depth), BF),
            pltpu.VMEM((EXPERTS, tokens, 128), F32),
            pltpu.VMEM((EXPERTS, tokens, 128), F32),
            pltpu.VMEM((tokens, 128), F32),
            pltpu.VMEM((tokens, 128), F32),
        ],
        compiler_params=params(("arbitrary",)),
        cost_estimate=cost(6 * tokens * depth * ff, 6 * depth * ff + 12 * tokens * depth),
        name="expert_units",
    )(place, *n2s, *gs, sel, router, weights)


def product_body(terms, chunks, extra, *refs):
    xs = refs[:terms]
    ws = refs[terms : 2 * terms]
    at = 2 * terms + (2 if extra else 0)
    outs = refs[at : at + chunks]
    total = None
    for x, w in zip(xs, ws):
        term = dot_nn(x[...], joined(w, 0))
        total = term if total is None else total + term
    if extra:
        lg_ref, rout_ref = refs[2 * terms : 2 * terms + 2]
        total = total + split_dot(lg_ref[...], rout_ref[...], dot_nn)
    rows = outs[0].shape[0]
    for c in range(chunks):
        outs[c][...] = total[rows * c : rows * (c + 1)].astype(BF)


def product_call(xs, picks, weights, chunks, extra, name):
    tokens, ff = xs[0].shape
    count, _, _, part = weights.shape
    depth = count * part
    rows = tokens // chunks
    per = max(1, BLOCK // part)
    wide = min(part * per, BLOCK)
    whole = lambda shape: pl.BlockSpec(shape, lambda s: (0,) * len(shape))
    place_at = (lambda i, s: (s, i, 0, 0)) if count > 1 else (lambda i, s: (0, i, 0, s))
    w_specs = [pl.BlockSpec((min(per, count), 1, ff, wide // min(per, count)), functools.partial(place_at, i)) for i in picks]
    return pl.pallas_call(
        functools.partial(product_body, len(xs), chunks, bool(extra)),
        grid=(depth // wide,),
        in_specs=[whole((tokens, ff))] * len(xs)
        + w_specs
        + ([whole(extra[0].shape), pl.BlockSpec((128, wide), lambda s: (0, s))] if extra else []),
        out_specs=[pl.BlockSpec((rows, wide), lambda s: (0, s))] * chunks,
        out_shape=[jax.ShapeDtypeStruct((rows, depth), BF)] * chunks,
        compiler_params=params(("arbitrary",)),
        cost_estimate=cost(2 * len(xs) * tokens * depth * ff, 4 * len(xs) * depth * ff),
        name=name,
    )(*xs, *([weights] * len(xs)), *extra)


def wgrad_body(count, chunks, *refs):
    hg_ref, gg_ref, ug_ref = refs[:3]
    n2s = refs[3 : 3 + chunks]
    gs = refs[3 + chunks : 3 + 2 * chunks]
    out_ref, n2_ref, g_ref = refs[3 + 2 * chunks :]
    part = out_ref.shape[3]
    rows = n2s[0].shape[0]

    @pl.when(pl.program_id(0) == 0)
    def _():
        for c in range(chunks):
            n2_ref[rows * c : rows * (c + 1), :] = n2s[c][...]
            g_ref[rows * c : rows * (c + 1), :] = gs[c][...]

    width = hg_ref.shape[1]
    pair = dot_tn(jnp.concatenate([gg_ref[...], ug_ref[...]], 1), n2_ref[...]).astype(BF)
    down = dot_tn(hg_ref[...], g_ref[...]).astype(BF)
    for which, total in enumerate((pair[:width], pair[width:], down)):
        for d in range(count):
            out_ref[d, which] = total[:, part * d : part * (d + 1)]


def wgrad_call(count, kept, n2s, gs):
    tokens, ff = kept[0].shape
    chunks, rows, depth = len(n2s), n2s[0].shape[0], n2s[0].shape[1]
    whole = lambda shape: pl.BlockSpec(shape, lambda s: (0,) * len(shape))
    return pl.pallas_call(
        functools.partial(wgrad_body, count, chunks),
        grid=(ff // BLOCK,),
        in_specs=[pl.BlockSpec((tokens, BLOCK), lambda s: (0, s))] * 3 + [whole((rows, depth))] * (2 * chunks),
        out_specs=pl.BlockSpec((count, 3, BLOCK, depth // count), lambda s: (0, 0, s, 0)),
        out_shape=jax.ShapeDtypeStruct((count, 3, ff, depth // count), BF),
        scratch_shapes=[pltpu.VMEM((tokens, depth), BF), pltpu.VMEM((tokens, depth), BF)],
        compiler_params=params(("arbitrary",)),
        cost_estimate=cost(6 * tokens * depth * ff, 12 * depth * ff),
        name="expert_weight_grads",
    )(*kept, *n2s, *gs)


def norm_back(grad, u, gain):
    scale = lax.rsqrt(jnp.mean(u * u, axis=1, keepdims=True) + EPSILON)
    m = grad * gain
    back = scale * m - u * (scale * scale * scale) * jnp.mean(u * m, axis=1, keepdims=True)
    return back, jnp.sum(grad * u * scale, axis=0, keepdims=True)


def resid_body(count, chunks, terms, index_ref, *refs):
    parts = refs[:terms]
    mid_ref, g_ref, gains_ref, w_ref = refs[terms : terms + 4]
    rest = refs[terms + 4 :]
    resid_ref, aog_ref, gain_ref = rest[:3]
    dos = rest[3:]
    grad = functools.reduce(jnp.add, [p[...].astype(F32) for p in parts])
    back, gain_part = norm_back(grad, mid_ref[...], gains_ref[1:2, :])
    resid = g_ref[...].astype(F32) + back
    resid_ref[...] = resid
    low = resid.astype(BF)
    aog_ref[...] = low
    gain_ref[...] = jnp.broadcast_to(gain_part, gain_ref.shape)
    for c in range(chunks):
        dos[c][...] = dot_nt(low, join_lanes(w_ref, index_ref, count, c)).astype(BF)


def resid_call(index, parts, mid, grad, gains, w_out):
    chunks, terms = w_out.shape[1], len(parts)
    shape = mid.shape
    width = w_out.shape[2]
    return pl.pallas_call(
        functools.partial(resid_body, w_out.shape[0], chunks, terms),
        in_specs=[sspec()] + [vspec()] * (terms + 4),
        out_specs=[vspec()] * (3 + chunks),
        out_shape=[
            jax.ShapeDtypeStruct(shape, F32),
            jax.ShapeDtypeStruct(shape, BF),
            jax.ShapeDtypeStruct((8, shape[1]), F32),
        ]
        + [jax.ShapeDtypeStruct((shape[0], width), BF)] * chunks,
        compiler_params=params(),
        cost_estimate=cost(2 * shape[0] * shape[1] ** 2, 4 * shape[1] ** 2),
        name="resid_grad",
    )(index, *parts, mid, grad, gains, w_out)


def final_body(chunks, *refs):
    parts = refs[:chunks]
    tok_ref, resid_ref, gains_ref, out_ref = refs[chunks:]
    grad = functools.reduce(jnp.add, [p[...].astype(F32) for p in parts])
    back, _ = norm_back(grad, tok_ref[...].astype(F32), gains_ref[0:1, :])
    out_ref[...] = resid_ref[...] + back


def final_call(parts, tok, resid, gains):
    return pl.pallas_call(
        functools.partial(final_body, len(parts)),
        in_specs=[vspec()] * (len(parts) + 3),
        out_specs=vspec(),
        out_shape=jax.ShapeDtypeStruct(tok.shape, F32),
        compiler_params=params(),
        cost_estimate=cost(20 * tok.size, 12 * tok.size),
        name="in_grad",
    )(*parts, tok, resid, gains)


def proj_body(count, chunks, rows, index_ref, place_ref, dq_ref, dk_ref, dv_ref, pack_ref, two_ref, router_ref, *refs):
    toks = refs[:chunks]
    outs = refs[chunks : 2 * chunks]
    gain_ref = refs[2 * chunks]
    depth = outs[0].shape[1]
    width = dq_ref.shape[1]
    weights = join_rows(pack_ref, index_ref, count, depth // count)
    gain = jnp.zeros((1, depth), F32)
    for c in range(chunks):
        at = pl.ds(pl.multiple_of(place_ref[c] * rows, rows), rows)
        grad = dot_nt(dq_ref[at, :], weights[:, :width])
        grad = grad + dot_nt(dk_ref[at, :], weights[:, width : 2 * width])
        grad = grad + dot_nt(dv_ref[at, :], weights[:, 2 * width :])
        outs[c][...] = grad.astype(BF)
        x = toks[c][...].astype(F32)
        scale = lax.rsqrt(jnp.mean(x * x, axis=1, keepdims=True) + EPSILON)
        gain = gain + jnp.sum(grad * x * scale, axis=0, keepdims=True)
    blank = jnp.zeros((6 - EXPERTS, depth), F32)
    gain_ref[...] = jnp.concatenate([gain, two_ref[0:1, :], router_ref[0:EXPERTS, :], blank], 0)


def proj_call(index, place, dq, dk, dv, pack, gain_two, router_part, toks):
    chunks, rows, depth = len(toks), toks[0].shape[0], toks[0].shape[1]
    return pl.pallas_call(
        functools.partial(proj_body, pack.shape[0], chunks, rows),
        in_specs=[sspec(), sspec()] + [vspec()] * (6 + chunks),
        out_specs=[vspec()] * (chunks + 1),
        out_shape=[jax.ShapeDtypeStruct((rows, depth), BF)] * chunks + [jax.ShapeDtypeStruct((8, depth), F32)],
        compiler_params=params(),
        cost_estimate=cost(6 * chunks * rows * depth * dq.shape[1], 8 * chunks * rows * depth),
        name="projection_grads",
    )(index, place, dq, dk, dv, pack, gain_two, router_part, *toks)


def attn_weights_body(count, smalls, slot_ref, n1_ref, dq_ref, dk_ref, dv_ref, table_ref, *refs):
    keep_ref, send_ref, small_ref, *grad_refs = refs[smalls:]
    small_ref[...] = functools.reduce(jnp.add, [r[...] for r in refs[:smalls]])
    depth = n1_ref.shape[1]
    width = dq_ref.shape[1]
    part = depth // count
    normed = n1_ref[...]
    pieces = width // 128
    for ref, grad_ref in zip((dq_ref, dk_ref, dv_ref), grad_refs):
        grad_ref[...] = dot_tn(normed, ref[...]).astype(BF)
    for out_ref, slot, d in parted(keep_ref, send_ref, slot_ref):
        rows = pl.ds(pl.multiple_of(d * part, 128), part)
        for m, grad_ref in enumerate(grad_refs):
            for piece in range(pieces):
                at = (m * pieces + piece) * part
                out_ref[slot, at : at + part, :] = grad_ref[rows, 128 * piece : 128 * (piece + 1)]
        at = 3 * pieces * part
        value = jnp.concatenate([small_ref[:, rows], table_ref[...]], 0).astype(BF)
        out_ref[slot, at : at + 16, :] = value


def attn_weights_call(slots, n1, dq, dk, dv, table, smalls, count):
    total, depth = n1.shape
    width = dq.shape[1]
    part = depth // count
    return pl.pallas_call(
        functools.partial(attn_weights_body, count, len(smalls)),
        in_specs=[sspec()] + [vspec()] * (5 + len(smalls)),
        out_specs=[vspec()] * 2,
        out_shape=[jax.ShapeDtypeStruct((count // 2, 3 * width * part // 128 + 16, 128), BF)] * 2,
        scratch_shapes=[pltpu.VMEM((8, depth), F32)] + [pltpu.VMEM((depth, width), BF)] * 3,
        compiler_params=params(),
        cost_estimate=cost(6 * total * depth * width, 8 * total * depth),
        name="attn_weight_grads",
    )(slots, n1, dq, dk, dv, table, *smalls)


def wo_grad_body(count, chunks, slot_ref, *refs):
    atts = refs[:chunks]
    aog_ref, keep_ref, send_ref, grad_ref = refs[chunks:]
    width = atts[0].shape[1]
    part = grad_ref.shape[1] // count
    for c in range(chunks):
        at = slice(c * width, (c + 1) * width)
        grad_ref[at, :] = dot_tn(atts[c][...], aog_ref[...]).astype(BF)
    for out_ref, slot, d in parted(keep_ref, send_ref, slot_ref):
        out_ref[slot] = grad_ref[:, pl.ds(pl.multiple_of(d * part, 128), part)]


def wo_grad_call(slots, atts, aog, count):
    chunks, width = len(atts), atts[0].shape[1]
    rows, depth = aog.shape
    return pl.pallas_call(
        functools.partial(wo_grad_body, count, chunks),
        in_specs=[sspec()] + [vspec()] * (chunks + 1),
        out_specs=[vspec()] * 2,
        out_shape=[jax.ShapeDtypeStruct((max(1, count // 2), chunks * width, depth // count), BF)] * 2,
        scratch_shapes=[pltpu.VMEM((chunks * width, depth), BF)],
        compiler_params=params(),
        cost_estimate=cost(2 * rows * depth * chunks * width, 4 * depth * chunks * width),
        name="w_output_grad",
    )(slots, *atts, aog)


def kept_choices(ids):
    lanes = jnp.arange(128, dtype=jnp.int32)[None, :]
    expert_range = jnp.arange(EXPERTS, dtype=jnp.int32)[None, :]
    first = (ids[:, 0:1] == expert_range).astype(jnp.int32)
    second = (ids[:, 1:2] == expert_range).astype(jnp.int32)
    runs = jnp.cumsum(jnp.concatenate([first, second], 1), axis=0)
    first_run = runs[:, :EXPERTS]
    second_run = runs[:, EXPERTS:] + first_run[-1][None, :]
    place_one = jnp.sum(first_run * first, axis=1, keepdims=True) - 1
    place_two = jnp.sum(second_run * second, axis=1, keepdims=True) - 1
    kept = ((ids[:, 0:1] == lanes) & (place_one < CAP)) | ((ids[:, 1:2] == lanes) & (place_two < CAP))
    return kept.astype(F32)


def on_device(
    tokens_in,
    out_grad,
    attn_gain,
    w_query,
    w_key,
    w_value,
    w_output,
    rel_table,
    moe_gain,
    w_router,
    w_gate,
    w_up,
    down_weight,
    expert_ids,
    piece_starts,
):
    rows, depth = tokens_in.shape
    width = w_query.shape[1]
    z_size = lax.axis_size("tensor")
    dp_size = lax.axis_size("dp")
    z_rank = lax.axis_index("tensor").astype(jnp.int32)
    dp_rank = lax.axis_index("dp").astype(jnp.int32)
    total = rows * z_size
    share = depth // dp_size
    unit = w_gate.shape[2]
    ff = EXPERTS * unit
    heads = rel_table.shape[0]
    direct = dp_size == 8 and share == 128
    place = z_rank ^ jnp.arange(z_size, dtype=jnp.int32)

    near = z_swap(tokens_in, 1, z_size)
    far = z_swap(tokens_in, 2, z_size)
    line_at = 2 * BLOCK - 1 - np.arange(total + 2 * BLOCK)
    line = jnp.dot(rel_table, jnp.asarray(onehot_of(line_at).T), precision=PRECISE)[:, None, :]
    sel = kept_choices(expert_ids)
    toks = [tokens_in, near, far, z_swap(after(far, near, sel, line), 1, z_size)]
    w_output_late = after(w_output, far)
    small = jnp.concatenate([attn_gain, moe_gain, w_router.T.reshape(-1)])[None, :]
    packed = jnp.concatenate([w_query, w_key, w_value], 1)
    wo_slots = jnp.stack(z_direct([w_output_late] * z_size, z_size))[None]
    ranks = dp_rank ^ jnp.arange(8, dtype=jnp.int32)
    if direct:
        index = dp_slots(ranks)
        slots = dp_rank ^ dp_scatter_slots(jnp.arange(8, dtype=jnp.int32))
        pad = jnp.zeros((15, packed.shape[1]), BF)
        pack = dp_step(jnp.concatenate([packed, small, pad], 0)[None], 2)
        pack = dp_step(after(pack, near), 4)
        wo_half = dp_step(after(wo_slots, near, far), 2)
        pack = dp_step(after(pack, toks[3], wo_half), 1)
        small_all = pack
    else:
        index = slots = jnp.zeros((1,), jnp.int32)
        pack = lax.all_gather(packed, "dp", axis=0, tiled=True)[None]
        small_all = lax.all_gather(small[0], "dp", axis=0).reshape(dp_size, 2 + EXPERTS, share)
        small_all = jnp.swapaxes(small_all, 0, 1).reshape(2 + EXPERTS, depth)
        small_all = jnp.concatenate([small_all, jnp.zeros((2, depth), BF)], 0)
        wo_all = lax.all_gather(wo_slots[0], "dp", axis=2, tiled=True)[None]

    local = jnp.stack(
        [
            jnp.swapaxes(w_gate, 1, 2).reshape(ff, share),
            jnp.swapaxes(w_up, 1, 2).reshape(ff, share),
            down_weight.reshape(ff, share),
        ]
    )
    if direct:
        experts_w = lax.all_gather(local, "dp", axis=0)
    else:
        experts_w = lax.all_gather(local, "dp", axis=2, tiled=True)[None]

    n1, q, k, v, kt, vt, gains, router = qkv_call(index, place, toks, pack, small_all, width)
    g_near = z_swap(after(out_grad, toks[3]), 1, z_size)
    g_far = z_swap(after(out_grad, toks[3]), 2, z_size)
    fwd = attn_fwd(piece_starts, place, z_size, q, k, vt, line)
    chances, ot = fwd[:2]
    atts = z_direct([after(fwd[2], g_near, g_far)] + [after(x, g_near, g_far) for x in fwd[3:]], z_size)
    if direct:
        wo_all = dp_step(after(dp_step(after(wo_half, n1), 4), atts[1]), 1)
    gs = [out_grad, g_near, g_far, z_swap(after(g_far, fwd[2]), 1, z_size)]
    mid, n2 = mid_call(index, [after(atts[0], gs[3])] + atts[1:], wo_all, tokens_in, gains)

    n2_near = z_swap(n2, 1, z_size)
    n2_far = z_swap(n2, 2, z_size)
    n2s = [n2, n2_near, n2_far, z_swap(after(n2_far, n2_near), 1, z_size)]
    hg, gg, ug, logit_grad, router_part = units_call(place, n2s, gs, sel, router, experts_w, unit)
    ngs = product_call([gg, ug], (0, 1), experts_w, z_size, [logit_grad, router], "normed_two_grads")
    passed = z_swap(ngs[3], 1, z_size)
    outs = product_call([after(hg, ngs[0])], (2,), experts_w, z_size, [], "expert_out")
    both = (ngs[2].astype(F32) + after(passed, outs[0]).astype(F32)).astype(BF)
    far = z_swap(both, 2, z_size)
    ng_near = z_swap(after(ngs[1], passed), 1, z_size)
    count = experts_w.shape[0]
    weight_grads = wgrad_call(experts_w.shape[0], [after(hg, both, *outs), gg, ug], n2s, gs)
    resid = resid_call(index, [after(ngs[0], weight_grads), ng_near, far], mid, out_grad, gains, wo_all)
    resid_grad, aog, gain_two = resid[:3]
    weight_grads = after(weight_grads, far, ng_near)
    if direct:
        expert_grads = lax.psum_scatter(weight_grads, "dp", scatter_dimension=0, tiled=False)
    else:
        expert_grads = lax.psum_scatter(weight_grads[0], "dp", scatter_dimension=2, tiled=True)
    out_passed = z_swap(after(outs[3], aog), 1, z_size)
    dos = z_direct(resid[3:], z_size)
    wo_keep, wo_send = wo_grad_call(slots, atts, aog, count)
    out_both = (outs[2].astype(F32) + out_passed.astype(F32)).astype(BF)
    dos[0] = after(dos[0], wo_keep, out_both)
    out_far = z_swap(out_both, 2, z_size)
    out_near = z_swap(after(outs[1], out_both), 1, z_size)
    if direct:
        wo_grads = dp_fold(wo_keep, after(wo_send, *dos), 1)
    dq, dk, dv, diag = attn_bwd(place, dos, chances, q, k, v, kt, ot)
    if direct:
        wo_grads = dp_fold(*halves(wo_grads), 2)
        dq = after(dq, wo_grads)
    dq = after(dq, out_far, out_near)
    proj = proj_call(index, place, dq, dk, dv, pack, gain_two, router_part, toks)

    diag_at = (
        BLOCK * np.arange(total // BLOCK + 1)[:, None] - (BLOCK * (total // BLOCK - 2) + 1) - np.arange(2 * BLOCK)[None, :]
    )
    table = jnp.einsum("hbt,btk->hk", diag, jnp.asarray(onehot_of(diag_at)), precision=PRECISE)
    n1_passed = z_swap(proj[3], 1, z_size)
    if direct:
        table_rows = jnp.pad(table.reshape(1, -1), ((0, 7), (0, 0)))
        smalls = z_direct([proj[z_size]] * z_size, z_size)
        wo_grads = dp_fold(*halves(wo_grads), 4)[0]
        attn_keep, attn_send = attn_weights_call(slots, n1, dq, dk, dv, after(table_rows, wo_grads), smalls, 8)
        n1_passed = after(n1_passed, attn_keep)
    n1_both = (proj[2].astype(F32) + n1_passed.astype(F32)).astype(BF)
    n1_far = z_swap(n1_both, 2, z_size)
    n1_near = z_swap(after(proj[1], n1_both), 1, z_size)
    in_grad = final_call([proj[0], n1_near, n1_far], tokens_in, resid_grad, gains)
    out_parts = [outs[0], out_near, out_far]
    out_rows = (mid + functools.reduce(jnp.add, [p.astype(F32) for p in out_parts])).astype(BF)

    if direct:
        attn_grads = dp_fold(attn_keep, after(attn_send, n1_both), 1)
        attn_grads = dp_fold(*halves(attn_grads), 2)
        attn_grads = dp_fold(*halves(after(attn_grads, n1_far, n1_near)), 4)
        attn_grads = attn_grads[0].astype(F32)
        per = width // 128
        cut = attn_grads[: 3 * per * share].reshape(3, per, share, 128)
        cut = jnp.swapaxes(cut, 1, 2).reshape(3, share, width)
        smalls = attn_grads[3 * per * share :]
        grad_table = smalls[8, : heads * BUCKETS].reshape(heads, BUCKETS)
        mine = z_rank
        grad_wo = after(wo_grads, n1_near)
    else:
        cut = jnp.stack([jnp.dot(n1.T, d, preferred_element_type=F32) for d in (dq, dk, dv)])
        cut = lax.psum_scatter(cut, "dp", scatter_dimension=1, tiled=True)
        smalls = lax.psum(proj[z_size], ("dp", "tensor"))
        grad_table = lax.psum(table, "dp")
        mine = dp_rank * z_size + z_rank
        grad_wo = lax.psum_scatter(wo_keep[0], "dp", scatter_dimension=1, tiled=True)
    wo_parts = z_direct([grad_wo[width * c : width * (c + 1)] for c in range(z_size)], z_size)
    grad_wo = functools.reduce(jnp.add, [p.astype(F32) for p in wo_parts])
    per_device = depth // (dp_size * z_size)
    own = lax.dynamic_slice_in_dim(smalls, mine * per_device, per_device, 1)

    wide = expert_grads.astype(F32).reshape(3, EXPERTS, unit, share)
    return (
        out_rows,
        in_grad,
        own[0],
        cut[0],
        cut[1],
        cut[2],
        grad_wo,
        grad_table,
        own[1],
        own[2 : 2 + EXPERTS].T,
        jnp.swapaxes(wide[0], 1, 2),
        jnp.swapaxes(wide[1], 1, 2),
        wide[2],
    )


def solution(mesh):
    rows = P(("dp", "tensor"), None)
    grid = P("dp", "tensor")
    flat = P(("dp", "tensor"))
    weights = (P(None, "dp", "tensor"), P(None, "dp", "tensor"), P(None, "tensor", "dp"))
    in_specs = (rows, rows, P("dp"), grid, grid, grid, P("tensor", "dp"), P("tensor", None), P("dp"), P("dp", None))
    out_specs = (rows, rows, flat, grid, grid, grid, P("tensor", "dp"), P("tensor", None), flat, rows)
    return jax.shard_map(
        on_device,
        mesh=mesh,
        in_specs=in_specs + weights + (P("dp", None), P("dp", None)),
        out_specs=out_specs + weights,
        check_vma=False,
    )
```

profile of v0, /device:TPU:14, one launch (start us, length us, event | category | flops | bytes accessed | tf_op | source)
XLA Modules:
  0.0 393.6 jit_solution(17420361323798181976)
XLA Ops:
  7.2 3.1 pad_maximum_fusion
  11.8 2.6 collective-permute-start.1
  15.3 2.3 reduce-window.6
  19.3 1.6 fusion.2.refs_8_
  20.9 16.6 %collective-permute-done.1.refs_2_ = bf16[256,1024]{1,0:T(8,128)(2,1)} collective-permute-done((bf16[256,1024]{1,0:T(8,128)(2,1)S(1)}, bf16[256,1024]{1,0:T(8,128)(2,1)}, u32[]{:S(2)}, u32[]{:S(2)}) %collective-permute-start.1) | collective-permute-done | bytes 524320 | tf_op jit(solution)/shard_map/ppermute | solution.py:66
  38.0 3.5 collective-permute-start.6
  41.6 2.0 collective-permute-start.2
  44.1 1.7 collective-permute-done.6
  45.8 1.5 collective-permute-done.5
  48.0 5.8 %collective-permute-done.8 = bf16[1,4,256,128]{3,2,1,0:T(8,128)(2,1)S(1)} collective-permute-done((bf16[1,4,256,128]{3,2,1,0:T(8,128)(2,1)S(1)}, bf16[1,4,256,128]{3,2,1,0:T(8,128)(2,1)S(1)}, u32[]{:S(2)}, u32[]{:S(2)}) %collective-permute-start.8) | collective-permute-done | bytes 262176 | tf_op jit(solution)/shard_map/ppermute | solution.py:94
  53.8 1.9 collective-permute-done.4
  57.6 2.3 collective-permute-start.11
  60.1 1.2 copy-done.18
  61.3 7.0 %norm_qkv.1 = (bf16[1024,1024]{1,0:T(8,128)(2,1)}, bf16[1024,256]{1,0:T(8,128)(2,1)}, bf16[1024,256]{1,0:T(8,128)(2,1)}, bf16[1024,256]{1,0:T(8,128)(2,1)}, bf16...) custom-call(s32[8]{0:T(128)} %shift-left_or_fusion.index_ref, ...), custom_call_target="tpu_custom_call" | custom-call | flops 1610612736 | bytes 8388608 | tf_op jit(solution)/shard_map/norm_qkv/pallas_call | solution.py:163
  68.3 1.5 collective-permute-start.16
  69.7 16.3 %attn_forward.1 = (bf16[4,1024,1024]{2,1,0:T(8,128)(2,1)}, f32[256,1024]{1,0:T(8,128)}, bf16[256,256]{1,0:T(8,128)(2,1)}, bf16[256,256]{1,0:T(8,128)(2,1)}, bf16...) custom-call(s32[1,2]{1,0:T(1,128)} %starts_ref.1, s32[4]{0:T(128)} %iota_xor_fusion.place_ref, ...), custom_call_target="tpu_custom_call" | custom-call | flops 4294967296 | bytes 10485760 | tf_op jit(solution)/shard_map/attn_forward/pallas_call | solution.py:250
  86.1 1.8 collective-permute-start.13
  87.9 6.0 %collective-permute-done.16 = bf16[2,4,256,128]{3,2,1,0:T(8,128)(2,1)S(1)} collective-permute-done((bf16[2,4,256,128]{3,2,1,0:T(8,128)(2,1)S(1)}, bf16[2,4,256,128]{3,2,1,0:T(8,128)(2,1)S(1)}, u32[]{:S(2)}, u32[]{:S(2)}) %collective-permute-start.16) | collective-permute-done | bytes 524320 | tf_op jit(solution)/shard_map/ppermute | solution.py:94
  94.1 1.5 collective-permute-start.12
  96.5 1.1 collective-permute-start.15
  97.7 12.6 %collective-permute-done.12.refs_7_.refs_10_ = bf16[256,1024]{1,0:T(8,128)(2,1)S(1)} collective-permute-done((bf16[256,1024]{1,0:T(8,128)(2,1)S(1)}, bf16[256,1024]{1,0:T(8,128)(2,1)S(1)}, u32[]{:S(2)}, u32[]{:S(2)}) %collective-permute-start.12) | collective-permute-done | bytes 524320 | tf_op jit(solution)/shard_map/ppermute | solution.py:66
  112.7 3.9 out_projection_norm.1
  116.6 4.0 %collective-permute-start.18 = (bf16[256,1024]{1,0:T(8,128)(2,1)}, bf16[256,1024]{1,0:T(8,128)(2,1)S(1)}, u32[]{:S(2)}, u32[]{:S(2)}) collective-permute-start(bf16[256,1024]{1,0:T(8,128)(2,1)} %get-tuple-element.119.refs_0_.refs_3_), channel_id=1, source_target_pairs={{0,1},{1,0},{2,3},{3,2},{4,5},{5,4},{6,7},{7,6},{8,9},{9,8},{10,11... | collective-permute-start | bytes 1572872 | tf_op jit(solution)/shard_map/ppermute | solution.py:66
  121.0 21.4 %collective-permute-done.18.refs_1_.refs_4_ = bf16[256,1024]{1,0:T(8,128)(2,1)S(1)} collective-permute-done((bf16[256,1024]{1,0:T(8,128)(2,1)}, bf16[256,1024]{1,0:T(8,128)(2,1)S(1)}, u32[]{:S(2)}, u32[]{:S(2)}) %collective-permute-start.18) | collective-permute-done | bytes 524320 | tf_op jit(solution)/shard_map/ppermute | solution.py:66
  142.4 1.9 collective-permute-done.19.refs_2_.refs_5_
  144.3 2.0 collective-permute-start.20
  146.3 10.8 %collective-permute-done.20.refs_3_.refs_6_ = bf16[256,1024]{1,0:T(8,128)(2,1)S(1)} collective-permute-done((bf16[256,1024]{1,0:T(8,128)(2,1)S(1)}, bf16[256,1024]{1,0:T(8,128)(2,1)S(1)}, u32[]{:S(2)}, u32[]{:S(2)}) %collective-permute-start.20) | collective-permute-done | bytes 524320 | tf_op jit(solution)/shard_map/ppermute | solution.py:66
  157.9 32.0 %expert_units.1 = (bf16[1024,2816]{1,0:T(8,128)(2,1)}, bf16[1024,2816]{1,0:T(8,128)(2,1)}, bf16[1024,2816]{1,0:T(8,128)(2,1)}, f32[1024,128]{1,0:T(8,128)}, f32[8,1024]{1,0:T(8,128)}) custom-call(s32[4]{0:T(128)} %iota_xor_fusion.place_ref, bf16[256,1024]{1,0:T(8,128)(2,1)} %get-tuple-element.119.refs_0_.refs_3_, bf16[256,1024]{1,0:T(8,128)(2,1)} %copy-done.38, ...), custom_call_target="tpu_custom_call" | custom-call | flops 17716740096 | bytes 29884416 | tf_op jit(solution)/shard_map/expert_units/pallas_call | solution.py:513
  189.9 19.8 %normed_two_grads.1 = (bf16[256,1024]{1,0:T(8,128)(2,1)}, bf16[256,1024]{1,0:T(8,128)(2,1)}, bf16[256,1024]{1,0:T(8,128)(2,1)}, bf16[256,1024]{1,0:T(8,128)(2,1)}) custom-call(bf16[1024,2816]{1,0:T(8,128)(2,1)} %get-tuple-element.123.refs_0_.refs_1_, bf16[1024,2816]{1,0:T(8,128)(2,1)} %get-tuple-element.124.refs_1_.refs_2_, ...), custom_call_target="tpu_custom_call" | custom-call | flops 11811160064 | bytes 23068672 | tf_op jit(solution)/shard_map/normed_two_grads/pallas_call | solution.py:563
  210.4 10.5 %expert_out.1 = (bf16[256,1024]{1,0:T(8,128)(2,1)}, bf16[256,1024]{1,0:T(8,128)(2,1)}, bf16[256,1024]{1,0:T(8,128)(2,1)}, bf16[256,1024]{1,0:T(8,128)(2,1)}) custom-call(bf16[1024,2816]{1,0:T(8,128)(2,1)} %get-tuple-element.135.refs_0_, bf16[8,3,2816,128]{3,2,1,0:T(8,128)(2,1)} %bitcast.79), custom_call_target="tpu_custom_call" | custom-call | flops 5905580032 | bytes 11534336 | tf_op jit(solution)/shard_map/expert_out/pallas_call | solution.py:563
  220.8 1.6 collective-permute-done.21
  222.7 1.2 collective-permute-start.22
  223.9 25.0 %expert_weight_grads.1 = bf16[8,3,2816,128]{3,2,1,0:T(8,128)(2,1)} custom-call(bf16[1024,2816]{1,0:T(8,128)(2,1)} %get-tuple-element.135.refs_0_, bf16[1024,2816]{1,0:T(8,128)(2,1)} %get-tuple-element.123.refs_0_.refs_1_, bf16[1024,2816]{1,0:T(8,128)(2,1)} %get-tuple-element.124.refs_1_.refs_2_, bf16[256,1024]{1,0:T(8,128)(2,1)} %get-tuple-element.119.refs_0_.refs_3_, ...), custom_call_target="tpu_custom_call" | custom-call | flops 17716740096 | bytes 34603008 | tf_op jit(solution)/shard_map/expert_weight_grads/pallas_call | solution.py:603
  249.9 4.7 %resid_grad.1 = (f32[256,1024]{1,0:T(8,128)}, bf16[256,1024]{1,0:T(8,128)(2,1)}, f32[8,1024]{1,0:T(8,128)}, bf16[256,256]{1,0:T(8,128)(2,1)}, bf16[256,256]{1,0:...) custom-call(s32[8]{0:T(128)} %shift-left_or_fusion.index_ref, ...), custom_call_target="tpu_custom_call" | custom-call | flops 536870912 | bytes 4194304 | tf_op jit(solution)/shard_map/resid_grad/pallas_call | solution.py:644
  256.0 1.1 collective-permute-start.27
  257.2 1.7 collective-permute-start.28
  259.5 3.9 w_output_grad.1
  263.5 5.8 %collective-permute-done.24 = bf16[256,1024]{1,0:T(8,128)(2,1)S(1)} collective-permute-done((bf16[256,1024]{1,0:T(8,128)(2,1)S(1)}, bf16[256,1024]{1,0:T(8,128)(2,1)S(1)}, u32[]{:S(2)}, u32[]{:S(2)}) %collective-permute-start.24) | collective-permute-done | bytes 524320 | tf_op jit(solution)/shard_map/ppermute | solution.py:66
  269.3 1.0 add_convert_fusion.5
  270.7 2.5 collective-permute-done.28.refs_2_
  273.3 2.5 collective-permute-start.26
  276.5 1.0 copy-done.3
  278.3 1.2 collective-permute-start.31
  279.5 15.0 %attn_backward.1 = (bf16[1024,256]{1,0:T(8,128)(2,1)}, bf16[1024,256]{1,0:T(8,128)(2,1)}, bf16[1024,256]{1,0:T(8,128)(2,1)}, f32[4,5,512]{2,1,0:T(8,128)}) custom-call(s32[4]{0:T(128)} %iota_xor_fusion.place_ref, bf16[256,256]{1,0:T(8,128)(2,1)} %get-tuple-element.144.refs_0_, bf16[256,256]{1,0:T(8,128)(2,1)} %copy-done.42, bf16[256,256]{1,0:T(8,128)(2,1)} %copy-done.43, ...), custom_call_target="tpu_custom_call" | custom-call | flops 171798691840 | bytes 10485760 | tf_op jit(solution)/shard_map/attn_backward/pallas_call | solution.py:365
  294.5 2.8 collective-permute-done.31
  297.3 1.2 add_convert_fusion.3
  299.2 1.1 collective-permute-done.25
  300.3 1.9 collective-permute-start.33
  302.2 5.9 %projection_grads.1 = (bf16[256,1024]{1,0:T(8,128)(2,1)}, bf16[256,1024]{1,0:T(8,128)(2,1)}, bf16[256,1024]{1,0:T(8,128)(2,1)}, bf16[256,1024]{1,0:T(8,128)(2,1)}, f32[8,1024]{1,0:T(8,128)}) custom-call(s32[8]{0:T(128)} %shift-left_or_fusion.index_ref, s32[4]{0:T(128)} %iota_xor_fusion.place_ref, bf16[1024,256]{1,0:T(8,128)(2,1)} %get-tuple-element.156.dq_ref, ...), custom_call_target="tpu_custom_call" | custom-call | flops 1610612736 | bytes 8388608 | tf_op jit(solution)/shard_map/projection_grads/pallas_call | solution.py:703
  308.1 3.4 collective-permute-start.32
  312.6 2.9 collective-permute-start.35
  316.2 7.1 %collective-permute-done.34.refs_1_ = f32[8,1024]{1,0:T(8,128)S(1)} collective-permute-done((f32[8,1024]{1,0:T(8,128)}, f32[8,1024]{1,0:T(8,128)S(1)}, u32[]{:S(2)}, u32[]{:S(2)}) %collective-permute-start.34) | collective-permute-done | bytes 32800 | tf_op jit(solution)/shard_map/ppermute | solution.py:66
  323.3 1.3 collective-permute-done.35.refs_2_
  325.9 5.3 %attn_weight_grads.1 = (bf16[4,784,128]{2,1,0:T(8,128)(2,1)}, bf16[4,784,128]{2,1,0:T(8,128)(2,1)}) custom-call(s32[8]{0:T(128)} %fusion.17.slot_ref, bf16[1024,1024]{1,0:T(8,128)(2,1)} %get-tuple-element.114.n1_ref, bf16[1024,256]{1,0:T(8,128)(2,1)} %get-tuple-element.156.dq_ref, bf16[1024,256]{1,0:T(8,128)(2,1)} %get-tuple-element.157.dk_ref, ...), custom_call_target="tpu_custom_call" | custom-call | flops 1610612736 | bytes 8388608 | tf_op jit(solution)/shard_map/attn_weight_grads/pallas_call | solution.py:739
  331.4 2.1 collective-permute-start.38
  334.3 2.3 add_convert_fusion.4
  336.6 20.3 %collective-permute-done.37.refs_1_ = bf16[256,1024]{1,0:T(8,128)(2,1)S(1)} collective-permute-done((bf16[256,1024]{1,0:T(8,128)(2,1)}, bf16[256,1024]{1,0:T(8,128)(2,1)S(1)}, u32[]{:S(2)}, u32[]{:S(2)}) %collective-permute-start.37) | collective-permute-done | bytes 524320 | tf_op jit(solution)/shard_map/ppermute | solution.py:66
  356.9 1.7 collective-permute-start.44
  358.6 1.4 collective-permute-start.43
  360.0 1.4 collective-permute-start.42
  362.2 3.4 in_grad.1
  366.9 10.2 %collective-permute-done.41 = bf16[1,784,128]{2,1,0:T(8,128)(2,1)S(1)} collective-permute-done((bf16[1,784,128]{2,1,0:T(8,128)(2,1)S(1)}, bf16[1,784,128]{2,1,0:T(8,128)(2,1)S(1)}, u32[]{:S(2)}, u32[]{:S(2)}) %collective-permute-start.41) | collective-permute-done | bytes 200736 | tf_op jit(solution)/shard_map/ppermute | solution.py:99
  381.4 1.7 reduce-scatter.2.cloned.1.call-done
  383.1 3.7 fusion.19
  (213 shorter events, 29.4 us)
Async XLA Ops:
  7.2 11.3 %copy-start = (f32[4,32]{1,0:T(4,128)S(1)}, f32[4,32]{1,0:T(4,128)}, u32[]{:S(2)}) copy-start(f32[4,32]{1,0:T(4,128)} %param.24) | copy-start | bytes 1540
  7.2 149.9 %all-gather.3.cloned.1.call-start = ((), (), s32[]{:S(2)}) async-start(), calls=%async_computation.2 | async-start | bytes 19464192 | tf_op jit(solution)/shard_map/all_gather | solution.py:859
  10.4 27.1 %copy-start.27 = (bf16[256,128]{1,0:T(8,128)(2,1)S(1)}, bf16[256,128]{1,0:T(8,128)(2,1)}, u32[]{:S(2)}) copy-start(bf16[256,128]{1,0:T(8,128)(2,1)} %param.23) | copy-start | bytes 196612
  10.5 372.6 %reduce-scatter.2.cloned.1.call-start = ((), (), s32[]{:S(2)}) async-start(), calls=%async_computation.1 | async-start | bytes 19464192 | tf_op jit(solution)/shard_map/reduce_scatter | solution.py:890
  11.4 30.2 %collective-permute-start = (bf16[256,1024]{1,0:T(8,128)(2,1)S(1)}, bf16[256,1024]{1,0:T(8,128)(2,1)S(1)}, u32[]{:S(2)}, u32[]{:S(2)}) collective-permute-start(bf16[256,1024]{1,0:T(8,128)(2,1)S(1)} %copy-done.6), channel_id=1, source_target_pairs={{0,1},{1,0},{2,3},{3,2},{4,5},{5,4},{6,7},{7,6},{8,9},{9,8},{10,11... | collective-permute-start | bytes 1572872 | tf_op jit(solution)/shard_map/ppermute | solution.py:66
  11.8 25.7 %collective-permute-start.1 = (bf16[256,1024]{1,0:T(8,128)(2,1)S(1)}, bf16[256,1024]{1,0:T(8,128)(2,1)}, u32[]{:S(2)}, u32[]{:S(2)}) collective-permute-start(bf16[256,1024]{1,0:T(8,128)(2,1)S(1)} %copy-done.6), channel_id=1, source_target_pairs={{0,2},{1,3},{2,0},{3,1},{4,6},{5,7},{6,4},{7,5},{8,10},{9,11},{10,... | collective-permute-start | bytes 1572872 | tf_op jit(solution)/shard_map/ppermute | solution.py:66
  14.7 26.9 %collective-permute-start.3 = (bf16[1,144,768]{2,1,0:T(8,128)(2,1)S(1)}, bf16[1,144,768]{2,1,0:T(8,128)(2,1)S(1)}, u32[]{:S(2)}, u32[]{:S(2)}) collective-permute-start(bf16[1,144,768]{2,1,0:T(8,128)(2,1)S(1)} %maximum_bitcast_fusion.1), channel_id=1, source_target_pairs={{0,8},{4,12},{8,0},{12,4},{16,24},{20,28},{24,16},{28,20},{1,9},{5... | collective-permute-start | bytes 663560 | tf_op jit(solution)/shard_map/ppermute | solution.py:94
  20.9 36.0 %copy-start.13 = (bf16[256,1024]{1,0:T(8,128)(2,1)S(1)}, bf16[256,1024]{1,0:T(8,128)(2,1)}, u32[]{:S(2)}) copy-start(bf16[256,1024]{1,0:T(8,128)(2,1)} %refs_4_.3) | copy-start | bytes 1572868
  37.5 6.6 %collective-permute-start.7 = (bf16[256,128]{1,0:T(8,128)(2,1)S(1)}, bf16[256,128]{1,0:T(8,128)(2,1)S(1)}, u32[]{:S(2)}, u32[]{:S(2)}) collective-permute-start(bf16[256,128]{1,0:T(8,128)(2,1)S(1)} %copy-done.27), channel_id=1, source_target_pairs={{0,3},{1,2},{2,1},{3,0},{4,7},{5,6},{6,5},{7,4},{8,11},{9,10},{10,... | collective-permute-start | bytes 196616 | tf_op jit(solution)/shard_map/ppermute | solution.py:66
  38.0 7.9 %collective-permute-start.6 = (bf16[256,128]{1,0:T(8,128)(2,1)S(1)}, bf16[256,128]{1,0:T(8,128)(2,1)S(1)}, u32[]{:S(2)}, u32[]{:S(2)}) collective-permute-start(bf16[256,128]{1,0:T(8,128)(2,1)S(1)} %copy-done.27), channel_id=1, source_target_pairs={{0,2},{1,3},{2,0},{3,1},{4,6},{5,7},{6,4},{7,5},{8,10},{9,11},{10,... | collective-permute-start | bytes 196616 | tf_op jit(solution)/shard_map/ppermute | solution.py:66
  41.5 5.9 %collective-permute-start.5 = (bf16[256,128]{1,0:T(8,128)(2,1)S(1)}, bf16[256,128]{1,0:T(8,128)(2,1)S(1)}, u32[]{:S(2)}, u32[]{:S(2)}) collective-permute-start(bf16[256,128]{1,0:T(8,128)(2,1)S(1)} %copy-done.27), channel_id=1, source_target_pairs={{0,1},{1,0},{2,3},{3,2},{4,5},{5,4},{6,7},{7,6},{8,9},{9,8},{10,11... | collective-permute-start | bytes 196616 | tf_op jit(solution)/shard_map/ppermute | solution.py:66
  41.6 18.3 %copy-start.33 = (bf16[256,1024]{1,0:T(8,128)(2,1)}, bf16[256,1024]{1,0:T(8,128)(2,1)S(1)}, u32[]{:S(2)}) copy-start(bf16[256,1024]{1,0:T(8,128)(2,1)S(1)} %collective-permute-done.refs_1_) | copy-start | bytes 1572868
  41.6 14.2 %collective-permute-start.2 = (bf16[256,1024]{1,0:T(8,128)(2,1)}, bf16[256,1024]{1,0:T(8,128)(2,1)}, u32[]{:S(2)}, u32[]{:S(2)}) collective-permute-start(bf16[256,1024]{1,0:T(8,128)(2,1)} %collective-permute-done.1.refs_2_), channel_id=1, source_target_pairs={{0,1},{1,0},{2,3},{3,2},{4,5},{5,4},{6,7},{7,6},{8,9},{9,8},{10,11... | collective-permute-start | bytes 1572872 | tf_op jit(solution)/shard_map/ppermute | solution.py:66
  43.6 12.1 %collective-permute-start.4 = (bf16[2,144,768]{2,1,0:T(8,128)(2,1)S(1)}, bf16[2,144,768]{2,1,0:T(8,128)(2,1)S(1)}, u32[]{:S(2)}, u32[]{:S(2)}) collective-permute-start(bf16[2,144,768]{2,1,0:T(8,128)(2,1)S(1)} %pad_maximum_fusion.3), channel_id=1, source_target_pairs={{0,16},{4,20},{8,24},{12,28},{16,0},{20,4},{24,8},{28,12},{1,17},{... | collective-permute-start | bytes 1327112 | tf_op jit(solution)/shard_map/ppermute | solution.py:94
  47.4 6.4 %collective-permute-start.8 = (bf16[1,4,256,128]{3,2,1,0:T(8,128)(2,1)S(1)}, bf16[1,4,256,128]{3,2,1,0:T(8,128)(2,1)S(1)}, u32[]{:S(2)}, u32[]{:S(2)}) collective-permute-start(bf16[1,4,256,128]{3,2,1,0:T(8,128)(2,1)S(1)} %maximum_bitcast_fusion), channel_id=1, source_target_pairs={{0,8},{4,12},{8,0},{12,4},{16,24},{20,28},{24,16},{28,20},{1,9},{5... | collective-permute-start | bytes 786440 | tf_op jit(solution)/shard_map/ppermute | solution.py:94
  55.8 4.1 %collective-permute-start.9 = (bf16[4,144,768]{2,1,0:T(8,128)(2,1)S(1)}, bf16[4,144,768]{2,1,0:T(8,128)(2,1)S(1)}, u32[]{:S(2)}, u32[]{:S(2)}) collective-permute-start(bf16[4,144,768]{2,1,0:T(8,128)(2,1)S(1)} %pad_maximum_fusion.2), channel_id=1, source_target_pairs={{0,4},{4,0},{8,12},{12,8},{16,20},{20,16},{24,28},{28,24},{1,5},{5... | collective-permute-start | bytes 2654216 | tf_op jit(solution)/shard_map/ppermute | solution.py:94
  57.0 29.1 %collective-permute-start.10 = (bf16[256,1024]{1,0:T(8,128)(2,1)S(1)}, bf16[256,1024]{1,0:T(8,128)(2,1)S(1)}, u32[]{:S(2)}, u32[]{:S(2)}) collective-permute-start(bf16[256,1024]{1,0:T(8,128)(2,1)S(1)} %copy-done.13), channel_id=1, source_target_pairs={{0,1},{1,0},{2,3},{3,2},{4,5},{5,4},{6,7},{7,6},{8,9},{9,8},{10,11... | collective-permute-start | bytes 1572872 | tf_op jit(solution)/shard_map/ppermute | solution.py:66
  57.6 28.5 %collective-permute-start.11 = (bf16[256,1024]{1,0:T(8,128)(2,1)S(1)}, bf16[256,1024]{1,0:T(8,128)(2,1)S(1)}, u32[]{:S(2)}, u32[]{:S(2)}) collective-permute-start(bf16[256,1024]{1,0:T(8,128)(2,1)S(1)} %copy-done.13), channel_id=1, source_target_pairs={{0,2},{1,3},{2,0},{3,1},{4,6},{5,7},{6,4},{7,5},{8,10},{9,11},{10,... | collective-permute-start | bytes 1572872 | tf_op jit(solution)/shard_map/ppermute | solution.py:66
  68.3 25.6 %collective-permute-start.16 = (bf16[2,4,256,128]{3,2,1,0:T(8,128)(2,1)S(1)}, bf16[2,4,256,128]{3,2,1,0:T(8,128)(2,1)S(1)}, u32[]{:S(2)}, u32[]{:S(2)}) collective-permute-start(bf16[2,4,256,128]{3,2,1,0:T(8,128)(2,1)S(1)} %constant_dynamic-update-slice_fusion), channel_id=1, source_target_pairs={{0,16},{4,20},{8,24},{12,28},{16,0},{20,4},{24,8},{28,12},{1,17},{... | collective-permute-start | bytes 1572872 | tf_op jit(solution)/shard_map/ppermute | solution.py:94
  86.1 9.6 %copy-start.46 = (bf16[256,256]{1,0:T(8,128)(2,1)S(1)}, bf16[256,256]{1,0:T(8,128)(2,1)}, u32[]{:S(2)}) copy-start(bf16[256,256]{1,0:T(8,128)(2,1)} %get-tuple-element.111) | copy-start | bytes 393220
  86.1 10.4 %copy-start.45 = (bf16[256,256]{1,0:T(8,128)(2,1)S(1)}, bf16[256,256]{1,0:T(8,128)(2,1)}, u32[]{:S(2)}) copy-start(bf16[256,256]{1,0:T(8,128)(2,1)} %get-tuple-element.113) | copy-start | bytes 393220
  86.1 11.6 %copy-start.34 = (bf16[256,1024]{1,0:T(8,128)(2,1)}, bf16[256,1024]{1,0:T(8,128)(2,1)S(1)}, u32[]{:S(2)}) copy-start(bf16[256,1024]{1,0:T(8,128)(2,1)S(1)} %collective-permute-done.10.refs_5_.refs_8_) | copy-start | bytes 1572868
  86.1 24.3 %copy-start.35 = (bf16[256,1024]{1,0:T(8,128)(2,1)}, bf16[256,1024]{1,0:T(8,128)(2,1)S(1)}, u32[]{:S(2)}) copy-start(bf16[256,1024]{1,0:T(8,128)(2,1)S(1)} %collective-permute-done.11.refs_6_.refs_9_) | copy-start | bytes 1572868
  86.1 7.9 %collective-permute-start.13 = (bf16[256,256]{1,0:T(8,128)(2,1)}, bf16[256,256]{1,0:T(8,128)(2,1)S(1)}, u32[]{:S(2)}, u32[]{:S(2)}) collective-permute-start(bf16[256,256]{1,0:T(8,128)(2,1)} %get-tuple-element.109), channel_id=1, source_target_pairs={{0,1},{1,0},{2,3},{3,2},{4,5},{5,4},{6,7},{7,6},{8,9},{9,8},{10,11... | collective-permute-start | bytes 393224 | tf_op jit(solution)/shard_map/ppermute | solution.py:66
  94.0 16.6 %copy-start.21 = (bf16[256,256]{1,0:T(8,128)(2,1)}, bf16[256,256]{1,0:T(8,128)(2,1)S(1)}, u32[]{:S(2)}) copy-start(bf16[256,256]{1,0:T(8,128)(2,1)S(1)} %collective-permute-done.13.refs_1_) | copy-start | bytes 393220
  94.0 16.4 %collective-permute-start.17 = (bf16[4,4,256,128]{3,2,1,0:T(8,128)(2,1)S(1)}, bf16[4,4,256,128]{3,2,1,0:T(8,128)(2,1)S(1)}, u32[]{:S(2)}, u32[]{:S(2)}) collective-permute-start(bf16[4,4,256,128]{3,2,1,0:T(8,128)(2,1)S(1)} %pad_maximum_fusion.1), channel_id=1, source_target_pairs={{0,4},{4,0},{8,12},{12,8},{16,20},{20,16},{24,28},{28,24},{1,5},{5... | collective-permute-start | bytes 3145736 | tf_op jit(solution)/shard_map/ppermute | solution.py:94
  94.1 16.2 %collective-permute-start.12 = (bf16[256,1024]{1,0:T(8,128)(2,1)S(1)}, bf16[256,1024]{1,0:T(8,128)(2,1)S(1)}, u32[]{:S(2)}, u32[]{:S(2)}) collective-permute-start(bf16[256,1024]{1,0:T(8,128)(2,1)S(1)} %collective-permute-done.11.refs_6_.refs_9_), channel_id=1, source_target_pairs={{0,1},{1,0},{2,3},{3,2},{4,5},{5,4},{6,7},{7,6},{8,9},{9,8},{10,11... | collective-permute-start | bytes 1572872 | tf_op jit(solution)/shard_map/ppermute | solution.py:66
  95.7 16.4 %collective-permute-start.14 = (bf16[256,256]{1,0:T(8,128)(2,1)S(1)}, bf16[256,256]{1,0:T(8,128)(2,1)S(1)}, u32[]{:S(2)}, u32[]{:S(2)}) collective-permute-start(bf16[256,256]{1,0:T(8,128)(2,1)S(1)} %copy-done.46), channel_id=1, source_target_pairs={{0,2},{1,3},{2,0},{3,1},{4,6},{5,7},{6,4},{7,5},{8,10},{9,11},{10,... | collective-permute-start | bytes 393224 | tf_op jit(solution)/shard_map/ppermute | solution.py:66
  96.5 15.5 %collective-permute-start.15 = (bf16[256,256]{1,0:T(8,128)(2,1)S(1)}, bf16[256,256]{1,0:T(8,128)(2,1)S(1)}, u32[]{:S(2)}, u32[]{:S(2)}) collective-permute-start(bf16[256,256]{1,0:T(8,128)(2,1)S(1)} %copy-done.45), channel_id=1, source_target_pairs={{0,3},{1,2},{2,1},{3,0},{4,7},{5,6},{6,5},{7,4},{8,11},{9,10},{10,... | collective-permute-start | bytes 393224 | tf_op jit(solution)/shard_map/ppermute | solution.py:66
  116.6 25.8 %collective-permute-start.18 = (bf16[256,1024]{1,0:T(8,128)(2,1)}, bf16[256,1024]{1,0:T(8,128)(2,1)S(1)}, u32[]{:S(2)}, u32[]{:S(2)}) collective-permute-start(bf16[256,1024]{1,0:T(8,128)(2,1)} %get-tuple-element.119.refs_0_.refs_3_), channel_id=1, source_target_pairs={{0,1},{1,0},{2,3},{3,2},{4,5},{5,4},{6,7},{7,6},{8,9},{9,8},{10,11... | collective-permute-start | bytes 1572872 | tf_op jit(solution)/shard_map/ppermute | solution.py:66
  120.6 23.7 %collective-permute-start.19 = (bf16[256,1024]{1,0:T(8,128)(2,1)}, bf16[256,1024]{1,0:T(8,128)(2,1)S(1)}, u32[]{:S(2)}, u32[]{:S(2)}) collective-permute-start(bf16[256,1024]{1,0:T(8,128)(2,1)} %get-tuple-element.119.refs_0_.refs_3_), channel_id=1, source_target_pairs={{0,2},{1,3},{2,0},{3,1},{4,6},{5,7},{6,4},{7,5},{8,10},{9,11},{10,... | collective-permute-start | bytes 1572872 | tf_op jit(solution)/shard_map/ppermute | solution.py:66
  142.4 14.7 %copy-start.38 = (bf16[256,1024]{1,0:T(8,128)(2,1)}, bf16[256,1024]{1,0:T(8,128)(2,1)S(1)}, u32[]{:S(2)}) copy-start(bf16[256,1024]{1,0:T(8,128)(2,1)S(1)} %collective-permute-done.18.refs_1_.refs_4_) | copy-start | bytes 1572868
  144.3 12.9 %copy-start.39 = (bf16[256,1024]{1,0:T(8,128)(2,1)}, bf16[256,1024]{1,0:T(8,128)(2,1)S(1)}, u32[]{:S(2)}) copy-start(bf16[256,1024]{1,0:T(8,128)(2,1)S(1)} %collective-permute-done.19.refs_2_.refs_5_) | copy-start | bytes 1572868
  144.3 12.9 %collective-permute-start.20 = (bf16[256,1024]{1,0:T(8,128)(2,1)S(1)}, bf16[256,1024]{1,0:T(8,128)(2,1)S(1)}, u32[]{:S(2)}, u32[]{:S(2)}) collective-permute-start(bf16[256,1024]{1,0:T(8,128)(2,1)S(1)} %collective-permute-done.19.refs_2_.refs_5_), channel_id=1, source_target_pairs={{0,1},{1,0},{2,3},{3,2},{4,5},{5,4},{6,7},{7,6},{8,9},{9,8},{10,11... | collective-permute-start | bytes 1572872 | tf_op jit(solution)/shard_map/ppermute | solution.py:66
  209.7 12.8 %copy-start.11 = (bf16[256,1024]{1,0:T(8,128)(2,1)S(1)}, bf16[256,1024]{1,0:T(8,128)(2,1)}, u32[]{:S(2)}) copy-start(bf16[256,1024]{1,0:T(8,128)(2,1)} %get-tuple-element.132) | copy-start | bytes 1572868
  209.7 13.0 %copy-start.41 = (bf16[256,1024]{1,0:T(8,128)(2,1)S(1)}, bf16[256,1024]{1,0:T(8,128)(2,1)}, u32[]{:S(2)}) copy-start(bf16[256,1024]{1,0:T(8,128)(2,1)} %get-tuple-element.138) | copy-start | bytes 1572868
  209.7 12.7 %collective-permute-start.21 = (bf16[256,1024]{1,0:T(8,128)(2,1)}, bf16[256,1024]{1,0:T(8,128)(2,1)S(1)}, u32[]{:S(2)}, u32[]{:S(2)}) collective-permute-start(bf16[256,1024]{1,0:T(8,128)(2,1)} %get-tuple-element.133), channel_id=1, source_target_pairs={{0,1},{1,0},{2,3},{3,2},{4,5},{5,4},{6,7},{7,6},{8,9},{9,8},{10,11... | collective-permute-start | bytes 1572872 | tf_op jit(solution)/shard_map/ppermute | solution.py:66
  222.6 26.3 %collective-permute-start.23 = (bf16[256,1024]{1,0:T(8,128)(2,1)S(1)}, bf16[256,1024]{1,0:T(8,128)(2,1)S(1)}, u32[]{:S(2)}, u32[]{:S(2)}) collective-permute-start(bf16[256,1024]{1,0:T(8,128)(2,1)S(1)} %add_convert_fusion.6), channel_id=1, source_target_pairs={{0,2},{1,3},{2,0},{3,1},{4,6},{5,7},{6,4},{7,5},{8,10},{9,11},{10,... | collective-permute-start | bytes 1572872 | tf_op jit(solution)/shard_map/ppermute | solution.py:66
  222.7 26.2 %collective-permute-start.22 = (bf16[256,1024]{1,0:T(8,128)(2,1)S(1)}, bf16[256,1024]{1,0:T(8,128)(2,1)S(1)}, u32[]{:S(2)}, u32[]{:S(2)}) collective-permute-start(bf16[256,1024]{1,0:T(8,128)(2,1)S(1)} %copy-done.41), channel_id=1, source_target_pairs={{0,1},{1,0},{2,3},{3,2},{4,5},{5,4},{6,7},{7,6},{8,9},{9,8},{10,11... | collective-permute-start | bytes 1572872 | tf_op jit(solution)/shard_map/ppermute | solution.py:66
  254.6 14.7 %copy-start.9 = (bf16[256,1024]{1,0:T(8,128)(2,1)S(1)}, bf16[256,1024]{1,0:T(8,128)(2,1)}, u32[]{:S(2)}) copy-start(bf16[256,1024]{1,0:T(8,128)(2,1)} %get-tuple-element.130) | copy-start | bytes 1572868
  254.6 14.7 %collective-permute-start.24 = (bf16[256,1024]{1,0:T(8,128)(2,1)S(1)}, bf16[256,1024]{1,0:T(8,128)(2,1)S(1)}, u32[]{:S(2)}, u32[]{:S(2)}) collective-permute-start(bf16[256,1024]{1,0:T(8,128)(2,1)S(1)} %copy-done.37), channel_id=1, source_target_pairs={{0,1},{1,0},{2,3},{3,2},{4,5},{5,4},{6,7},{7,6},{8,9},{9,8},{10,11... | collective-permute-start | bytes 1572872 | tf_op jit(solution)/shard_map/ppermute | solution.py:66
  256.0 14.7 %collective-permute-start.27 = (bf16[256,256]{1,0:T(8,128)(2,1)}, bf16[256,256]{1,0:T(8,128)(2,1)S(1)}, u32[]{:S(2)}, u32[]{:S(2)}) collective-permute-start(bf16[256,256]{1,0:T(8,128)(2,1)} %get-tuple-element.145), channel_id=1, source_target_pairs={{0,1},{1,0},{2,3},{3,2},{4,5},{5,4},{6,7},{7,6},{8,9},{9,8},{10,11... | collective-permute-start | bytes 393224 | tf_op jit(solution)/shard_map/ppermute | solution.py:66
  257.2 16.1 %collective-permute-start.28 = (bf16[256,256]{1,0:T(8,128)(2,1)}, bf16[256,256]{1,0:T(8,128)(2,1)S(1)}, u32[]{:S(2)}, u32[]{:S(2)}) collective-permute-start(bf16[256,256]{1,0:T(8,128)(2,1)} %get-tuple-element.146), channel_id=1, source_target_pairs={{0,2},{1,3},{2,0},{3,1},{4,6},{5,7},{6,4},{7,5},{8,10},{9,11},{10,... | collective-permute-start | bytes 393224 | tf_op jit(solution)/shard_map/ppermute | solution.py:66
  258.9 14.3 %collective-permute-start.29 = (bf16[256,256]{1,0:T(8,128)(2,1)}, bf16[256,256]{1,0:T(8,128)(2,1)S(1)}, u32[]{:S(2)}, u32[]{:S(2)}) collective-permute-start(bf16[256,256]{1,0:T(8,128)(2,1)} %get-tuple-element.147), channel_id=1, source_target_pairs={{0,3},{1,2},{2,1},{3,0},{4,7},{5,6},{6,5},{7,4},{8,11},{9,10},{10,... | collective-permute-start | bytes 393224 | tf_op jit(solution)/shard_map/ppermute | solution.py:66
  263.4 12.8 %copy-start.7 = (bf16[4,1024,128]{2,1,0:T(8,128)(2,1)S(1)}, bf16[4,1024,128]{2,1,0:T(8,128)(2,1)}, u32[]{:S(2)}) copy-start(bf16[4,1024,128]{2,1,0:T(8,128)(2,1)} %get-tuple-element.143) | copy-start | bytes 3145732
  273.2 3.0 collective-permute-start.30
  273.3 25.9 %collective-permute-start.26 = (bf16[256,1024]{1,0:T(8,128)(2,1)}, bf16[256,1024]{1,0:T(8,128)(2,1)}, u32[]{:S(2)}, u32[]{:S(2)}) collective-permute-start(bf16[256,1024]{1,0:T(8,128)(2,1)} %add_convert_fusion.5), channel_id=1, source_target_pairs={{0,2},{1,3},{2,0},{3,1},{4,6},{5,7},{6,4},{7,5},{8,10},{9,11},{10,... | collective-permute-start | bytes 1572872 | tf_op jit(solution)/shard_map/ppermute | solution.py:66
  275.8 24.5 %collective-permute-start.25 = (bf16[256,1024]{1,0:T(8,128)(2,1)}, bf16[256,1024]{1,0:T(8,128)(2,1)}, u32[]{:S(2)}, u32[]{:S(2)}) collective-permute-start(bf16[256,1024]{1,0:T(8,128)(2,1)} %get-tuple-element.141), channel_id=1, source_target_pairs={{0,1},{1,0},{2,3},{3,2},{4,5},{5,4},{6,7},{7,6},{8,9},{9,8},{10,11... | collective-permute-start | bytes 1572872 | tf_op jit(solution)/shard_map/ppermute | solution.py:66
  278.3 19.0 %collective-permute-start.31 = (bf16[2,1024,128]{2,1,0:T(8,128)(2,1)}, bf16[2,1024,128]{2,1,0:T(8,128)(2,1)}, u32[]{:S(2)}, u32[]{:S(2)}) collective-permute-start(bf16[2,1024,128]{2,1,0:T(8,128)(2,1)} %slice.151), channel_id=1, source_target_pairs={{0,8},{4,12},{8,0},{12,4},{16,24},{20,28},{24,16},{28,20},{1,9},{5... | collective-permute-start | bytes 1572872 | tf_op jit(solution)/shard_map/ppermute | solution.py:99
  279.5 17.8 %copy-start.4 = (bf16[4,1024,128]{2,1,0:T(8,128)(2,1)S(1)}, bf16[4,1024,128]{2,1,0:T(8,128)(2,1)}, u32[]{:S(2)}) copy-start(bf16[4,1024,128]{2,1,0:T(8,128)(2,1)} %copy-done.3) | copy-start | bytes 3145732
  300.3 15.8 %collective-permute-start.33 = (bf16[1,1024,128]{2,1,0:T(8,128)(2,1)S(1)}, bf16[1,1024,128]{2,1,0:T(8,128)(2,1)S(1)}, u32[]{:S(2)}, u32[]{:S(2)}) collective-permute-start(bf16[1,1024,128]{2,1,0:T(8,128)(2,1)S(1)} %slice.153), channel_id=1, source_target_pairs={{0,16},{4,20},{8,24},{12,28},{16,0},{20,4},{24,8},{28,12},{1,17},{... | collective-permute-start | bytes 786440 | tf_op jit(solution)/shard_map/ppermute | solution.py:99
  308.1 23.0 %collective-permute-start.32 = (bf16[256,1024]{1,0:T(8,128)(2,1)}, bf16[256,1024]{1,0:T(8,128)(2,1)S(1)}, u32[]{:S(2)}, u32[]{:S(2)}) collective-permute-start(bf16[256,1024]{1,0:T(8,128)(2,1)} %get-tuple-element.164), channel_id=1, source_target_pairs={{0,1},{1,0},{2,3},{3,2},{4,5},{5,4},{6,7},{7,6},{8,9},{9,8},{10,11... | collective-permute-start | bytes 1572872 | tf_op jit(solution)/shard_map/ppermute | solution.py:66
  312.6 10.7 %collective-permute-start.34 = (f32[8,1024]{1,0:T(8,128)}, f32[8,1024]{1,0:T(8,128)S(1)}, u32[]{:S(2)}, u32[]{:S(2)}) collective-permute-start(f32[8,1024]{1,0:T(8,128)} %get-tuple-element.167.refs_0_), channel_id=1, source_target_pairs={{0,1},{1,0},{2,3},{3,2},{4,5},{5,4},{6,7},{7,6},{8,9},{9,8},{10,11... | collective-permute-start | bytes 98312 | tf_op jit(solution)/shard_map/ppermute | solution.py:66
  312.6 12.0 %collective-permute-start.35 = (f32[8,1024]{1,0:T(8,128)}, f32[8,1024]{1,0:T(8,128)S(1)}, u32[]{:S(2)}, u32[]{:S(2)}) collective-permute-start(f32[8,1024]{1,0:T(8,128)} %get-tuple-element.167.refs_0_), channel_id=1, source_target_pairs={{0,2},{1,3},{2,0},{3,1},{4,6},{5,7},{6,4},{7,5},{8,10},{9,11},{10,... | collective-permute-start | bytes 98312 | tf_op jit(solution)/shard_map/ppermute | solution.py:66
  315.5 9.1 %collective-permute-start.36 = (f32[8,1024]{1,0:T(8,128)}, f32[8,1024]{1,0:T(8,128)S(1)}, u32[]{:S(2)}, u32[]{:S(2)}) collective-permute-start(f32[8,1024]{1,0:T(8,128)} %get-tuple-element.167.refs_0_), channel_id=1, source_target_pairs={{0,3},{1,2},{2,1},{3,0},{4,7},{5,6},{6,5},{7,4},{8,11},{9,10},{10,... | collective-permute-start | bytes 98312 | tf_op jit(solution)/shard_map/ppermute | solution.py:66
  316.2 15.0 %copy-start.10 = (bf16[256,1024]{1,0:T(8,128)(2,1)S(1)}, bf16[256,1024]{1,0:T(8,128)(2,1)}, u32[]{:S(2)}) copy-start(bf16[256,1024]{1,0:T(8,128)(2,1)} %get-tuple-element.163) | copy-start | bytes 1572868
  331.3 2.6 collective-permute-start.39
  331.4 30.0 %collective-permute-start.38 = (bf16[256,1024]{1,0:T(8,128)(2,1)S(1)}, bf16[256,1024]{1,0:T(8,128)(2,1)S(1)}, u32[]{:S(2)}, u32[]{:S(2)}) collective-permute-start(bf16[256,1024]{1,0:T(8,128)(2,1)S(1)} %add_convert_fusion.2), channel_id=1, source_target_pairs={{0,2},{1,3},{2,0},{3,1},{4,6},{5,7},{6,4},{7,5},{8,10},{9,11},{10,... | collective-permute-start | bytes 1572872 | tf_op jit(solution)/shard_map/ppermute | solution.py:66
  333.5 23.4 %collective-permute-start.37 = (bf16[256,1024]{1,0:T(8,128)(2,1)}, bf16[256,1024]{1,0:T(8,128)(2,1)S(1)}, u32[]{:S(2)}, u32[]{:S(2)}) collective-permute-start(bf16[256,1024]{1,0:T(8,128)(2,1)} %get-tuple-element.170), channel_id=1, source_target_pairs={{0,1},{1,0},{2,3},{3,2},{4,5},{5,4},{6,7},{7,6},{8,9},{9,8},{10,11... | collective-permute-start | bytes 1572872 | tf_op jit(solution)/shard_map/ppermute | solution.py:66
  334.2 31.4 %collective-permute-start.40 = (bf16[2,784,128]{2,1,0:T(8,128)(2,1)S(1)}, bf16[2,784,128]{2,1,0:T(8,128)(2,1)S(1)}, u32[]{:S(2)}, u32[]{:S(2)}) collective-permute-start(bf16[2,784,128]{2,1,0:T(8,128)(2,1)S(1)} %slice.155), channel_id=1, source_target_pairs={{0,8},{4,12},{8,0},{12,4},{16,24},{20,28},{24,16},{28,20},{1,9},{5... | collective-permute-start | bytes 1204232 | tf_op jit(solution)/shard_map/ppermute | solution.py:99
  356.9 9.2 %collective-permute-start.44 = (bf16[256,128]{1,0:T(8,128)(2,1)S(1)}, bf16[256,128]{1,0:T(8,128)(2,1)S(1)}, u32[]{:S(2)}, u32[]{:S(2)}) collective-permute-start(bf16[256,128]{1,0:T(8,128)(2,1)S(1)} %get-tuple-element.186), channel_id=1, source_target_pairs={{0,3},{1,2},{2,1},{3,0},{4,7},{5,6},{6,5},{7,4},{8,11},{9,10},{10,... | collective-permute-start | bytes 196616 | tf_op jit(solution)/shard_map/ppermute | solution.py:66
  358.6 7.6 %collective-permute-start.43 = (bf16[256,128]{1,0:T(8,128)(2,1)S(1)}, bf16[256,128]{1,0:T(8,128)(2,1)S(1)}, u32[]{:S(2)}, u32[]{:S(2)}) collective-permute-start(bf16[256,128]{1,0:T(8,128)(2,1)S(1)} %get-tuple-element.187), channel_id=1, source_target_pairs={{0,2},{1,3},{2,0},{3,1},{4,6},{5,7},{6,4},{7,5},{8,10},{9,11},{10,... | collective-permute-start | bytes 196616 | tf_op jit(solution)/shard_map/ppermute | solution.py:66
  360.0 6.2 %collective-permute-start.42 = (bf16[256,128]{1,0:T(8,128)(2,1)S(1)}, bf16[256,128]{1,0:T(8,128)(2,1)S(1)}, u32[]{:S(2)}, u32[]{:S(2)}) collective-permute-start(bf16[256,128]{1,0:T(8,128)(2,1)S(1)} %get-tuple-element.185), channel_id=1, source_target_pairs={{0,1},{1,0},{2,3},{3,2},{4,5},{5,4},{6,7},{7,6},{8,9},{9,8},{10,11... | collective-permute-start | bytes 196616 | tf_op jit(solution)/shard_map/ppermute | solution.py:66
  365.8 11.3 %collective-permute-start.41 = (bf16[1,784,128]{2,1,0:T(8,128)(2,1)S(1)}, bf16[1,784,128]{2,1,0:T(8,128)(2,1)S(1)}, u32[]{:S(2)}, u32[]{:S(2)}) collective-permute-start(bf16[1,784,128]{2,1,0:T(8,128)(2,1)S(1)} %slice.128), channel_id=1, source_target_pairs={{0,16},{4,20},{8,24},{12,28},{16,0},{20,4},{24,8},{28,12},{1,17},{... | collective-permute-start | bytes 602120 | tf_op jit(solution)/shard_map/ppermute | solution.py:99
  (33 other events, 108.2 us)
Sparse Core Ops, SparseCore 0:
  10.6 108.3 all-gather.2
  249.1 133.9 reduce-scatter.1
where the time goes:
time: 397 us; the launch traced here: 394 us
  Pallas kernels  153 us (39%)
  waiting for transfers between devices  137 us (35%)
  starting transfers between devices  53.6 us (14%)
  local copies, waits for them, and re-layouts  19.4 us (5%)
  other arithmetic  15.6 us (4%)
  between operations  14.7 us (4%)
    ppermute x33, waiting for transfers between devices, z_swap(): return lax.ppermute(x, 'tensor', [(i, i ^ mask) for i in range(size)])  108 us
    ppermute x33, starting transfers between devices, z_swap(): return lax.ppermute(x, 'tensor', [(i, i ^ mask) for i in range(size)])  46.4 us
    pallas_call x1, Pallas kernels, units_call(): pl.pallas_call(functools.partial(units_body, chunks, unit), grid=(ff // B...  32 us
    pallas_call x2, Pallas kernels, product_call(): pl.pallas_call(functools.partial(product_body, len(xs), chunks, bool(extr...  30.2 us
    pallas_call x1, Pallas kernels, wgrad_call(): pl.pallas_call(functools.partial(wgrad_body, count, chunks), grid=(ff //...  25 us
    pallas_call x1, Pallas kernels, attn_fwd(): pl.pallas_call(functools.partial(fwd_body, total, chunks), grid=(heads,),...  16.3 us
    pallas_call x1, Pallas kernels, attn_bwd(): pl.pallas_call(functools.partial(bwd_body, total, chunks), grid=(heads,),...  15 us
    ppermute x6, waiting for transfers between devices, dp_step(): other = lax.ppermute(x, 'dp', [(i, i ^ bit) for i in range(8)])  13.7 us
  transfers between devices with their start and end apart: 47, of which 24 were waited for; matrix products, arithmetic and copies ran while one was open for 5% of the time, Pallas kernels for 26%

commit v1 on v0

--- a/solution.py
+++ b/solution.py
@@ -87,7 +87,8 @@
 
 
 def dp_slots(ranks):
-    return ((ranks >> 1) & 3) | ((ranks & 1) << 2)
+    x, y, core = (ranks >> 1) & 1, (ranks >> 2) & 1, ranks & 1
+    return jnp.concatenate([x | (y << 1) | (core << 2), y | (x << 1) | (core << 2)])
 
 
 def dp_step(x, bit):
@@ -114,23 +115,27 @@
         yield (keep_ref if j < half else send_ref), j % half, order_ref[j]
 
 
-def join_rows(ref, index_ref, count, rows):
-    if count == 1:
-        return ref[0, 0:rows, :]
-    return jnp.concatenate([ref[index_ref[c], 0:rows, :] for c in range(count)], 0)
+def join_rows(first_ref, last_ref, index_ref, count, rows):
+    split = first_ref.shape[1]
+    pieces = []
+    for c in range(count):
+        pieces.append(first_ref[index_ref[c], :, :])
+        pieces.append(last_ref[index_ref[count + c], 0 : rows - split, :])
+    return jnp.concatenate(pieces, 0)
 
 
 def qkv_body(count, chunks, rows, index_ref, place_ref, *refs):
     toks = refs[:chunks]
-    pack_ref, small_ref = refs[chunks : chunks + 2]
-    n1_ref, q_ref, k_ref, v_ref, kt_ref, vt_ref, gains_ref, router_ref = refs[chunks + 2 :]
+    first_ref, last_ref, small_ref = refs[chunks : chunks + 3]
+    n1_ref, q_ref, k_ref, v_ref, kt_ref, vt_ref, gains_ref, router_ref = refs[chunks + 3 :]
     depth = n1_ref.shape[1] // count
-    weights = join_rows(pack_ref, index_ref, count, depth)
+    weights = join_rows(first_ref, last_ref, index_ref, count, depth)
     width = q_ref.shape[1]
     if count == 1:
         small = [small_ref[r : r + 1, :] for r in range(2 + EXPERTS)]
     else:
-        lines = [small_ref[index_ref[d], depth : depth + 1, :].astype(F32) for d in range(count)]
+        row = depth - first_ref.shape[1]
+        lines = [small_ref[index_ref[count + d], row : row + 1, :].astype(F32) for d in range(count)]
         small = [
             jnp.concatenate([x[:, depth * r : depth * (r + 1)] for x in lines], 1) for r in range(2 + EXPERTS)
         ]
@@ -161,15 +166,15 @@
     total = chunks * rows
     shapes = [(total, depth)] + [(total, width)] * 3 + [(width, total)] * 2
     return pl.pallas_call(
-        functools.partial(qkv_body, pack.shape[0], chunks, rows),
-        in_specs=[sspec(), sspec()] + [vspec()] * (chunks + 2),
+        functools.partial(qkv_body, pack[0].shape[0], chunks, rows),
+        in_specs=[sspec(), sspec()] + [vspec()] * (chunks + 3),
         out_specs=[vspec()] * 8,
         out_shape=[jax.ShapeDtypeStruct(s, BF) for s in shapes]
         + [jax.ShapeDtypeStruct((8, depth), F32), jax.ShapeDtypeStruct((128, depth), BF)],
         compiler_params=params(),
         cost_estimate=cost(2 * total * depth * 3 * width, 8 * total * depth),
         name="norm_qkv",
-    )(index, place, *toks, pack, small)
+    )(index, place, *toks, *pack, small)
 
 
 def extents(total):
@@ -388,18 +393,18 @@
     )(place, *grads, chances, q, k, v, kt, ot)
 
 
-def join_lanes(ref, index_ref, count, slot):
-    if count == 1:
-        return ref[0, slot]
-    return jnp.concatenate([ref[index_ref[c], slot] for c in range(count)], 1)
+def join_lanes(low_ref, high_ref, index_ref, count, slot):
+    low = [low_ref[index_ref[c], slot] for c in range(count)]
+    high = [high_ref[index_ref[count + c], slot] for c in range(count)]
+    return jnp.concatenate([jnp.concatenate(low, 1), jnp.concatenate(high, 1)], 0)
 
 
 def mid_body(count, chunks, index_ref, *refs):
     atts = refs[:chunks]
-    w_ref, tok_ref, gain_ref, mid_ref, n2_ref = refs[chunks:]
+    low_ref, high_ref, tok_ref, gain_ref, mid_ref, n2_ref = refs[chunks:]
     u = tok_ref[...].astype(F32)
     for c in range(chunks):
-        u = u + dot_nn(atts[c][...], join_lanes(w_ref, index_ref, count, c))
+        u = u + dot_nn(atts[c][...], join_lanes(low_ref, high_ref, index_ref, count, c))
     mid_ref[...] = u
     scale = lax.rsqrt(jnp.mean(u * u, axis=1, keepdims=True) + EPSILON)
     n2_ref[...] = (u * scale * gain_ref[1:2, :]).astype(BF)
@@ -408,14 +413,14 @@
 def mid_call(index, atts, w_out, tok, gains):
     chunks = len(atts)
     return pl.pallas_call(
-        functools.partial(mid_body, w_out.shape[0], chunks),
-        in_specs=[sspec()] + [vspec()] * (chunks + 3),
+        functools.partial(mid_body, w_out[0].shape[0], chunks),
+        in_specs=[sspec()] + [vspec()] * (chunks + 4),
         out_specs=[vspec()] * 2,
         out_shape=[jax.ShapeDtypeStruct(tok.shape, F32), jax.ShapeDtypeStruct(tok.shape, BF)],
         compiler_params=params(),
         cost_estimate=cost(2 * tok.shape[0] * tok.shape[1] ** 2, 4 * tok.shape[1] ** 2),
         name="out_projection_norm",
-    )(index, *atts, w_out, tok, gains)
+    )(index, *atts, *w_out, tok, gains)
 
 
 def split_dot(a, b, dot):
@@ -622,8 +627,8 @@
 
 def resid_body(count, chunks, terms, index_ref, *refs):
     parts = refs[:terms]
-    mid_ref, g_ref, gains_ref, w_ref = refs[terms : terms + 4]
-    rest = refs[terms + 4 :]
+    mid_ref, g_ref, gains_ref, low_ref, high_ref = refs[terms : terms + 5]
+    rest = refs[terms + 5 :]
     resid_ref, aog_ref, gain_ref = rest[:3]
     dos = rest[3:]
     grad = functools.reduce(jnp.add, [p[...].astype(F32) for p in parts])
@@ -634,16 +639,16 @@
     aog_ref[...] = low
     gain_ref[...] = jnp.broadcast_to(gain_part, gain_ref.shape)
     for c in range(chunks):
-        dos[c][...] = dot_nt(low, join_lanes(w_ref, index_ref, count, c)).astype(BF)
+        dos[c][...] = dot_nt(low, join_lanes(low_ref, high_ref, index_ref, count, c)).astype(BF)
 
 
 def resid_call(index, parts, mid, grad, gains, w_out):
-    chunks, terms = w_out.shape[1], len(parts)
+    chunks, terms = w_out[0].shape[1], len(parts)
     shape = mid.shape
-    width = w_out.shape[2]
-    return pl.pallas_call(
-        functools.partial(resid_body, w_out.shape[0], chunks, terms),
-        in_specs=[sspec()] + [vspec()] * (terms + 4),
+    width = 2 * w_out[0].shape[2]
+    return pl.pallas_call(
+        functools.partial(resid_body, w_out[0].shape[0], chunks, terms),
+        in_specs=[sspec()] + [vspec()] * (terms + 5),
         out_specs=[vspec()] * (3 + chunks),
         out_shape=[
             jax.ShapeDtypeStruct(shape, F32),
@@ -654,7 +659,7 @@
         compiler_params=params(),
         cost_estimate=cost(2 * shape[0] * shape[1] ** 2, 4 * shape[1] ** 2),
         name="resid_grad",
-    )(index, *parts, mid, grad, gains, w_out)
+    )(index, *parts, mid, grad, gains, *w_out)
 
 
 def final_body(chunks, *refs):
@@ -677,13 +682,13 @@
     )(*parts, tok, resid, gains)
 
 
-def proj_body(count, chunks, rows, index_ref, place_ref, dq_ref, dk_ref, dv_ref, pack_ref, two_ref, router_ref, *refs):
+def proj_body(count, chunks, rows, index_ref, place_ref, dq_ref, dk_ref, dv_ref, first_ref, last_ref, two_ref, router_ref, *refs):
     toks = refs[:chunks]
     outs = refs[chunks : 2 * chunks]
     gain_ref = refs[2 * chunks]
     depth = outs[0].shape[1]
     width = dq_ref.shape[1]
-    weights = join_rows(pack_ref, index_ref, count, depth // count)
+    weights = join_rows(first_ref, last_ref, index_ref, count, depth // count)
     gain = jnp.zeros((1, depth), F32)
     for c in range(chunks):
         at = pl.ds(pl.multiple_of(place_ref[c] * rows, rows), rows)
@@ -701,14 +706,14 @@
 def proj_call(index, place, dq, dk, dv, pack, gain_two, router_part, toks):
     chunks, rows, depth = len(toks), toks[0].shape[0], toks[0].shape[1]
     return pl.pallas_call(
-        functools.partial(proj_body, pack.shape[0], chunks, rows),
-        in_specs=[sspec(), sspec()] + [vspec()] * (6 + chunks),
+        functools.partial(proj_body, pack[0].shape[0], chunks, rows),
+        in_specs=[sspec(), sspec()] + [vspec()] * (7 + chunks),
         out_specs=[vspec()] * (chunks + 1),
         out_shape=[jax.ShapeDtypeStruct((rows, depth), BF)] * chunks + [jax.ShapeDtypeStruct((8, depth), F32)],
         compiler_params=params(),
         cost_estimate=cost(6 * chunks * rows * depth * dq.shape[1], 8 * chunks * rows * depth),
         name="projection_grads",
-    )(index, place, dq, dk, dv, pack, gain_two, router_part, *toks)
+    )(index, place, dq, dk, dv, *pack, gain_two, router_part, *toks)
 
 
 def attn_weights_body(count, smalls, slot_ref, n1_ref, dq_ref, dk_ref, dv_ref, table_ref, *refs):
@@ -831,22 +836,28 @@
     packed = jnp.concatenate([w_query, w_key, w_value], 1)
     wo_slots = jnp.stack(z_direct([w_output_late] * z_size, z_size))[None]
     ranks = dp_rank ^ jnp.arange(8, dtype=jnp.int32)
+    half = wo_slots.shape[2] // 2
     if direct:
         index = dp_slots(ranks)
         slots = dp_rank ^ dp_scatter_slots(jnp.arange(8, dtype=jnp.int32))
-        pad = jnp.zeros((15, packed.shape[1]), BF)
-        pack = dp_step(jnp.concatenate([packed, small, pad], 0)[None], 2)
-        pack = dp_step(after(pack, near), 4)
-        wo_half = dp_step(after(wo_slots, near, far), 2)
-        pack = dp_step(after(pack, toks[3], wo_half), 1)
-        small_all = pack
+        first = dp_step(packed[:80][None], 2)
+        last = dp_step(jnp.concatenate([packed[80:], small, jnp.zeros((15, packed.shape[1]), BF)], 0)[None], 4)
+        first, last = dp_step(after(first, near), 4), dp_step(after(last, near), 2)
+        wo_low = dp_step(after(wo_slots[:, :, :half], near, far), 2)
+        wo_high = dp_step(after(wo_slots[:, :, half:], near, far), 4)
+        first = dp_step(after(first, toks[3], wo_low, wo_high), 1)
+        last = dp_step(after(last, toks[3], wo_low, wo_high), 1)
+        pack, small_all = [first, last], last
     else:
-        index = slots = jnp.zeros((1,), jnp.int32)
+        slots = jnp.zeros((1,), jnp.int32)
+        index = jnp.zeros((2,), jnp.int32)
         pack = lax.all_gather(packed, "dp", axis=0, tiled=True)[None]
+        pack = [pack[:, : depth // 2], pack[:, depth // 2 :]]
         small_all = lax.all_gather(small[0], "dp", axis=0).reshape(dp_size, 2 + EXPERTS, share)
         small_all = jnp.swapaxes(small_all, 0, 1).reshape(2 + EXPERTS, depth)
         small_all = jnp.concatenate([small_all, jnp.zeros((2, depth), BF)], 0)
         wo_all = lax.all_gather(wo_slots[0], "dp", axis=2, tiled=True)[None]
+        wo_all = [wo_all[:, :, :half], wo_all[:, :, half:]]
 
     local = jnp.stack(
         [
@@ -867,7 +878,8 @@
     chances, ot = fwd[:2]
     atts = z_direct([after(fwd[2], g_near, g_far)] + [after(x, g_near, g_far) for x in fwd[3:]], z_size)
     if direct:
-        wo_all = dp_step(after(dp_step(after(wo_half, n1), 4), atts[1]), 1)
+        wo_low, wo_high = dp_step(after(wo_low, n1), 4), dp_step(after(wo_high, n1), 2)
+        wo_all = [dp_step(after(x, atts[1]), 1) for x in (wo_low, wo_high)]
     gs = [out_grad, g_near, g_far, z_swap(after(g_far, fwd[2]), 1, z_size)]
     mid, n2 = mid_call(index, [after(atts[0], gs[3])] + atts[1:], wo_all, tokens_in, gains)
 

time: 397 us -> 386 us (0.972)
  waiting for transfers between devices: 137 us -> 120 us
  starting transfers between devices: 53.6 us -> 57.7 us
    ppermute x33, waiting for transfers between devices: 108 us -> 99.8 us  [z_swap(): return lax.ppermute(x, 'tensor', [(i, i ^ mask) for i in range(size)])]
    ppermute x6 -> x12, waiting for transfers between devices: 13.7 us -> 5.88 us  [dp_step(): other = lax.ppermute(x, 'dp', [(i, i ^ bit) for i in range(8)])]
    unnamed x107 -> x114, local copies, waits for them, and re-layouts: 10.3 us -> 10.3 us
  transfers between devices with their start and end apart: 47 -> 53, of which waited for: 24 -> 22; matrix products, arithmetic and copies ran while one was open for 5% -> 6% of each run, Pallas kernels for 26% -> 26%
where the time goes in v1:
time: 386 us; the launch traced here: 382 us
  Pallas kernels  152 us (39%)
  waiting for transfers between devices  120 us (31%)
  starting transfers between devices  57.7 us (15%)
  local copies, waits for them, and re-layouts  19.5 us (5%)
  other arithmetic  17 us (4%)
  between operations  14.9 us (4%)
    ppermute x33, waiting for transfers between devices, z_swap(): return lax.ppermute(x, 'tensor', [(i, i ^ mask) for i in range(size)])  99.8 us
    ppermute x33, starting transfers between devices, z_swap(): return lax.ppermute(x, 'tensor', [(i, i ^ mask) for i in range(size)])  45.4 us
    pallas_call x1, Pallas kernels, units_call(): pl.pallas_call(functools.partial(units_body, chunks, unit), grid=(ff // B...  32 us
    pallas_call x2, Pallas kernels, product_call(): pl.pallas_call(functools.partial(product_body, len(xs), chunks, bool(extr...  30.2 us
    pallas_call x1, Pallas kernels, wgrad_call(): pl.pallas_call(functools.partial(wgrad_body, count, chunks), grid=(ff //...  25 us
    pallas_call x1, Pallas kernels, attn_fwd(): pl.pallas_call(functools.partial(fwd_body, total, chunks), grid=(heads,),...  16.3 us
    pallas_call x1, Pallas kernels, attn_bwd(): pl.pallas_call(functools.partial(bwd_body, total, chunks), grid=(heads,),...  15 us
    ppermute x6, waiting for transfers between devices, dp_fold(): other = lax.ppermute(send, 'dp', [(i, i ^ bit) for i in range(8)])  14.7 us
  transfers between devices with their start and end apart: 53, of which 22 were waited for; matrix products, arithmetic and copies ran while one was open for 6% of the time, Pallas kernels for 26%

profile of v1, /device:TPU:14, one launch (start us, length us, event | category | flops | bytes accessed | tf_op | source)
XLA Modules:
  0.0 382.5 jit_solution(13357271423722662911)
XLA Ops:
  7.2 3.1 pad_maximum_fusion
  11.9 2.6 collective-permute-start.1
  16.0 2.3 reduce-window.6
  19.1 1.6 fusion.2.refs_8_
  21.7 15.8 %collective-permute-done.1.refs_2_ = bf16[256,1024]{1,0:T(8,128)(2,1)S(1)} collective-permute-done((bf16[256,1024]{1,0:T(8,128)(2,1)S(1)}, bf16[256,1024]{1,0:T(8,128)(2,1)S(1)}, u32[]{:S(2)}, u32[]{:S(2)}) %collective-permute-start.1) | collective-permute-done | bytes 524320 | tf_op jit(solution)/shard_map/ppermute | solution.py:66
  37.9 3.5 collective-permute-start.6
  41.5 2.0 collective-permute-start.2
  44.6 1.2 collective-permute-done.6
  45.7 1.5 collective-permute-done.5
  48.5 4.3 %collective-permute-done.8 = bf16[1,4,128,128]{3,2,1,0:T(8,128)(2,1)S(1)} collective-permute-done((bf16[1,4,128,128]{3,2,1,0:T(8,128)(2,1)S(1)}, bf16[1,4,128,128]{3,2,1,0:T(8,128)(2,1)S(1)}, u32[]{:S(2)}, u32[]{:S(2)}) %collective-permute-start.8) | collective-permute-done | bytes 131104 | tf_op jit(solution)/shard_map/ppermute | solution.py:95
  52.9 1.5 collective-permute-done.9
  56.6 1.1 collective-permute-start.14
  57.7 1.4 collective-permute-start.15
  60.2 1.0 copy-done.19
  61.2 6.6 %norm_qkv.1 = (bf16[1024,1024]{1,0:T(8,128)(2,1)}, bf16[1024,256]{1,0:T(8,128)(2,1)}, bf16[1024,256]{1,0:T(8,128)(2,1)}, bf16[1024,256]{1,0:T(8,128)(2,1)}, bf16...) custom-call(s32[16]{0:T(128)} %pad_add_fusion.index_ref, ...), custom_call_target="tpu_custom_call" | custom-call | flops 1610612736 | bytes 8388608 | tf_op jit(solution)/shard_map/norm_qkv/pallas_call | solution.py:168
  67.8 1.5 collective-permute-start.20
  69.9 16.3 %attn_forward.1 = (bf16[4,1024,1024]{2,1,0:T(8,128)(2,1)}, f32[256,1024]{1,0:T(8,128)}, bf16[256,256]{1,0:T(8,128)(2,1)}, bf16[256,256]{1,0:T(8,128)(2,1)}, bf16...) custom-call(s32[1,2]{1,0:T(1,128)} %starts_ref.1, s32[4]{0:T(128)} %iota_xor_fusion.place_ref, ...), custom_call_target="tpu_custom_call" | custom-call | flops 4294967296 | bytes 10485760 | tf_op jit(solution)/shard_map/attn_forward/pallas_call | solution.py:255
  86.3 1.7 collective-permute-start.17
  88.4 4.6 %collective-permute-done.17.refs_1_ = bf16[256,256]{1,0:T(8,128)(2,1)S(1)} collective-permute-done((bf16[256,256]{1,0:T(8,128)(2,1)}, bf16[256,256]{1,0:T(8,128)(2,1)S(1)}, u32[]{:S(2)}, u32[]{:S(2)}) %collective-permute-start.17) | collective-permute-done | bytes 131104 | tf_op jit(solution)/shard_map/ppermute | solution.py:66
  93.6 1.0 collective-permute-start.18
  94.6 2.1 collective-permute-start.19
  96.8 8.5 %collective-permute-done.16.refs_7_.refs_10_ = bf16[256,1024]{1,0:T(8,128)(2,1)S(1)} collective-permute-done((bf16[256,1024]{1,0:T(8,128)(2,1)S(1)}, bf16[256,1024]{1,0:T(8,128)(2,1)S(1)}, u32[]{:S(2)}, u32[]{:S(2)}) %collective-permute-start.16) | collective-permute-done | bytes 524320 | tf_op jit(solution)/shard_map/ppermute | solution.py:66
  105.5 1.1 collective-permute-done.18.refs_2_
  106.6 2.2 collective-permute-done.19.refs_3_
  109.5 3.8 out_projection_norm.1
  114.7 19.4 %collective-permute-done.24.refs_1_.refs_4_ = bf16[256,1024]{1,0:T(8,128)(2,1)S(1)} collective-permute-done((bf16[256,1024]{1,0:T(8,128)(2,1)}, bf16[256,1024]{1,0:T(8,128)(2,1)S(1)}, u32[]{:S(2)}, u32[]{:S(2)}) %collective-permute-start.24) | collective-permute-done | bytes 524320 | tf_op jit(solution)/shard_map/ppermute | solution.py:66
  134.0 1.9 collective-permute-done.25.refs_2_.refs_5_
  136.0 2.3 collective-permute-start.26
  138.2 9.3 %collective-permute-done.26.refs_3_.refs_6_ = bf16[256,1024]{1,0:T(8,128)(2,1)S(1)} collective-permute-done((bf16[256,1024]{1,0:T(8,128)(2,1)S(1)}, bf16[256,1024]{1,0:T(8,128)(2,1)S(1)}, u32[]{:S(2)}, u32[]{:S(2)}) %collective-permute-start.26) | collective-permute-done | bytes 524320 | tf_op jit(solution)/shard_map/ppermute | solution.py:66
  148.3 32.0 %expert_units.1 = (bf16[1024,2816]{1,0:T(8,128)(2,1)}, bf16[1024,2816]{1,0:T(8,128)(2,1)}, bf16[1024,2816]{1,0:T(8,128)(2,1)}, f32[1024,128]{1,0:T(8,128)}, f32[8,1024]{1,0:T(8,128)}) custom-call(s32[4]{0:T(128)} %iota_xor_fusion.place_ref, bf16[256,1024]{1,0:T(8,128)(2,1)} %get-tuple-element.129.refs_0_.refs_3_, bf16[256,1024]{1,0:T(8,128)(2,1)} %copy-done.41, ...), custom_call_target="tpu_custom_call" | custom-call | flops 17716740096 | bytes 29884416 | tf_op jit(solution)/shard_map/expert_units/pallas_call | solution.py:518
  180.3 19.7 %normed_two_grads.1 = (bf16[256,1024]{1,0:T(8,128)(2,1)}, bf16[256,1024]{1,0:T(8,128)(2,1)}, bf16[256,1024]{1,0:T(8,128)(2,1)}, bf16[256,1024]{1,0:T(8,128)(2,1)}) custom-call(bf16[1024,2816]{1,0:T(8,128)(2,1)} %get-tuple-element.133.refs_0_.refs_1_, bf16[1024,2816]{1,0:T(8,128)(2,1)} %get-tuple-element.134.refs_1_.refs_2_, ...), custom_call_target="tpu_custom_call" | custom-call | flops 11811160064 | bytes 23068672 | tf_op jit(solution)/shard_map/normed_two_grads/pallas_call | solution.py:568
  200.1 2.0 collective-permute-start.27
  202.0 10.5 %expert_out.1 = (bf16[256,1024]{1,0:T(8,128)(2,1)}, bf16[256,1024]{1,0:T(8,128)(2,1)}, bf16[256,1024]{1,0:T(8,128)(2,1)}, bf16[256,1024]{1,0:T(8,128)(2,1)}) custom-call(bf16[1024,2816]{1,0:T(8,128)(2,1)} %get-tuple-element.145.refs_0_, bf16[8,3,2816,128]{3,2,1,0:T(8,128)(2,1)} %bitcast.81), custom_call_target="tpu_custom_call" | custom-call | flops 5905580032 | bytes 11534336 | tf_op jit(solution)/shard_map/expert_out/pallas_call | solution.py:568
  213.4 1.8 collective-permute-start.28
  215.2 25.0 %expert_weight_grads.1 = bf16[8,3,2816,128]{3,2,1,0:T(8,128)(2,1)} custom-call(bf16[1024,2816]{1,0:T(8,128)(2,1)} %get-tuple-element.145.refs_0_, bf16[1024,2816]{1,0:T(8,128)(2,1)} %get-tuple-element.133.refs_0_.refs_1_, bf16[1024,2816]{1,0:T(8,128)(2,1)} %get-tuple-element.134.refs_1_.refs_2_, bf16[256,1024]{1,0:T(8,128)(2,1)} %get-tuple-element.129.refs_0_.refs_3_, ...), custom_call_target="tpu_custom_call" | custom-call | flops 17716740096 | bytes 34603008 | tf_op jit(solution)/shard_map/expert_weight_grads/pallas_call | solution.py:608
  241.2 4.9 %resid_grad.1 = (f32[256,1024]{1,0:T(8,128)}, bf16[256,1024]{1,0:T(8,128)(2,1)}, f32[8,1024]{1,0:T(8,128)}, bf16[256,256]{1,0:T(8,128)(2,1)}, bf16[256,256]{1,0:...) custom-call(s32[16]{0:T(128)} %pad_add_fusion.index_ref, ...), custom_call_target="tpu_custom_call" | custom-call | flops 536870912 | bytes 4194304 | tf_op jit(solution)/shard_map/resid_grad/pallas_call | solution.py:649
  246.9 1.8 collective-permute-start.33
  249.3 1.0 collective-permute-start.35
  250.4 3.9 %w_output_grad.1 = (bf16[4,1024,128]{2,1,0:T(8,128)(2,1)}, bf16[4,1024,128]{2,1,0:T(8,128)(2,1)}) custom-call(s32[8]{0:T(128)} %fusion.17.slot_ref, bf16[256,256]{1,0:T(8,128)(2,1)} %get-tuple-element.115.refs_0_, bf16[256,256]{1,0:T(8,128)(2,1)} %copy-done.22, bf16[256,256]{1,0:T(8,128)(2,1)} %copy-done.23, bf16[256,256]{1,0:T(8,128)(2,1)} %copy-done.24, ...), custom_call_target="tpu_custom_call" | custom-call | flops 536870912 | bytes 4194304 | tf_op jit(solution)/shard_map/w_output_grad/pallas_call | solution.py:771
  254.3 5.5 %collective-permute-done.30 = bf16[256,1024]{1,0:T(8,128)(2,1)S(1)} collective-permute-done((bf16[256,1024]{1,0:T(8,128)(2,1)S(1)}, bf16[256,1024]{1,0:T(8,128)(2,1)S(1)}, u32[]{:S(2)}, u32[]{:S(2)}) %collective-permute-start.30) | collective-permute-done | bytes 524320 | tf_op jit(solution)/shard_map/ppermute | solution.py:66
  259.8 1.0 add_convert_fusion.5
  261.2 1.9 collective-permute-done.34.refs_2_
  263.1 3.2 collective-permute-start.32
  266.4 1.1 collective-permute-done.36
  267.8 1.0 copy-done.4
  269.6 1.1 collective-permute-start.37
  270.7 15.0 %attn_backward.1 = (bf16[1024,256]{1,0:T(8,128)(2,1)}, bf16[1024,256]{1,0:T(8,128)(2,1)}, bf16[1024,256]{1,0:T(8,128)(2,1)}, f32[4,5,512]{2,1,0:T(8,128)}) custom-call(s32[4]{0:T(128)} %iota_xor_fusion.place_ref, bf16[256,256]{1,0:T(8,128)(2,1)} %get-tuple-element.154.refs_0_, bf16[256,256]{1,0:T(8,128)(2,1)} %copy-done.45, bf16[256,256]{1,0:T(8,128)(2,1)} %copy-done.46, ...), custom_call_target="tpu_custom_call" | custom-call | flops 171798691840 | bytes 10485760 | tf_op jit(solution)/shard_map/attn_backward/pallas_call | solution.py:370
  285.7 3.2 collective-permute-done.37
  288.9 1.2 add_convert_fusion.3
  290.2 3.3 collective-permute-start.39
  293.5 5.8 %projection_grads.1 = (bf16[256,1024]{1,0:T(8,128)(2,1)}, bf16[256,1024]{1,0:T(8,128)(2,1)}, bf16[256,1024]{1,0:T(8,128)(2,1)}, bf16[256,1024]{1,0:T(8,128)(2,1)}, f32[8,1024]{1,0:T(8,128)}) custom-call(s32[16]{0:T(128)} %pad_add_fusion.index_ref, s32[4]{0:T(128)} %iota_xor_fusion.place_ref, bf16[1024,256]{1,0:T(8,128)(2,1)} %get-tuple-element.166.dq_ref, ...), custom_call_target="tpu_custom_call" | custom-call | flops 1610612736 | bytes 8388608 | tf_op jit(solution)/shard_map/projection_grads/pallas_call | solution.py:708
  299.3 2.8 collective-permute-start.38
  303.8 2.9 collective-permute-start.42
  306.8 7.0 %collective-permute-done.40.refs_1_ = f32[8,1024]{1,0:T(8,128)S(1)} collective-permute-done((f32[8,1024]{1,0:T(8,128)}, f32[8,1024]{1,0:T(8,128)S(1)}, u32[]{:S(2)}, u32[]{:S(2)}) %collective-permute-start.40) | collective-permute-done | bytes 32800 | tf_op jit(solution)/shard_map/ppermute | solution.py:66
  315.4 5.3 %attn_weight_grads.1 = (bf16[4,784,128]{2,1,0:T(8,128)(2,1)}, bf16[4,784,128]{2,1,0:T(8,128)(2,1)}) custom-call(s32[8]{0:T(128)} %fusion.17.slot_ref, bf16[1024,1024]{1,0:T(8,128)(2,1)} %get-tuple-element.122.n1_ref, bf16[1024,256]{1,0:T(8,128)(2,1)} %get-tuple-element.166.dq_ref, bf16[1024,256]{1,0:T(8,128)(2,1)} %get-tuple-element.167.dk_ref, ...), custom_call_target="tpu_custom_call" | custom-call | flops 1610612736 | bytes 8388608 | tf_op jit(solution)/shard_map/attn_weight_grads/pallas_call | solution.py:744
  321.0 2.2 collective-permute-start.44
  323.9 1.4 add_convert_fusion.1
  325.4 1.0 collective-permute-start.46
  326.4 2.4 add_convert_fusion.4
  328.8 18.7 %collective-permute-done.43.refs_1_ = bf16[256,1024]{1,0:T(8,128)(2,1)S(1)} collective-permute-done((bf16[256,1024]{1,0:T(8,128)(2,1)}, bf16[256,1024]{1,0:T(8,128)(2,1)S(1)}, u32[]{:S(2)}, u32[]{:S(2)}) %collective-permute-start.43) | collective-permute-done | bytes 524320 | tf_op jit(solution)/shard_map/ppermute | solution.py:66
  348.2 3.6 collective-permute-start.49
  352.6 3.6 in_grad.1
  357.2 10.4 %collective-permute-done.47 = bf16[1,784,128]{2,1,0:T(8,128)(2,1)S(1)} collective-permute-done((bf16[1,784,128]{2,1,0:T(8,128)(2,1)S(1)}, bf16[1,784,128]{2,1,0:T(8,128)(2,1)S(1)}, u32[]{:S(2)}, u32[]{:S(2)}) %collective-permute-start.47) | collective-permute-done | bytes 200736 | tf_op jit(solution)/shard_map/ppermute | solution.py:100
  371.9 3.7 fusion.19
  (243 shorter events, 31.5 us)
Async XLA Ops:
  7.2 13.6 %copy-start = (f32[4,32]{1,0:T(4,128)S(1)}, f32[4,32]{1,0:T(4,128)}, u32[]{:S(2)}) copy-start(f32[4,32]{1,0:T(4,128)} %param.24) | copy-start | bytes 1540
  7.2 140.3 %all-gather.3.cloned.1.call-start = ((), (), s32[]{:S(2)}) async-start(), calls=%async_computation.2 | async-start | bytes 19464192 | tf_op jit(solution)/shard_map/all_gather | solution.py:870
  10.4 27.0 %copy-start.28 = (bf16[256,128]{1,0:T(8,128)(2,1)S(1)}, bf16[256,128]{1,0:T(8,128)(2,1)}, u32[]{:S(2)}) copy-start(bf16[256,128]{1,0:T(8,128)(2,1)} %param.23) | copy-start | bytes 196612
  10.5 361.4 %reduce-scatter.2.cloned.1.call-start = ((), (), s32[]{:S(2)}) async-start(), calls=%async_computation.1 | async-start | bytes 19464192 | tf_op jit(solution)/shard_map/reduce_scatter | solution.py:902
  11.4 30.1 %collective-permute-start = (bf16[256,1024]{1,0:T(8,128)(2,1)S(1)}, bf16[256,1024]{1,0:T(8,128)(2,1)S(1)}, u32[]{:S(2)}, u32[]{:S(2)}) collective-permute-start(bf16[256,1024]{1,0:T(8,128)(2,1)S(1)} %copy-done.7), channel_id=1, source_target_pairs={{0,1},{1,0},{2,3},{3,2},{4,5},{5,4},{6,7},{7,6},{8,9},{9,8},{10,11... | collective-permute-start | bytes 1572872 | tf_op jit(solution)/shard_map/ppermute | solution.py:66
  11.9 25.6 %collective-permute-start.1 = (bf16[256,1024]{1,0:T(8,128)(2,1)S(1)}, bf16[256,1024]{1,0:T(8,128)(2,1)S(1)}, u32[]{:S(2)}, u32[]{:S(2)}) collective-permute-start(bf16[256,1024]{1,0:T(8,128)(2,1)S(1)} %copy-done.7), channel_id=1, source_target_pairs={{0,2},{1,3},{2,0},{3,1},{4,6},{5,7},{6,4},{7,5},{8,10},{9,11},{10,... | collective-permute-start | bytes 1572872 | tf_op jit(solution)/shard_map/ppermute | solution.py:66
  14.5 27.0 %collective-permute-start.3 = (bf16[1,80,768]{2,1,0:T(8,128)(2,1)S(1)}, bf16[1,80,768]{2,1,0:T(8,128)(2,1)S(1)}, u32[]{:S(2)}, u32[]{:S(2)}) collective-permute-start(bf16[1,80,768]{2,1,0:T(8,128)(2,1)S(1)} %slice_bitcast_fusion), channel_id=1, source_target_pairs={{0,8},{4,12},{8,0},{12,4},{16,24},{20,28},{24,16},{28,20},{1,9},{5... | collective-permute-start | bytes 368648 | tf_op jit(solution)/shard_map/ppermute | solution.py:95
  15.4 6.3 %collective-permute-start.11 = (bf16[1,64,768]{2,1,0:T(8,128)(2,1)S(1)}, bf16[1,64,768]{2,1,0:T(8,128)(2,1)S(1)}, u32[]{:S(2)}, u32[]{:S(2)}) collective-permute-start(bf16[1,64,768]{2,1,0:T(8,128)(2,1)S(1)} %maximum_bitcast_fusion.1), channel_id=1, source_target_pairs={{0,16},{4,20},{8,24},{12,28},{16,0},{20,4},{24,8},{28,12},{1,17},{... | collective-permute-start | bytes 294920 | tf_op jit(solution)/shard_map/ppermute | solution.py:95
  21.7 35.0 %copy-start.13 = (bf16[256,1024]{1,0:T(8,128)(2,1)S(1)}, bf16[256,1024]{1,0:T(8,128)(2,1)}, u32[]{:S(2)}) copy-start(bf16[256,1024]{1,0:T(8,128)(2,1)} %refs_4_.3) | copy-start | bytes 1572868
  37.4 17.1 %copy-start.35 = (bf16[256,1024]{1,0:T(8,128)(2,1)}, bf16[256,1024]{1,0:T(8,128)(2,1)S(1)}, u32[]{:S(2)}) copy-start(bf16[256,1024]{1,0:T(8,128)(2,1)S(1)} %collective-permute-done.1.refs_2_) | copy-start | bytes 1572868
  37.4 6.6 %collective-permute-start.7 = (bf16[256,128]{1,0:T(8,128)(2,1)S(1)}, bf16[256,128]{1,0:T(8,128)(2,1)S(1)}, u32[]{:S(2)}, u32[]{:S(2)}) collective-permute-start(bf16[256,128]{1,0:T(8,128)(2,1)S(1)} %copy-done.28), channel_id=1, source_target_pairs={{0,3},{1,2},{2,1},{3,0},{4,7},{5,6},{6,5},{7,4},{8,11},{9,10},{10,... | collective-permute-start | bytes 196616 | tf_op jit(solution)/shard_map/ppermute | solution.py:66
  37.9 7.9 %collective-permute-start.6 = (bf16[256,128]{1,0:T(8,128)(2,1)S(1)}, bf16[256,128]{1,0:T(8,128)(2,1)S(1)}, u32[]{:S(2)}, u32[]{:S(2)}) collective-permute-start(bf16[256,128]{1,0:T(8,128)(2,1)S(1)} %copy-done.28), channel_id=1, source_target_pairs={{0,2},{1,3},{2,0},{3,1},{4,6},{5,7},{6,4},{7,5},{8,10},{9,11},{10,... | collective-permute-start | bytes 196616 | tf_op jit(solution)/shard_map/ppermute | solution.py:66
  41.4 5.9 %collective-permute-start.5 = (bf16[256,128]{1,0:T(8,128)(2,1)S(1)}, bf16[256,128]{1,0:T(8,128)(2,1)S(1)}, u32[]{:S(2)}, u32[]{:S(2)}) collective-permute-start(bf16[256,128]{1,0:T(8,128)(2,1)S(1)} %copy-done.28), channel_id=1, source_target_pairs={{0,1},{1,0},{2,3},{3,2},{4,5},{5,4},{6,7},{7,6},{8,9},{9,8},{10,11... | collective-permute-start | bytes 196616 | tf_op jit(solution)/shard_map/ppermute | solution.py:66
  41.5 17.7 %copy-start.34 = (bf16[256,1024]{1,0:T(8,128)(2,1)}, bf16[256,1024]{1,0:T(8,128)(2,1)S(1)}, u32[]{:S(2)}) copy-start(bf16[256,1024]{1,0:T(8,128)(2,1)S(1)} %collective-permute-done.refs_1_) | copy-start | bytes 1572868
  41.5 13.5 %collective-permute-start.2 = (bf16[256,1024]{1,0:T(8,128)(2,1)S(1)}, bf16[256,1024]{1,0:T(8,128)(2,1)S(1)}, u32[]{:S(2)}, u32[]{:S(2)}) collective-permute-start(bf16[256,1024]{1,0:T(8,128)(2,1)S(1)} %collective-permute-done.1.refs_2_), channel_id=1, source_target_pairs={{0,1},{1,0},{2,3},{3,2},{4,5},{5,4},{6,7},{7,6},{8,9},{9,8},{10,11... | collective-permute-start | bytes 1572872 | tf_op jit(solution)/shard_map/ppermute | solution.py:66
  43.5 11.0 %collective-permute-start.4 = (bf16[2,80,768]{2,1,0:T(8,128)(2,1)S(1)}, bf16[2,80,768]{2,1,0:T(8,128)(2,1)S(1)}, u32[]{:S(2)}, u32[]{:S(2)}) collective-permute-start(bf16[2,80,768]{2,1,0:T(8,128)(2,1)S(1)} %pad_maximum_fusion.5), channel_id=1, source_target_pairs={{0,16},{4,20},{8,24},{12,28},{16,0},{20,4},{24,8},{28,12},{1,17},{... | collective-permute-start | bytes 737288 | tf_op jit(solution)/shard_map/ppermute | solution.py:95
  44.0 10.4 %collective-permute-start.12 = (bf16[2,64,768]{2,1,0:T(8,128)(2,1)S(1)}, bf16[2,64,768]{2,1,0:T(8,128)(2,1)S(1)}, u32[]{:S(2)}, u32[]{:S(2)}) collective-permute-start(bf16[2,64,768]{2,1,0:T(8,128)(2,1)S(1)} %pad_maximum_fusion.6), channel_id=1, source_target_pairs={{0,8},{4,12},{8,0},{12,4},{16,24},{20,28},{24,16},{28,20},{1,9},{5... | collective-permute-start | bytes 589832 | tf_op jit(solution)/shard_map/ppermute | solution.py:95
  47.3 5.5 %collective-permute-start.8 = (bf16[1,4,128,128]{3,2,1,0:T(8,128)(2,1)S(1)}, bf16[1,4,128,128]{3,2,1,0:T(8,128)(2,1)S(1)}, u32[]{:S(2)}, u32[]{:S(2)}) collective-permute-start(bf16[1,4,128,128]{3,2,1,0:T(8,128)(2,1)S(1)} %get-tuple-element.103), channel_id=1, source_target_pairs={{0,8},{4,12},{8,0},{12,4},{16,24},{20,28},{24,16},{28,20},{1,9},{5... | collective-permute-start | bytes 393224 | tf_op jit(solution)/shard_map/ppermute | solution.py:95
  47.9 6.5 %collective-permute-start.9 = (bf16[1,4,128,128]{3,2,1,0:T(8,128)(2,1)S(1)}, bf16[1,4,128,128]{3,2,1,0:T(8,128)(2,1)S(1)}, u32[]{:S(2)}, u32[]{:S(2)}) collective-permute-start(bf16[1,4,128,128]{3,2,1,0:T(8,128)(2,1)S(1)} %get-tuple-element.104), channel_id=1, source_target_pairs={{0,16},{4,20},{8,24},{12,28},{16,0},{20,4},{24,8},{28,12},{1,17},{... | collective-permute-start | bytes 393224 | tf_op jit(solution)/shard_map/ppermute | solution.py:95
  55.0 4.3 %collective-permute-start.10 = (bf16[4,80,768]{2,1,0:T(8,128)(2,1)S(1)}, bf16[4,80,768]{2,1,0:T(8,128)(2,1)S(1)}, u32[]{:S(2)}, u32[]{:S(2)}) collective-permute-start(bf16[4,80,768]{2,1,0:T(8,128)(2,1)S(1)} %pad_maximum_fusion.3), channel_id=1, source_target_pairs={{0,4},{4,0},{8,12},{12,8},{16,20},{20,16},{24,28},{28,24},{1,5},{5... | collective-permute-start | bytes 1474568 | tf_op jit(solution)/shard_map/ppermute | solution.py:95
  55.0 4.2 %collective-permute-start.13 = (bf16[4,64,768]{2,1,0:T(8,128)(2,1)S(1)}, bf16[4,64,768]{2,1,0:T(8,128)(2,1)S(1)}, u32[]{:S(2)}, u32[]{:S(2)}) collective-permute-start(bf16[4,64,768]{2,1,0:T(8,128)(2,1)S(1)} %pad_maximum_fusion.4), channel_id=1, source_target_pairs={{0,4},{4,0},{8,12},{12,8},{16,20},{20,16},{24,28},{28,24},{1,5},{5... | collective-permute-start | bytes 1179656 | tf_op jit(solution)/shard_map/ppermute | solution.py:95
  56.6 29.6 %collective-permute-start.14 = (bf16[256,1024]{1,0:T(8,128)(2,1)S(1)}, bf16[256,1024]{1,0:T(8,128)(2,1)S(1)}, u32[]{:S(2)}, u32[]{:S(2)}) collective-permute-start(bf16[256,1024]{1,0:T(8,128)(2,1)S(1)} %copy-done.13), channel_id=1, source_target_pairs={{0,1},{1,0},{2,3},{3,2},{4,5},{5,4},{6,7},{7,6},{8,9},{9,8},{10,11... | collective-permute-start | bytes 1572872 | tf_op jit(solution)/shard_map/ppermute | solution.py:66
  57.7 28.5 %collective-permute-start.15 = (bf16[256,1024]{1,0:T(8,128)(2,1)S(1)}, bf16[256,1024]{1,0:T(8,128)(2,1)S(1)}, u32[]{:S(2)}, u32[]{:S(2)}) collective-permute-start(bf16[256,1024]{1,0:T(8,128)(2,1)S(1)} %copy-done.13), channel_id=1, source_target_pairs={{0,2},{1,3},{2,0},{3,1},{4,6},{5,7},{6,4},{7,5},{8,10},{9,11},{10,... | collective-permute-start | bytes 1572872 | tf_op jit(solution)/shard_map/ppermute | solution.py:66
  67.8 20.5 %collective-permute-start.20 = (bf16[2,4,128,128]{3,2,1,0:T(8,128)(2,1)S(1)}, bf16[2,4,128,128]{3,2,1,0:T(8,128)(2,1)S(1)}, u32[]{:S(2)}, u32[]{:S(2)}) collective-permute-start(bf16[2,4,128,128]{3,2,1,0:T(8,128)(2,1)S(1)} %constant_dynamic-update-slice_fusion.3), channel_id=1, source_target_pairs={{0,16},{4,20},{8,24},{12,28},{16,0},{20,4},{24,8},{28,12},{1,17},{... | collective-permute-start | bytes 786440 | tf_op jit(solution)/shard_map/ppermute | solution.py:95
  69.3 23.7 %collective-permute-start.22 = (bf16[2,4,128,128]{3,2,1,0:T(8,128)(2,1)S(1)}, bf16[2,4,128,128]{3,2,1,0:T(8,128)(2,1)S(1)}, u32[]{:S(2)}, u32[]{:S(2)}) collective-permute-start(bf16[2,4,128,128]{3,2,1,0:T(8,128)(2,1)S(1)} %constant_dynamic-update-slice_fusion.5), channel_id=1, source_target_pairs={{0,8},{4,12},{8,0},{12,4},{16,24},{20,28},{24,16},{28,20},{1,9},{5... | collective-permute-start | bytes 786440 | tf_op jit(solution)/shard_map/ppermute | solution.py:95
  86.3 19.1 %copy-start.38 = (bf16[256,1024]{1,0:T(8,128)(2,1)}, bf16[256,1024]{1,0:T(8,128)(2,1)S(1)}, u32[]{:S(2)}) copy-start(bf16[256,1024]{1,0:T(8,128)(2,1)S(1)} %collective-permute-done.15.refs_6_.refs_9_) | copy-start | bytes 1572868
  86.3 6.7 %collective-permute-start.17 = (bf16[256,256]{1,0:T(8,128)(2,1)}, bf16[256,256]{1,0:T(8,128)(2,1)S(1)}, u32[]{:S(2)}, u32[]{:S(2)}) collective-permute-start(bf16[256,256]{1,0:T(8,128)(2,1)} %get-tuple-element.117), channel_id=1, source_target_pairs={{0,1},{1,0},{2,3},{3,2},{4,5},{5,4},{6,7},{7,6},{8,9},{9,8},{10,11... | collective-permute-start | bytes 393224 | tf_op jit(solution)/shard_map/ppermute | solution.py:66
  88.0 17.3 %collective-permute-start.16 = (bf16[256,1024]{1,0:T(8,128)(2,1)S(1)}, bf16[256,1024]{1,0:T(8,128)(2,1)S(1)}, u32[]{:S(2)}, u32[]{:S(2)}) collective-permute-start(bf16[256,1024]{1,0:T(8,128)(2,1)S(1)} %collective-permute-done.15.refs_6_.refs_9_), channel_id=1, source_target_pairs={{0,1},{1,0},{2,3},{3,2},{4,5},{5,4},{6,7},{7,6},{8,9},{9,8},{10,11... | collective-permute-start | bytes 1572872 | tf_op jit(solution)/shard_map/ppermute | solution.py:66
  93.0 12.3 %collective-permute-start.21 = (bf16[4,4,128,128]{3,2,1,0:T(8,128)(2,1)S(1)}, bf16[4,4,128,128]{3,2,1,0:T(8,128)(2,1)S(1)}, u32[]{:S(2)}, u32[]{:S(2)}) collective-permute-start(bf16[4,4,128,128]{3,2,1,0:T(8,128)(2,1)S(1)} %pad_maximum_fusion.1), channel_id=1, source_target_pairs={{0,4},{4,0},{8,12},{12,8},{16,20},{20,16},{24,28},{28,24},{1,5},{5... | collective-permute-start | bytes 1572872 | tf_op jit(solution)/shard_map/ppermute | solution.py:95
  93.0 12.4 %collective-permute-start.23 = (bf16[4,4,128,128]{3,2,1,0:T(8,128)(2,1)S(1)}, bf16[4,4,128,128]{3,2,1,0:T(8,128)(2,1)S(1)}, u32[]{:S(2)}, u32[]{:S(2)}) collective-permute-start(bf16[4,4,128,128]{3,2,1,0:T(8,128)(2,1)S(1)} %pad_maximum_fusion.2), channel_id=1, source_target_pairs={{0,4},{4,0},{8,12},{12,8},{16,20},{20,16},{24,28},{28,24},{1,5},{5... | collective-permute-start | bytes 1572872 | tf_op jit(solution)/shard_map/ppermute | solution.py:95
  93.6 13.0 %collective-permute-start.18 = (bf16[256,256]{1,0:T(8,128)(2,1)}, bf16[256,256]{1,0:T(8,128)(2,1)S(1)}, u32[]{:S(2)}, u32[]{:S(2)}) collective-permute-start(bf16[256,256]{1,0:T(8,128)(2,1)} %get-tuple-element.119), channel_id=1, source_target_pairs={{0,2},{1,3},{2,0},{3,1},{4,6},{5,7},{6,4},{7,5},{8,10},{9,11},{10,... | collective-permute-start | bytes 393224 | tf_op jit(solution)/shard_map/ppermute | solution.py:66
  94.6 14.2 %collective-permute-start.19 = (bf16[256,256]{1,0:T(8,128)(2,1)}, bf16[256,256]{1,0:T(8,128)(2,1)S(1)}, u32[]{:S(2)}, u32[]{:S(2)}) collective-permute-start(bf16[256,256]{1,0:T(8,128)(2,1)} %get-tuple-element.121), channel_id=1, source_target_pairs={{0,3},{1,2},{2,1},{3,0},{4,7},{5,6},{6,5},{7,4},{8,11},{9,10},{10,... | collective-permute-start | bytes 393224 | tf_op jit(solution)/shard_map/ppermute | solution.py:66
  113.3 20.7 %collective-permute-start.24 = (bf16[256,1024]{1,0:T(8,128)(2,1)}, bf16[256,1024]{1,0:T(8,128)(2,1)S(1)}, u32[]{:S(2)}, u32[]{:S(2)}) collective-permute-start(bf16[256,1024]{1,0:T(8,128)(2,1)} %get-tuple-element.129.refs_0_.refs_3_), channel_id=1, source_target_pairs={{0,1},{1,0},{2,3},{3,2},{4,5},{5,4},{6,7},{7,6},{8,9},{9,8},{10,11... | collective-permute-start | bytes 1572872 | tf_op jit(solution)/shard_map/ppermute | solution.py:66
  114.0 22.0 %collective-permute-start.25 = (bf16[256,1024]{1,0:T(8,128)(2,1)}, bf16[256,1024]{1,0:T(8,128)(2,1)S(1)}, u32[]{:S(2)}, u32[]{:S(2)}) collective-permute-start(bf16[256,1024]{1,0:T(8,128)(2,1)} %get-tuple-element.129.refs_0_.refs_3_), channel_id=1, source_target_pairs={{0,2},{1,3},{2,0},{3,1},{4,6},{5,7},{6,4},{7,5},{8,10},{9,11},{10,... | collective-permute-start | bytes 1572872 | tf_op jit(solution)/shard_map/ppermute | solution.py:66
  134.0 13.5 %copy-start.41 = (bf16[256,1024]{1,0:T(8,128)(2,1)}, bf16[256,1024]{1,0:T(8,128)(2,1)S(1)}, u32[]{:S(2)}) copy-start(bf16[256,1024]{1,0:T(8,128)(2,1)S(1)} %collective-permute-done.24.refs_1_.refs_4_) | copy-start | bytes 1572868
  136.0 11.6 %collective-permute-start.26 = (bf16[256,1024]{1,0:T(8,128)(2,1)S(1)}, bf16[256,1024]{1,0:T(8,128)(2,1)S(1)}, u32[]{:S(2)}, u32[]{:S(2)}) collective-permute-start(bf16[256,1024]{1,0:T(8,128)(2,1)S(1)} %collective-permute-done.25.refs_2_.refs_5_), channel_id=1, source_target_pairs={{0,1},{1,0},{2,3},{3,2},{4,5},{5,4},{6,7},{7,6},{8,9},{9,8},{10,11... | collective-permute-start | bytes 1572872 | tf_op jit(solution)/shard_map/ppermute | solution.py:66
  200.1 13.4 %copy-start.44 = (bf16[256,1024]{1,0:T(8,128)(2,1)S(1)}, bf16[256,1024]{1,0:T(8,128)(2,1)}, u32[]{:S(2)}) copy-start(bf16[256,1024]{1,0:T(8,128)(2,1)} %get-tuple-element.148) | copy-start | bytes 1572868
  200.1 12.4 %collective-permute-start.27 = (bf16[256,1024]{1,0:T(8,128)(2,1)}, bf16[256,1024]{1,0:T(8,128)(2,1)S(1)}, u32[]{:S(2)}, u32[]{:S(2)}) collective-permute-start(bf16[256,1024]{1,0:T(8,128)(2,1)} %get-tuple-element.143), channel_id=1, source_target_pairs={{0,1},{1,0},{2,3},{3,2},{4,5},{5,4},{6,7},{7,6},{8,9},{9,8},{10,11... | collective-permute-start | bytes 1572872 | tf_op jit(solution)/shard_map/ppermute | solution.py:66
  212.7 27.5 %collective-permute-start.29 = (bf16[256,1024]{1,0:T(8,128)(2,1)S(1)}, bf16[256,1024]{1,0:T(8,128)(2,1)S(1)}, u32[]{:S(2)}, u32[]{:S(2)}) collective-permute-start(bf16[256,1024]{1,0:T(8,128)(2,1)S(1)} %add_convert_fusion.6), channel_id=1, source_target_pairs={{0,2},{1,3},{2,0},{3,1},{4,6},{5,7},{6,4},{7,5},{8,10},{9,11},{10,... | collective-permute-start | bytes 1572872 | tf_op jit(solution)/shard_map/ppermute | solution.py:66
  213.4 26.8 %collective-permute-start.28 = (bf16[256,1024]{1,0:T(8,128)(2,1)S(1)}, bf16[256,1024]{1,0:T(8,128)(2,1)S(1)}, u32[]{:S(2)}, u32[]{:S(2)}) collective-permute-start(bf16[256,1024]{1,0:T(8,128)(2,1)S(1)} %copy-done.44), channel_id=1, source_target_pairs={{0,1},{1,0},{2,3},{3,2},{4,5},{5,4},{6,7},{7,6},{8,9},{9,8},{10,11... | collective-permute-start | bytes 1572872 | tf_op jit(solution)/shard_map/ppermute | solution.py:66
  246.1 13.7 %copy-start.9 = (bf16[256,1024]{1,0:T(8,128)(2,1)S(1)}, bf16[256,1024]{1,0:T(8,128)(2,1)}, u32[]{:S(2)}) copy-start(bf16[256,1024]{1,0:T(8,128)(2,1)} %get-tuple-element.140) | copy-start | bytes 1572868
  246.1 13.7 %collective-permute-start.30 = (bf16[256,1024]{1,0:T(8,128)(2,1)S(1)}, bf16[256,1024]{1,0:T(8,128)(2,1)S(1)}, u32[]{:S(2)}, u32[]{:S(2)}) collective-permute-start(bf16[256,1024]{1,0:T(8,128)(2,1)S(1)} %copy-done.40), channel_id=1, source_target_pairs={{0,1},{1,0},{2,3},{3,2},{4,5},{5,4},{6,7},{7,6},{8,9},{9,8},{10,11... | collective-permute-start | bytes 1572872 | tf_op jit(solution)/shard_map/ppermute | solution.py:66
  246.9 14.3 %collective-permute-start.33 = (bf16[256,256]{1,0:T(8,128)(2,1)}, bf16[256,256]{1,0:T(8,128)(2,1)S(1)}, u32[]{:S(2)}, u32[]{:S(2)}) collective-permute-start(bf16[256,256]{1,0:T(8,128)(2,1)} %get-tuple-element.155), channel_id=1, source_target_pairs={{0,1},{1,0},{2,3},{3,2},{4,5},{5,4},{6,7},{7,6},{8,9},{9,8},{10,11... | collective-permute-start | bytes 393224 | tf_op jit(solution)/shard_map/ppermute | solution.py:66
  248.7 14.4 %collective-permute-start.34 = (bf16[256,256]{1,0:T(8,128)(2,1)}, bf16[256,256]{1,0:T(8,128)(2,1)S(1)}, u32[]{:S(2)}, u32[]{:S(2)}) collective-permute-start(bf16[256,256]{1,0:T(8,128)(2,1)} %get-tuple-element.156), channel_id=1, source_target_pairs={{0,2},{1,3},{2,0},{3,1},{4,6},{5,7},{6,4},{7,5},{8,10},{9,11},{10,... | collective-permute-start | bytes 393224 | tf_op jit(solution)/shard_map/ppermute | solution.py:66
  249.3 13.7 %collective-permute-start.35 = (bf16[256,256]{1,0:T(8,128)(2,1)}, bf16[256,256]{1,0:T(8,128)(2,1)S(1)}, u32[]{:S(2)}, u32[]{:S(2)}) collective-permute-start(bf16[256,256]{1,0:T(8,128)(2,1)} %get-tuple-element.157), channel_id=1, source_target_pairs={{0,3},{1,2},{2,1},{3,0},{4,7},{5,6},{6,5},{7,4},{8,11},{9,10},{10,... | collective-permute-start | bytes 393224 | tf_op jit(solution)/shard_map/ppermute | solution.py:66
  263.1 4.4 %collective-permute-start.36 = (bf16[4,1024,128]{2,1,0:T(8,128)(2,1)}, bf16[4,1024,128]{2,1,0:T(8,128)(2,1)S(1)}, u32[]{:S(2)}, u32[]{:S(2)}) collective-permute-start(bf16[4,1024,128]{2,1,0:T(8,128)(2,1)} %get-tuple-element.164), channel_id=1, source_target_pairs={{0,4},{4,0},{8,12},{12,8},{16,20},{20,16},{24,28},{28,24},{1,5},{5... | collective-permute-start | bytes 3145736 | tf_op jit(solution)/shard_map/ppermute | solution.py:100
  263.1 27.0 %collective-permute-start.32 = (bf16[256,1024]{1,0:T(8,128)(2,1)}, bf16[256,1024]{1,0:T(8,128)(2,1)}, u32[]{:S(2)}, u32[]{:S(2)}) collective-permute-start(bf16[256,1024]{1,0:T(8,128)(2,1)} %add_convert_fusion.5), channel_id=1, source_target_pairs={{0,2},{1,3},{2,0},{3,1},{4,6},{5,7},{6,4},{7,5},{8,10},{9,11},{10,... | collective-permute-start | bytes 1572872 | tf_op jit(solution)/shard_map/ppermute | solution.py:66
  266.4 23.8 %collective-permute-start.31 = (bf16[256,1024]{1,0:T(8,128)(2,1)}, bf16[256,1024]{1,0:T(8,128)(2,1)}, u32[]{:S(2)}, u32[]{:S(2)}) collective-permute-start(bf16[256,1024]{1,0:T(8,128)(2,1)} %get-tuple-element.151), channel_id=1, source_target_pairs={{0,1},{1,0},{2,3},{3,2},{4,5},{5,4},{6,7},{7,6},{8,9},{9,8},{10,11... | collective-permute-start | bytes 1572872 | tf_op jit(solution)/shard_map/ppermute | solution.py:66
  269.6 19.4 %collective-permute-start.37 = (bf16[2,1024,128]{2,1,0:T(8,128)(2,1)}, bf16[2,1024,128]{2,1,0:T(8,128)(2,1)}, u32[]{:S(2)}, u32[]{:S(2)}) collective-permute-start(bf16[2,1024,128]{2,1,0:T(8,128)(2,1)} %slice.171), channel_id=1, source_target_pairs={{0,8},{4,12},{8,0},{12,4},{16,24},{20,28},{24,16},{28,20},{1,9},{5... | collective-permute-start | bytes 1572872 | tf_op jit(solution)/shard_map/ppermute | solution.py:100
  270.7 18.2 %copy-start.5 = (bf16[4,1024,128]{2,1,0:T(8,128)(2,1)S(1)}, bf16[4,1024,128]{2,1,0:T(8,128)(2,1)}, u32[]{:S(2)}) copy-start(bf16[4,1024,128]{2,1,0:T(8,128)(2,1)} %copy-done.4) | copy-start | bytes 3145732
  290.2 16.5 %collective-permute-start.39 = (bf16[1,1024,128]{2,1,0:T(8,128)(2,1)S(1)}, bf16[1,1024,128]{2,1,0:T(8,128)(2,1)S(1)}, u32[]{:S(2)}, u32[]{:S(2)}) collective-permute-start(bf16[1,1024,128]{2,1,0:T(8,128)(2,1)S(1)} %slice.173), channel_id=1, source_target_pairs={{0,16},{4,20},{8,24},{12,28},{16,0},{20,4},{24,8},{28,12},{1,17},{... | collective-permute-start | bytes 786440 | tf_op jit(solution)/shard_map/ppermute | solution.py:100
  299.3 21.4 %collective-permute-start.38 = (bf16[256,1024]{1,0:T(8,128)(2,1)}, bf16[256,1024]{1,0:T(8,128)(2,1)S(1)}, u32[]{:S(2)}, u32[]{:S(2)}) collective-permute-start(bf16[256,1024]{1,0:T(8,128)(2,1)} %get-tuple-element.174), channel_id=1, source_target_pairs={{0,1},{1,0},{2,3},{3,2},{4,5},{5,4},{6,7},{7,6},{8,9},{9,8},{10,11... | collective-permute-start | bytes 1572872 | tf_op jit(solution)/shard_map/ppermute | solution.py:66
  303.2 10.5 %collective-permute-start.40 = (f32[8,1024]{1,0:T(8,128)}, f32[8,1024]{1,0:T(8,128)S(1)}, u32[]{:S(2)}, u32[]{:S(2)}) collective-permute-start(f32[8,1024]{1,0:T(8,128)} %get-tuple-element.177.refs_0_), channel_id=1, source_target_pairs={{0,1},{1,0},{2,3},{3,2},{4,5},{5,4},{6,7},{7,6},{8,9},{9,8},{10,11... | collective-permute-start | bytes 98312 | tf_op jit(solution)/shard_map/ppermute | solution.py:66
  303.2 10.9 %collective-permute-start.41 = (f32[8,1024]{1,0:T(8,128)}, f32[8,1024]{1,0:T(8,128)S(1)}, u32[]{:S(2)}, u32[]{:S(2)}) collective-permute-start(f32[8,1024]{1,0:T(8,128)} %get-tuple-element.177.refs_0_), channel_id=1, source_target_pairs={{0,2},{1,3},{2,0},{3,1},{4,6},{5,7},{6,4},{7,5},{8,10},{9,11},{10,... | collective-permute-start | bytes 98312 | tf_op jit(solution)/shard_map/ppermute | solution.py:66
  303.8 10.3 %collective-permute-start.42 = (f32[8,1024]{1,0:T(8,128)}, f32[8,1024]{1,0:T(8,128)S(1)}, u32[]{:S(2)}, u32[]{:S(2)}) collective-permute-start(f32[8,1024]{1,0:T(8,128)} %get-tuple-element.177.refs_0_), channel_id=1, source_target_pairs={{0,3},{1,2},{2,1},{3,0},{4,7},{5,6},{6,5},{7,4},{8,11},{9,10},{10,... | collective-permute-start | bytes 98312 | tf_op jit(solution)/shard_map/ppermute | solution.py:66
  306.8 13.9 %copy-start.10 = (bf16[256,1024]{1,0:T(8,128)(2,1)S(1)}, bf16[256,1024]{1,0:T(8,128)(2,1)}, u32[]{:S(2)}) copy-start(bf16[256,1024]{1,0:T(8,128)(2,1)} %get-tuple-element.173) | copy-start | bytes 1572868
  320.9 3.0 collective-permute-start.45
  321.0 30.8 %collective-permute-start.44 = (bf16[256,1024]{1,0:T(8,128)(2,1)S(1)}, bf16[256,1024]{1,0:T(8,128)(2,1)S(1)}, u32[]{:S(2)}, u32[]{:S(2)}) collective-permute-start(bf16[256,1024]{1,0:T(8,128)(2,1)S(1)} %add_convert_fusion.2), channel_id=1, source_target_pairs={{0,2},{1,3},{2,0},{3,1},{4,6},{5,7},{6,4},{7,5},{8,10},{9,11},{10,... | collective-permute-start | bytes 1572872 | tf_op jit(solution)/shard_map/ppermute | solution.py:66
  323.2 24.2 %collective-permute-start.43 = (bf16[256,1024]{1,0:T(8,128)(2,1)}, bf16[256,1024]{1,0:T(8,128)(2,1)S(1)}, u32[]{:S(2)}, u32[]{:S(2)}) collective-permute-start(bf16[256,1024]{1,0:T(8,128)(2,1)} %get-tuple-element.180), channel_id=1, source_target_pairs={{0,1},{1,0},{2,3},{3,2},{4,5},{5,4},{6,7},{7,6},{8,9},{9,8},{10,11... | collective-permute-start | bytes 1572872 | tf_op jit(solution)/shard_map/ppermute | solution.py:66
  325.4 30.9 %collective-permute-start.46 = (bf16[2,784,128]{2,1,0:T(8,128)(2,1)S(1)}, bf16[2,784,128]{2,1,0:T(8,128)(2,1)S(1)}, u32[]{:S(2)}, u32[]{:S(2)}) collective-permute-start(bf16[2,784,128]{2,1,0:T(8,128)(2,1)S(1)} %slice.175), channel_id=1, source_target_pairs={{0,8},{4,12},{8,0},{12,4},{16,24},{20,28},{24,16},{28,20},{1,9},{5... | collective-permute-start | bytes 1204232 | tf_op jit(solution)/shard_map/ppermute | solution.py:100
  347.5 9.0 %collective-permute-start.50 = (bf16[256,128]{1,0:T(8,128)(2,1)S(1)}, bf16[256,128]{1,0:T(8,128)(2,1)S(1)}, u32[]{:S(2)}, u32[]{:S(2)}) collective-permute-start(bf16[256,128]{1,0:T(8,128)(2,1)S(1)} %get-tuple-element.196), channel_id=1, source_target_pairs={{0,3},{1,2},{2,1},{3,0},{4,7},{5,6},{6,5},{7,4},{8,11},{9,10},{10,... | collective-permute-start | bytes 196616 | tf_op jit(solution)/shard_map/ppermute | solution.py:66
  348.2 8.3 %collective-permute-start.49 = (bf16[256,128]{1,0:T(8,128)(2,1)S(1)}, bf16[256,128]{1,0:T(8,128)(2,1)S(1)}, u32[]{:S(2)}, u32[]{:S(2)}) collective-permute-start(bf16[256,128]{1,0:T(8,128)(2,1)S(1)} %get-tuple-element.197), channel_id=1, source_target_pairs={{0,2},{1,3},{2,0},{3,1},{4,6},{5,7},{6,4},{7,5},{8,10},{9,11},{10,... | collective-permute-start | bytes 196616 | tf_op jit(solution)/shard_map/ppermute | solution.py:66
  351.8 4.7 %collective-permute-start.48 = (bf16[256,128]{1,0:T(8,128)(2,1)S(1)}, bf16[256,128]{1,0:T(8,128)(2,1)S(1)}, u32[]{:S(2)}, u32[]{:S(2)}) collective-permute-start(bf16[256,128]{1,0:T(8,128)(2,1)S(1)} %get-tuple-element.195), channel_id=1, source_target_pairs={{0,1},{1,0},{2,3},{3,2},{4,5},{5,4},{6,7},{7,6},{8,9},{9,8},{10,11... | collective-permute-start | bytes 196616 | tf_op jit(solution)/shard_map/ppermute | solution.py:66
  356.4 11.2 %collective-permute-start.47 = (bf16[1,784,128]{2,1,0:T(8,128)(2,1)S(1)}, bf16[1,784,128]{2,1,0:T(8,128)(2,1)S(1)}, u32[]{:S(2)}, u32[]{:S(2)}) collective-permute-start(bf16[1,784,128]{2,1,0:T(8,128)(2,1)S(1)} %slice.144), channel_id=1, source_target_pairs={{0,16},{4,20},{8,24},{12,28},{16,0},{20,4},{24,8},{28,12},{1,17},{... | collective-permute-start | bytes 602120 | tf_op jit(solution)/shard_map/ppermute | solution.py:100
  (40 other events, 197.8 us)
Sparse Core Ops, SparseCore 0:
  10.6 102.8 all-gather.2
  240.4 131.3 reduce-scatter.1

commit v2 on v1

--- a/solution.py
+++ b/solution.py
@@ -177,9 +177,8 @@
     )(index, place, *toks, *pack, small)
 
 
-def extents(total):
-    blocks = total // BLOCK
-    return [(i, min(BLOCK * (i + 2), total)) for i in range(blocks)]
+def extent_of(i, total):
+    return min(BLOCK * (i + 2), total)
 
 
 def fwd_body(total, chunks, starts_ref, place_ref, q_ref, k_ref, vt_ref, line_ref, p_ref, ot_ref, *refs):
@@ -216,26 +215,33 @@
         rolled = pltpu.roll(spread, BLOCK + 1, 1, stride=1, stride_axis=0)
         strip_ref[BLOCK * beta : BLOCK * (beta + 1), :] = rolled[:, :BLOCK]
 
-    lanes = lax.broadcasted_iota(jnp.int32, (BLOCK, width), 1)
+    lanes = lax.broadcasted_iota(jnp.int32, (2 * BLOCK, width), 1)
     own = (lanes >= head * dim) & (lanes < (head + 1) * dim)
     at_head = pl.ds(pl.multiple_of(head * dim, dim), dim)
-    for i, extent in extents(total):
-        q_rows = q_ref[BLOCK * i : BLOCK * (i + 1), :]
+    for pair in range(0, blocks, 2):
+        both = slice(BLOCK * pair, BLOCK * (pair + 2))
+        reach = extent_of(pair + 1, total)
+        q_rows = q_ref[both, :]
         q_own = jnp.where(own, q_rows, jnp.zeros_like(q_rows))
-        base = BLOCK * (blocks - 1 - i)
-        scores = dot_nt(k_ref[0:extent, :], q_own) + strip_ref[base : base + extent, :]
-        parts = [scores[BLOCK * j : BLOCK * (j + 1)] for j in range(extent // BLOCK)]
-        for j in (i, i + 1):
-            if j < blocks:
-                parts[j] = parts[j] + mask_ref[2 * i + j - i]
-        top = functools.reduce(jnp.maximum, parts)
-        top = jnp.max(top, axis=0, keepdims=True)
-        parts = [jnp.exp(part - top) for part in parts]
-        total_sum = jnp.sum(functools.reduce(jnp.add, parts), axis=0, keepdims=True)
-        inverse = 1.0 / total_sum
-        chances = jnp.concatenate([(part * inverse).astype(BF) for part in parts], 0)
-        p_ref[0, 0:extent, BLOCK * i : BLOCK * (i + 1)] = chances
-        ot_ref[at_head, BLOCK * i : BLOCK * (i + 1)] = dot_nn(vt_ref[at_head, 0:extent], chances)
+        raw = dot_nt(k_ref[0:reach, :], q_own)
+        for i in (pair, pair + 1):
+            extent = extent_of(i, total)
+            cols = slice(BLOCK * i, BLOCK * (i + 1))
+            base = BLOCK * (blocks - 1 - i)
+            scores = raw[0:extent, BLOCK * (i - pair) : BLOCK * (i - pair + 1)] + strip_ref[base : base + extent, :]
+            parts = [scores[BLOCK * j : BLOCK * (j + 1)] for j in range(extent // BLOCK)]
+            for j in (i, i + 1):
+                if j < blocks:
+                    parts[j] = parts[j] + mask_ref[2 * i + j - i]
+            top = functools.reduce(jnp.maximum, parts)
+            top = jnp.max(top, axis=0, keepdims=True)
+            parts = [jnp.exp(part - top) for part in parts]
+            total_sum = jnp.sum(functools.reduce(jnp.add, parts), axis=0, keepdims=True)
+            inverse = 1.0 / total_sum
+            p_ref[0, 0:extent, cols] = jnp.concatenate([(part * inverse).astype(BF) for part in parts], 0)
+            if extent < total:
+                p_ref[0, extent : extent + BLOCK, cols] = jnp.zeros((BLOCK, BLOCK), BF)
+        ot_ref[at_head, both] = dot_nn(vt_ref[at_head, 0:reach], p_ref[0, 0:reach, both])
 
     @pl.when(head == heads - 1)
     def _():
@@ -318,6 +324,7 @@
             at = pl.ds(pl.multiple_of(place_ref[c] * rows, rows), rows)
             do_ref[at, :] = grads[c][...]
         dot_ref[...] = jnp.transpose(do_ref[...].astype(F32))
+        ds_ref[...] = jnp.zeros_like(ds_ref)
         dka_ref[...] = jnp.zeros_like(dka_ref)
         dva_ref[...] = jnp.zeros_like(dva_ref)
 
@@ -328,27 +335,32 @@
     q_own = jnp.where(own, q_ref[...], jnp.zeros_like(q_ref))
     do_own = jnp.where(own, do_ref[...], jnp.zeros_like(do_ref))
     written = 0
-    for i, extent in reversed(extents(total)):
-        cols = slice(BLOCK * i, BLOCK * (i + 1))
-        chance_grad = dot_nt(v_ref[0:extent, :], do_own[cols, :])
-        chances = p_ref[0, 0:extent, cols].astype(F32)
-        score_grad = (chances * (chance_grad - inner[:, cols])).astype(BF)
-        ds_ref[0:extent, cols] = score_grad
-        dqt_ref[at_head, cols] = dot_nn(kt_ref[at_head, 0:extent], score_grad)
-        base = BLOCK * (blocks - 1 - i)
-        wide = score_grad.astype(F32)
-        if i == blocks - 1:
-            acc_ref[0:extent, :] = wide
-            written = extent
-        else:
-            old = written - base
-            acc_ref[base:written, :] += wide[:old]
-            if base + extent > written:
-                acc_ref[written : base + extent, :] = wide[old:]
-                written = base + extent
-    for j in range(blocks):
-        first = max(0, BLOCK * (j - 1))
-        keys = slice(BLOCK * j, BLOCK * (j + 1))
+    for pair in range(blocks - 2, -1, -2):
+        both = slice(BLOCK * pair, BLOCK * (pair + 2))
+        reach = extent_of(pair + 1, total)
+        pair_grad = dot_nt(v_ref[0:reach, :], do_own[both, :])
+        for i in (pair + 1, pair):
+            extent = extent_of(i, total)
+            cols = slice(BLOCK * i, BLOCK * (i + 1))
+            chance_grad = pair_grad[0:extent, BLOCK * (i - pair) : BLOCK * (i - pair + 1)]
+            chances = p_ref[0, 0:extent, cols].astype(F32)
+            score_grad = (chances * (chance_grad - inner[:, cols])).astype(BF)
+            ds_ref[0:extent, cols] = score_grad
+            base = BLOCK * (blocks - 1 - i)
+            wide = score_grad.astype(F32)
+            if i == blocks - 1:
+                acc_ref[0:extent, :] = wide
+                written = extent
+            else:
+                old = written - base
+                acc_ref[base:written, :] += wide[:old]
+                if base + extent > written:
+                    acc_ref[written : base + extent, :] = wide[old:]
+                    written = base + extent
+        dqt_ref[at_head, both] = dot_nn(kt_ref[at_head, 0:reach], ds_ref[0:reach, both])
+    for pair in range(0, blocks, 2):
+        first = max(0, BLOCK * (pair - 1))
+        keys = slice(BLOCK * pair, BLOCK * (pair + 2))
         dka_ref[keys, :] += dot_nn(ds_ref[keys, first:], q_own[first:, :])
         dva_ref[keys, :] += dot_nn(p_ref[0, keys, first:], do_own[first:, :])
     for beta in range(blocks + 1):

time: 386 us -> 383 us (level)
  transfers between devices with their start and end apart: 53 -> 53, of which waited for: 22 -> 23; matrix products, arithmetic and copies ran while one was open for 6% -> 6% of each run, Pallas kernels for 26% -> 26%
where the time goes in v2:
time: 383 us; the launch traced here: 380 us
  Pallas kernels  149 us (39%)
  waiting for transfers between devices  121 us (32%)
  starting transfers between devices  58 us (15%)
  local copies, waits for them, and re-layouts  19.5 us (5%)
  other arithmetic  17 us (4%)
  between operations  14.9 us (4%)
    ppermute x33, waiting for transfers between devices, z_swap(): return lax.ppermute(x, 'tensor', [(i, i ^ mask) for i in range(size)])  100 us
    ppermute x33, starting transfers between devices, z_swap(): return lax.ppermute(x, 'tensor', [(i, i ^ mask) for i in range(size)])  45.8 us
    pallas_call x1, Pallas kernels, units_call(): pl.pallas_call(functools.partial(units_body, chunks, unit), grid=(ff // B...  32 us
    pallas_call x2, Pallas kernels, product_call(): pl.pallas_call(functools.partial(product_body, len(xs), chunks, bool(extr...  30.2 us
    pallas_call x1, Pallas kernels, wgrad_call(): pl.pallas_call(functools.partial(wgrad_body, count, chunks), grid=(ff //...  25 us
    ppermute x6, waiting for transfers between devices, dp_fold(): other = lax.ppermute(send, 'dp', [(i, i ^ bit) for i in range(8)])  15.2 us
    pallas_call x1, Pallas kernels, attn_bwd(): pl.pallas_call(functools.partial(bwd_body, total, chunks), grid=(heads,),...  14 us
    pallas_call x1, Pallas kernels, attn_fwd(): pl.pallas_call(functools.partial(fwd_body, total, chunks), grid=(heads,),...  13.7 us
  transfers between devices with their start and end apart: 53, of which 23 were waited for; matrix products, arithmetic and copies ran while one was open for 6% of the time, Pallas kernels for 26%

profile of v2, /device:TPU:14, one launch (start us, length us, event | category | flops | bytes accessed | tf_op | source)
XLA Modules:
  0.0 379.7 jit_solution(11376837066277336277)
XLA Ops:
  7.2 3.1 pad_maximum_fusion
  10.5 0.9 copy-done.7
  11.9 2.6 collective-permute-start.1
  16.0 2.3 reduce-window.6
  19.1 1.6 fusion.2.refs_8_
  21.7 15.8 %collective-permute-done.1.refs_2_ = bf16[256,1024]{1,0:T(8,128)(2,1)S(1)} collective-permute-done((bf16[256,1024]{1,0:T(8,128)(2,1)S(1)}, bf16[256,1024]{1,0:T(8,128)(2,1)S(1)}, u32[]{:S(2)}, u32[]{:S(2)}) %collective-permute-start.1) | collective-permute-done | bytes 524320 | tf_op jit(solution)/shard_map/ppermute | solution.py:66
  37.9 3.5 collective-permute-start.6
  41.5 2.0 collective-permute-start.2
  44.6 1.2 collective-permute-done.6
  45.7 1.5 collective-permute-done.5
  48.5 4.3 %collective-permute-done.8 = bf16[1,4,128,128]{3,2,1,0:T(8,128)(2,1)S(1)} collective-permute-done((bf16[1,4,128,128]{3,2,1,0:T(8,128)(2,1)S(1)}, bf16[1,4,128,128]{3,2,1,0:T(8,128)(2,1)S(1)}, u32[]{:S(2)}, u32[]{:S(2)}) %collective-permute-start.8) | collective-permute-done | bytes 131104 | tf_op jit(solution)/shard_map/ppermute | solution.py:95
  52.9 1.5 collective-permute-done.9
  56.6 1.1 collective-permute-start.14
  57.7 1.4 collective-permute-start.15
  60.2 1.0 copy-done.19
  61.2 6.6 %norm_qkv.1 = (bf16[1024,1024]{1,0:T(8,128)(2,1)}, bf16[1024,256]{1,0:T(8,128)(2,1)}, bf16[1024,256]{1,0:T(8,128)(2,1)}, bf16[1024,256]{1,0:T(8,128)(2,1)}, bf16...) custom-call(s32[16]{0:T(128)} %pad_add_fusion.index_ref, ...), custom_call_target="tpu_custom_call" | custom-call | flops 1610612736 | bytes 8388608 | tf_op jit(solution)/shard_map/norm_qkv/pallas_call | solution.py:168
  67.8 1.5 collective-permute-start.20
  69.9 13.7 %attn_forward.1 = (bf16[4,1024,1024]{2,1,0:T(8,128)(2,1)}, f32[256,1024]{1,0:T(8,128)}, bf16[256,256]{1,0:T(8,128)(2,1)}, bf16[256,256]{1,0:T(8,128)(2,1)}, bf16...) custom-call(s32[1,2]{1,0:T(1,128)} %starts_ref.1, s32[4]{0:T(128)} %iota_xor_fusion.place_ref, ...), custom_call_target="tpu_custom_call" | custom-call | flops 4294967296 | bytes 10485760 | tf_op jit(solution)/shard_map/attn_forward/pallas_call | solution.py:261
  83.6 1.7 collective-permute-start.17
  85.8 4.6 %collective-permute-done.17.refs_1_ = bf16[256,256]{1,0:T(8,128)(2,1)S(1)} collective-permute-done((bf16[256,256]{1,0:T(8,128)(2,1)}, bf16[256,256]{1,0:T(8,128)(2,1)S(1)}, u32[]{:S(2)}, u32[]{:S(2)}) %collective-permute-start.17) | collective-permute-done | bytes 131104 | tf_op jit(solution)/shard_map/ppermute | solution.py:66
  91.0 1.3 collective-permute-start.18
  92.3 1.8 collective-permute-start.19
  94.1 8.5 %collective-permute-done.16.refs_7_.refs_10_ = bf16[256,1024]{1,0:T(8,128)(2,1)S(1)} collective-permute-done((bf16[256,1024]{1,0:T(8,128)(2,1)S(1)}, bf16[256,1024]{1,0:T(8,128)(2,1)S(1)}, u32[]{:S(2)}, u32[]{:S(2)}) %collective-permute-start.16) | collective-permute-done | bytes 524320 | tf_op jit(solution)/shard_map/ppermute | solution.py:66
  102.9 1.1 collective-permute-done.18.refs_2_
  104.0 2.2 collective-permute-done.19.refs_3_
  106.8 3.8 %out_projection_norm.1 = (f32[256,1024]{1,0:T(8,128)}, bf16[256,1024]{1,0:T(8,128)(2,1)}) custom-call(s32[16]{0:T(128)} %pad_add_fusion.index_ref, bf16[256,256]{1,0:T(8,128)(2,1)} %get-tuple-element.115.refs_0_, bf16[256,256]{1,0:T(8,128)(2,1)} %copy-done.22, bf16[256,256]{1,0:T(8,128)(2,1)} %copy-done.23, bf16[256,256]{1,0:T(8,128)(2,1)} %copy-done.24, ...), custom_call_target="tpu_custom_call" | custom-call | flops 536870912 | bytes 4194304 | tf_op jit(solution)/shard_map/out_projection_norm/pallas_call | solution.py:427
  112.1 19.3 %collective-permute-done.24.refs_1_.refs_4_ = bf16[256,1024]{1,0:T(8,128)(2,1)S(1)} collective-permute-done((bf16[256,1024]{1,0:T(8,128)(2,1)}, bf16[256,1024]{1,0:T(8,128)(2,1)S(1)}, u32[]{:S(2)}, u32[]{:S(2)}) %collective-permute-start.24) | collective-permute-done | bytes 524320 | tf_op jit(solution)/shard_map/ppermute | solution.py:66
  131.4 1.9 collective-permute-done.25.refs_2_.refs_5_
  133.3 2.3 collective-permute-start.26
  135.7 9.2 %collective-permute-done.26.refs_3_.refs_6_ = bf16[256,1024]{1,0:T(8,128)(2,1)S(1)} collective-permute-done((bf16[256,1024]{1,0:T(8,128)(2,1)S(1)}, bf16[256,1024]{1,0:T(8,128)(2,1)S(1)}, u32[]{:S(2)}, u32[]{:S(2)}) %collective-permute-start.26) | collective-permute-done | bytes 524320 | tf_op jit(solution)/shard_map/ppermute | solution.py:66
  145.7 32.0 %expert_units.1 = (bf16[1024,2816]{1,0:T(8,128)(2,1)}, bf16[1024,2816]{1,0:T(8,128)(2,1)}, bf16[1024,2816]{1,0:T(8,128)(2,1)}, f32[1024,128]{1,0:T(8,128)}, f32[8,1024]{1,0:T(8,128)}) custom-call(s32[4]{0:T(128)} %iota_xor_fusion.place_ref, bf16[256,1024]{1,0:T(8,128)(2,1)} %get-tuple-element.129.refs_0_.refs_3_, bf16[256,1024]{1,0:T(8,128)(2,1)} %copy-done.41, ...), custom_call_target="tpu_custom_call" | custom-call | flops 17716740096 | bytes 29884416 | tf_op jit(solution)/shard_map/expert_units/pallas_call | solution.py:530
  177.7 19.7 %normed_two_grads.1 = (bf16[256,1024]{1,0:T(8,128)(2,1)}, bf16[256,1024]{1,0:T(8,128)(2,1)}, bf16[256,1024]{1,0:T(8,128)(2,1)}, bf16[256,1024]{1,0:T(8,128)(2,1)}) custom-call(bf16[1024,2816]{1,0:T(8,128)(2,1)} %get-tuple-element.133.refs_0_.refs_1_, bf16[1024,2816]{1,0:T(8,128)(2,1)} %get-tuple-element.134.refs_1_.refs_2_, ...), custom_call_target="tpu_custom_call" | custom-call | flops 11811160064 | bytes 23068672 | tf_op jit(solution)/shard_map/normed_two_grads/pallas_call | solution.py:580
  197.4 2.1 collective-permute-start.27
  199.5 10.5 %expert_out.1 = (bf16[256,1024]{1,0:T(8,128)(2,1)}, bf16[256,1024]{1,0:T(8,128)(2,1)}, bf16[256,1024]{1,0:T(8,128)(2,1)}, bf16[256,1024]{1,0:T(8,128)(2,1)}) custom-call(bf16[1024,2816]{1,0:T(8,128)(2,1)} %get-tuple-element.145.refs_0_, bf16[8,3,2816,128]{3,2,1,0:T(8,128)(2,1)} %bitcast.81), custom_call_target="tpu_custom_call" | custom-call | flops 5905580032 | bytes 11534336 | tf_op jit(solution)/shard_map/expert_out/pallas_call | solution.py:580
  210.8 1.8 collective-permute-start.28
  212.6 25.0 %expert_weight_grads.1 = bf16[8,3,2816,128]{3,2,1,0:T(8,128)(2,1)} custom-call(bf16[1024,2816]{1,0:T(8,128)(2,1)} %get-tuple-element.145.refs_0_, bf16[1024,2816]{1,0:T(8,128)(2,1)} %get-tuple-element.133.refs_0_.refs_1_, bf16[1024,2816]{1,0:T(8,128)(2,1)} %get-tuple-element.134.refs_1_.refs_2_, bf16[256,1024]{1,0:T(8,128)(2,1)} %get-tuple-element.129.refs_0_.refs_3_, ...), custom_call_target="tpu_custom_call" | custom-call | flops 17716740096 | bytes 34603008 | tf_op jit(solution)/shard_map/expert_weight_grads/pallas_call | solution.py:620
  238.5 4.9 %resid_grad.1 = (f32[256,1024]{1,0:T(8,128)}, bf16[256,1024]{1,0:T(8,128)(2,1)}, f32[8,1024]{1,0:T(8,128)}, bf16[256,256]{1,0:T(8,128)(2,1)}, bf16[256,256]{1,0:...) custom-call(s32[16]{0:T(128)} %pad_add_fusion.index_ref, ...), custom_call_target="tpu_custom_call" | custom-call | flops 536870912 | bytes 4194304 | tf_op jit(solution)/shard_map/resid_grad/pallas_call | solution.py:661
  244.3 1.8 collective-permute-start.33
  246.7 1.0 collective-permute-start.35
  247.7 3.9 %w_output_grad.1 = (bf16[4,1024,128]{2,1,0:T(8,128)(2,1)}, bf16[4,1024,128]{2,1,0:T(8,128)(2,1)}) custom-call(s32[8]{0:T(128)} %fusion.17.slot_ref, bf16[256,256]{1,0:T(8,128)(2,1)} %get-tuple-element.115.refs_0_, bf16[256,256]{1,0:T(8,128)(2,1)} %copy-done.22, bf16[256,256]{1,0:T(8,128)(2,1)} %copy-done.23, bf16[256,256]{1,0:T(8,128)(2,1)} %copy-done.24, ...), custom_call_target="tpu_custom_call" | custom-call | flops 536870912 | bytes 4194304 | tf_op jit(solution)/shard_map/w_output_grad/pallas_call | solution.py:783
  251.7 5.5 %collective-permute-done.30 = bf16[256,1024]{1,0:T(8,128)(2,1)S(1)} collective-permute-done((bf16[256,1024]{1,0:T(8,128)(2,1)S(1)}, bf16[256,1024]{1,0:T(8,128)(2,1)S(1)}, u32[]{:S(2)}, u32[]{:S(2)}) %collective-permute-start.30) | collective-permute-done | bytes 524320 | tf_op jit(solution)/shard_map/ppermute | solution.py:66
  257.2 1.0 add_convert_fusion.5
  258.6 1.9 collective-permute-done.34.refs_2_
  260.6 3.2 collective-permute-start.32
  264.6 1.0 copy-done.4
  266.4 0.9 collective-permute-start.37
  267.3 14.0 %attn_backward.1 = (bf16[1024,256]{1,0:T(8,128)(2,1)}, bf16[1024,256]{1,0:T(8,128)(2,1)}, bf16[1024,256]{1,0:T(8,128)(2,1)}, f32[4,5,512]{2,1,0:T(8,128)}) custom-call(s32[4]{0:T(128)} %iota_xor_fusion.place_ref, bf16[256,256]{1,0:T(8,128)(2,1)} %get-tuple-element.154.refs_0_, bf16[256,256]{1,0:T(8,128)(2,1)} %copy-done.45, bf16[256,256]{1,0:T(8,128)(2,1)} %copy-done.46, ...), custom_call_target="tpu_custom_call" | custom-call | flops 171798691840 | bytes 10485760 | tf_op jit(solution)/shard_map/attn_backward/pallas_call | solution.py:382
  281.3 4.2 %collective-permute-done.37 = bf16[2,1024,128]{2,1,0:T(8,128)(2,1)} collective-permute-done((bf16[2,1024,128]{2,1,0:T(8,128)(2,1)}, bf16[2,1024,128]{2,1,0:T(8,128)(2,1)}, u32[]{:S(2)}, u32[]{:S(2)}) %collective-permute-start.37) | collective-permute-done | bytes 524320 | tf_op jit(solution)/shard_map/ppermute | solution.py:100
  285.5 1.2 add_convert_fusion.3
  287.6 3.3 collective-permute-start.39
  290.8 5.8 %projection_grads.1 = (bf16[256,1024]{1,0:T(8,128)(2,1)}, bf16[256,1024]{1,0:T(8,128)(2,1)}, bf16[256,1024]{1,0:T(8,128)(2,1)}, bf16[256,1024]{1,0:T(8,128)(2,1)}, f32[8,1024]{1,0:T(8,128)}) custom-call(s32[16]{0:T(128)} %pad_add_fusion.index_ref, s32[4]{0:T(128)} %iota_xor_fusion.place_ref, bf16[1024,256]{1,0:T(8,128)(2,1)} %get-tuple-element.166.dq_ref, ...), custom_call_target="tpu_custom_call" | custom-call | flops 1610612736 | bytes 8388608 | tf_op jit(solution)/shard_map/projection_grads/pallas_call | solution.py:720
  296.6 3.0 collective-permute-start.38
  301.2 3.0 collective-permute-start.42
  304.3 6.7 %collective-permute-done.40.refs_1_ = f32[8,1024]{1,0:T(8,128)S(1)} collective-permute-done((f32[8,1024]{1,0:T(8,128)}, f32[8,1024]{1,0:T(8,128)S(1)}, u32[]{:S(2)}, u32[]{:S(2)}) %collective-permute-start.40) | collective-permute-done | bytes 32800 | tf_op jit(solution)/shard_map/ppermute | solution.py:66
  312.8 5.3 %attn_weight_grads.1 = (bf16[4,784,128]{2,1,0:T(8,128)(2,1)}, bf16[4,784,128]{2,1,0:T(8,128)(2,1)}) custom-call(s32[8]{0:T(128)} %fusion.17.slot_ref, bf16[1024,1024]{1,0:T(8,128)(2,1)} %get-tuple-element.122.n1_ref, bf16[1024,256]{1,0:T(8,128)(2,1)} %get-tuple-element.166.dq_ref, bf16[1024,256]{1,0:T(8,128)(2,1)} %get-tuple-element.167.dk_ref, ...), custom_call_target="tpu_custom_call" | custom-call | flops 1610612736 | bytes 8388608 | tf_op jit(solution)/shard_map/attn_weight_grads/pallas_call | solution.py:756
  318.3 2.2 collective-permute-start.44
  321.2 1.4 add_convert_fusion.1
  322.7 1.3 collective-permute-start.46
  324.0 2.4 add_convert_fusion.4
  326.4 18.3 %collective-permute-done.43.refs_1_ = bf16[256,1024]{1,0:T(8,128)(2,1)S(1)} collective-permute-done((bf16[256,1024]{1,0:T(8,128)(2,1)}, bf16[256,1024]{1,0:T(8,128)(2,1)S(1)}, u32[]{:S(2)}, u32[]{:S(2)}) %collective-permute-start.43) | collective-permute-done | bytes 524320 | tf_op jit(solution)/shard_map/ppermute | solution.py:66
  345.5 3.6 collective-permute-start.49
  349.9 3.5 in_grad.1
  354.4 10.4 %collective-permute-done.47 = bf16[1,784,128]{2,1,0:T(8,128)(2,1)S(1)} collective-permute-done((bf16[1,784,128]{2,1,0:T(8,128)(2,1)S(1)}, bf16[1,784,128]{2,1,0:T(8,128)(2,1)S(1)}, u32[]{:S(2)}, u32[]{:S(2)}) %collective-permute-start.47) | collective-permute-done | bytes 200736 | tf_op jit(solution)/shard_map/ppermute | solution.py:100
  369.2 3.7 fusion.19
  (243 shorter events, 32.0 us)
Async XLA Ops:
  7.2 13.6 %copy-start = (f32[4,32]{1,0:T(4,128)S(1)}, f32[4,32]{1,0:T(4,128)}, u32[]{:S(2)}) copy-start(f32[4,32]{1,0:T(4,128)} %param.24) | copy-start | bytes 1540
  7.2 137.7 %all-gather.3.cloned.1.call-start = ((), (), s32[]{:S(2)}) async-start(), calls=%async_computation.2 | async-start | bytes 19464192 | tf_op jit(solution)/shard_map/all_gather | solution.py:882
  10.4 27.0 %copy-start.28 = (bf16[256,128]{1,0:T(8,128)(2,1)S(1)}, bf16[256,128]{1,0:T(8,128)(2,1)}, u32[]{:S(2)}) copy-start(bf16[256,128]{1,0:T(8,128)(2,1)} %param.23) | copy-start | bytes 196612
  10.5 358.7 %reduce-scatter.2.cloned.1.call-start = ((), (), s32[]{:S(2)}) async-start(), calls=%async_computation.1 | async-start | bytes 19464192 | tf_op jit(solution)/shard_map/reduce_scatter | solution.py:914
  11.4 30.1 %collective-permute-start = (bf16[256,1024]{1,0:T(8,128)(2,1)S(1)}, bf16[256,1024]{1,0:T(8,128)(2,1)S(1)}, u32[]{:S(2)}, u32[]{:S(2)}) collective-permute-start(bf16[256,1024]{1,0:T(8,128)(2,1)S(1)} %copy-done.7), channel_id=1, source_target_pairs={{0,1},{1,0},{2,3},{3,2},{4,5},{5,4},{6,7},{7,6},{8,9},{9,8},{10,11... | collective-permute-start | bytes 1572872 | tf_op jit(solution)/shard_map/ppermute | solution.py:66
  11.9 25.6 %collective-permute-start.1 = (bf16[256,1024]{1,0:T(8,128)(2,1)S(1)}, bf16[256,1024]{1,0:T(8,128)(2,1)S(1)}, u32[]{:S(2)}, u32[]{:S(2)}) collective-permute-start(bf16[256,1024]{1,0:T(8,128)(2,1)S(1)} %copy-done.7), channel_id=1, source_target_pairs={{0,2},{1,3},{2,0},{3,1},{4,6},{5,7},{6,4},{7,5},{8,10},{9,11},{10,... | collective-permute-start | bytes 1572872 | tf_op jit(solution)/shard_map/ppermute | solution.py:66
  14.5 27.0 %collective-permute-start.3 = (bf16[1,80,768]{2,1,0:T(8,128)(2,1)S(1)}, bf16[1,80,768]{2,1,0:T(8,128)(2,1)S(1)}, u32[]{:S(2)}, u32[]{:S(2)}) collective-permute-start(bf16[1,80,768]{2,1,0:T(8,128)(2,1)S(1)} %slice_bitcast_fusion), channel_id=1, source_target_pairs={{0,8},{4,12},{8,0},{12,4},{16,24},{20,28},{24,16},{28,20},{1,9},{5... | collective-permute-start | bytes 368648 | tf_op jit(solution)/shard_map/ppermute | solution.py:95
  15.4 6.3 %collective-permute-start.11 = (bf16[1,64,768]{2,1,0:T(8,128)(2,1)S(1)}, bf16[1,64,768]{2,1,0:T(8,128)(2,1)S(1)}, u32[]{:S(2)}, u32[]{:S(2)}) collective-permute-start(bf16[1,64,768]{2,1,0:T(8,128)(2,1)S(1)} %maximum_bitcast_fusion.1), channel_id=1, source_target_pairs={{0,16},{4,20},{8,24},{12,28},{16,0},{20,4},{24,8},{28,12},{1,17},{... | collective-permute-start | bytes 294920 | tf_op jit(solution)/shard_map/ppermute | solution.py:95
  21.7 35.0 %copy-start.13 = (bf16[256,1024]{1,0:T(8,128)(2,1)S(1)}, bf16[256,1024]{1,0:T(8,128)(2,1)}, u32[]{:S(2)}) copy-start(bf16[256,1024]{1,0:T(8,128)(2,1)} %refs_4_.3) | copy-start | bytes 1572868
  37.4 17.1 %copy-start.35 = (bf16[256,1024]{1,0:T(8,128)(2,1)}, bf16[256,1024]{1,0:T(8,128)(2,1)S(1)}, u32[]{:S(2)}) copy-start(bf16[256,1024]{1,0:T(8,128)(2,1)S(1)} %collective-permute-done.1.refs_2_) | copy-start | bytes 1572868
  37.4 6.6 %collective-permute-start.7 = (bf16[256,128]{1,0:T(8,128)(2,1)S(1)}, bf16[256,128]{1,0:T(8,128)(2,1)S(1)}, u32[]{:S(2)}, u32[]{:S(2)}) collective-permute-start(bf16[256,128]{1,0:T(8,128)(2,1)S(1)} %copy-done.28), channel_id=1, source_target_pairs={{0,3},{1,2},{2,1},{3,0},{4,7},{5,6},{6,5},{7,4},{8,11},{9,10},{10,... | collective-permute-start | bytes 196616 | tf_op jit(solution)/shard_map/ppermute | solution.py:66
  37.9 7.9 %collective-permute-start.6 = (bf16[256,128]{1,0:T(8,128)(2,1)S(1)}, bf16[256,128]{1,0:T(8,128)(2,1)S(1)}, u32[]{:S(2)}, u32[]{:S(2)}) collective-permute-start(bf16[256,128]{1,0:T(8,128)(2,1)S(1)} %copy-done.28), channel_id=1, source_target_pairs={{0,2},{1,3},{2,0},{3,1},{4,6},{5,7},{6,4},{7,5},{8,10},{9,11},{10,... | collective-permute-start | bytes 196616 | tf_op jit(solution)/shard_map/ppermute | solution.py:66
  41.4 5.9 %collective-permute-start.5 = (bf16[256,128]{1,0:T(8,128)(2,1)S(1)}, bf16[256,128]{1,0:T(8,128)(2,1)S(1)}, u32[]{:S(2)}, u32[]{:S(2)}) collective-permute-start(bf16[256,128]{1,0:T(8,128)(2,1)S(1)} %copy-done.28), channel_id=1, source_target_pairs={{0,1},{1,0},{2,3},{3,2},{4,5},{5,4},{6,7},{7,6},{8,9},{9,8},{10,11... | collective-permute-start | bytes 196616 | tf_op jit(solution)/shard_map/ppermute | solution.py:66
  41.5 17.7 %copy-start.34 = (bf16[256,1024]{1,0:T(8,128)(2,1)}, bf16[256,1024]{1,0:T(8,128)(2,1)S(1)}, u32[]{:S(2)}) copy-start(bf16[256,1024]{1,0:T(8,128)(2,1)S(1)} %collective-permute-done.refs_1_) | copy-start | bytes 1572868
  41.5 13.5 %collective-permute-start.2 = (bf16[256,1024]{1,0:T(8,128)(2,1)S(1)}, bf16[256,1024]{1,0:T(8,128)(2,1)S(1)}, u32[]{:S(2)}, u32[]{:S(2)}) collective-permute-start(bf16[256,1024]{1,0:T(8,128)(2,1)S(1)} %collective-permute-done.1.refs_2_), channel_id=1, source_target_pairs={{0,1},{1,0},{2,3},{3,2},{4,5},{5,4},{6,7},{7,6},{8,9},{9,8},{10,11... | collective-permute-start | bytes 1572872 | tf_op jit(solution)/shard_map/ppermute | solution.py:66
  43.5 11.0 %collective-permute-start.4 = (bf16[2,80,768]{2,1,0:T(8,128)(2,1)S(1)}, bf16[2,80,768]{2,1,0:T(8,128)(2,1)S(1)}, u32[]{:S(2)}, u32[]{:S(2)}) collective-permute-start(bf16[2,80,768]{2,1,0:T(8,128)(2,1)S(1)} %pad_maximum_fusion.5), channel_id=1, source_target_pairs={{0,16},{4,20},{8,24},{12,28},{16,0},{20,4},{24,8},{28,12},{1,17},{... | collective-permute-start | bytes 737288 | tf_op jit(solution)/shard_map/ppermute | solution.py:95
  44.0 10.4 %collective-permute-start.12 = (bf16[2,64,768]{2,1,0:T(8,128)(2,1)S(1)}, bf16[2,64,768]{2,1,0:T(8,128)(2,1)S(1)}, u32[]{:S(2)}, u32[]{:S(2)}) collective-permute-start(bf16[2,64,768]{2,1,0:T(8,128)(2,1)S(1)} %pad_maximum_fusion.6), channel_id=1, source_target_pairs={{0,8},{4,12},{8,0},{12,4},{16,24},{20,28},{24,16},{28,20},{1,9},{5... | collective-permute-start | bytes 589832 | tf_op jit(solution)/shard_map/ppermute | solution.py:95
  47.3 5.5 %collective-permute-start.8 = (bf16[1,4,128,128]{3,2,1,0:T(8,128)(2,1)S(1)}, bf16[1,4,128,128]{3,2,1,0:T(8,128)(2,1)S(1)}, u32[]{:S(2)}, u32[]{:S(2)}) collective-permute-start(bf16[1,4,128,128]{3,2,1,0:T(8,128)(2,1)S(1)} %get-tuple-element.103), channel_id=1, source_target_pairs={{0,8},{4,12},{8,0},{12,4},{16,24},{20,28},{24,16},{28,20},{1,9},{5... | collective-permute-start | bytes 393224 | tf_op jit(solution)/shard_map/ppermute | solution.py:95
  47.9 6.5 %collective-permute-start.9 = (bf16[1,4,128,128]{3,2,1,0:T(8,128)(2,1)S(1)}, bf16[1,4,128,128]{3,2,1,0:T(8,128)(2,1)S(1)}, u32[]{:S(2)}, u32[]{:S(2)}) collective-permute-start(bf16[1,4,128,128]{3,2,1,0:T(8,128)(2,1)S(1)} %get-tuple-element.104), channel_id=1, source_target_pairs={{0,16},{4,20},{8,24},{12,28},{16,0},{20,4},{24,8},{28,12},{1,17},{... | collective-permute-start | bytes 393224 | tf_op jit(solution)/shard_map/ppermute | solution.py:95
  55.0 4.3 %collective-permute-start.10 = (bf16[4,80,768]{2,1,0:T(8,128)(2,1)S(1)}, bf16[4,80,768]{2,1,0:T(8,128)(2,1)S(1)}, u32[]{:S(2)}, u32[]{:S(2)}) collective-permute-start(bf16[4,80,768]{2,1,0:T(8,128)(2,1)S(1)} %pad_maximum_fusion.3), channel_id=1, source_target_pairs={{0,4},{4,0},{8,12},{12,8},{16,20},{20,16},{24,28},{28,24},{1,5},{5... | collective-permute-start | bytes 1474568 | tf_op jit(solution)/shard_map/ppermute | solution.py:95
  55.0 4.2 %collective-permute-start.13 = (bf16[4,64,768]{2,1,0:T(8,128)(2,1)S(1)}, bf16[4,64,768]{2,1,0:T(8,128)(2,1)S(1)}, u32[]{:S(2)}, u32[]{:S(2)}) collective-permute-start(bf16[4,64,768]{2,1,0:T(8,128)(2,1)S(1)} %pad_maximum_fusion.4), channel_id=1, source_target_pairs={{0,4},{4,0},{8,12},{12,8},{16,20},{20,16},{24,28},{28,24},{1,5},{5... | collective-permute-start | bytes 1179656 | tf_op jit(solution)/shard_map/ppermute | solution.py:95
  56.6 26.9 %collective-permute-start.14 = (bf16[256,1024]{1,0:T(8,128)(2,1)S(1)}, bf16[256,1024]{1,0:T(8,128)(2,1)S(1)}, u32[]{:S(2)}, u32[]{:S(2)}) collective-permute-start(bf16[256,1024]{1,0:T(8,128)(2,1)S(1)} %copy-done.13), channel_id=1, source_target_pairs={{0,1},{1,0},{2,3},{3,2},{4,5},{5,4},{6,7},{7,6},{8,9},{9,8},{10,11... | collective-permute-start | bytes 1572872 | tf_op jit(solution)/shard_map/ppermute | solution.py:66
  57.7 25.9 %collective-permute-start.15 = (bf16[256,1024]{1,0:T(8,128)(2,1)S(1)}, bf16[256,1024]{1,0:T(8,128)(2,1)S(1)}, u32[]{:S(2)}, u32[]{:S(2)}) collective-permute-start(bf16[256,1024]{1,0:T(8,128)(2,1)S(1)} %copy-done.13), channel_id=1, source_target_pairs={{0,2},{1,3},{2,0},{3,1},{4,6},{5,7},{6,4},{7,5},{8,10},{9,11},{10,... | collective-permute-start | bytes 1572872 | tf_op jit(solution)/shard_map/ppermute | solution.py:66
  67.8 17.9 %collective-permute-start.20 = (bf16[2,4,128,128]{3,2,1,0:T(8,128)(2,1)S(1)}, bf16[2,4,128,128]{3,2,1,0:T(8,128)(2,1)S(1)}, u32[]{:S(2)}, u32[]{:S(2)}) collective-permute-start(bf16[2,4,128,128]{3,2,1,0:T(8,128)(2,1)S(1)} %constant_dynamic-update-slice_fusion.3), channel_id=1, source_target_pairs={{0,16},{4,20},{8,24},{12,28},{16,0},{20,4},{24,8},{28,12},{1,17},{... | collective-permute-start | bytes 786440 | tf_op jit(solution)/shard_map/ppermute | solution.py:95
  69.3 21.1 %collective-permute-start.22 = (bf16[2,4,128,128]{3,2,1,0:T(8,128)(2,1)S(1)}, bf16[2,4,128,128]{3,2,1,0:T(8,128)(2,1)S(1)}, u32[]{:S(2)}, u32[]{:S(2)}) collective-permute-start(bf16[2,4,128,128]{3,2,1,0:T(8,128)(2,1)S(1)} %constant_dynamic-update-slice_fusion.5), channel_id=1, source_target_pairs={{0,8},{4,12},{8,0},{12,4},{16,24},{20,28},{24,16},{28,20},{1,9},{5... | collective-permute-start | bytes 786440 | tf_op jit(solution)/shard_map/ppermute | solution.py:95
  83.6 19.2 %copy-start.38 = (bf16[256,1024]{1,0:T(8,128)(2,1)}, bf16[256,1024]{1,0:T(8,128)(2,1)S(1)}, u32[]{:S(2)}) copy-start(bf16[256,1024]{1,0:T(8,128)(2,1)S(1)} %collective-permute-done.15.refs_6_.refs_9_) | copy-start | bytes 1572868
  83.6 6.7 %collective-permute-start.17 = (bf16[256,256]{1,0:T(8,128)(2,1)}, bf16[256,256]{1,0:T(8,128)(2,1)S(1)}, u32[]{:S(2)}, u32[]{:S(2)}) collective-permute-start(bf16[256,256]{1,0:T(8,128)(2,1)} %get-tuple-element.117), channel_id=1, source_target_pairs={{0,1},{1,0},{2,3},{3,2},{4,5},{5,4},{6,7},{7,6},{8,9},{9,8},{10,11... | collective-permute-start | bytes 393224 | tf_op jit(solution)/shard_map/ppermute | solution.py:66
  85.3 17.4 %collective-permute-start.16 = (bf16[256,1024]{1,0:T(8,128)(2,1)S(1)}, bf16[256,1024]{1,0:T(8,128)(2,1)S(1)}, u32[]{:S(2)}, u32[]{:S(2)}) collective-permute-start(bf16[256,1024]{1,0:T(8,128)(2,1)S(1)} %collective-permute-done.15.refs_6_.refs_9_), channel_id=1, source_target_pairs={{0,1},{1,0},{2,3},{3,2},{4,5},{5,4},{6,7},{7,6},{8,9},{9,8},{10,11... | collective-permute-start | bytes 1572872 | tf_op jit(solution)/shard_map/ppermute | solution.py:66
  90.3 12.3 %collective-permute-start.21 = (bf16[4,4,128,128]{3,2,1,0:T(8,128)(2,1)S(1)}, bf16[4,4,128,128]{3,2,1,0:T(8,128)(2,1)S(1)}, u32[]{:S(2)}, u32[]{:S(2)}) collective-permute-start(bf16[4,4,128,128]{3,2,1,0:T(8,128)(2,1)S(1)} %pad_maximum_fusion.1), channel_id=1, source_target_pairs={{0,4},{4,0},{8,12},{12,8},{16,20},{20,16},{24,28},{28,24},{1,5},{5... | collective-permute-start | bytes 1572872 | tf_op jit(solution)/shard_map/ppermute | solution.py:95
  90.4 12.4 %collective-permute-start.23 = (bf16[4,4,128,128]{3,2,1,0:T(8,128)(2,1)S(1)}, bf16[4,4,128,128]{3,2,1,0:T(8,128)(2,1)S(1)}, u32[]{:S(2)}, u32[]{:S(2)}) collective-permute-start(bf16[4,4,128,128]{3,2,1,0:T(8,128)(2,1)S(1)} %pad_maximum_fusion.2), channel_id=1, source_target_pairs={{0,4},{4,0},{8,12},{12,8},{16,20},{20,16},{24,28},{28,24},{1,5},{5... | collective-permute-start | bytes 1572872 | tf_op jit(solution)/shard_map/ppermute | solution.py:95
  91.0 13.0 %collective-permute-start.18 = (bf16[256,256]{1,0:T(8,128)(2,1)}, bf16[256,256]{1,0:T(8,128)(2,1)S(1)}, u32[]{:S(2)}, u32[]{:S(2)}) collective-permute-start(bf16[256,256]{1,0:T(8,128)(2,1)} %get-tuple-element.119), channel_id=1, source_target_pairs={{0,2},{1,3},{2,0},{3,1},{4,6},{5,7},{6,4},{7,5},{8,10},{9,11},{10,... | collective-permute-start | bytes 393224 | tf_op jit(solution)/shard_map/ppermute | solution.py:66
  92.3 13.9 %collective-permute-start.19 = (bf16[256,256]{1,0:T(8,128)(2,1)}, bf16[256,256]{1,0:T(8,128)(2,1)S(1)}, u32[]{:S(2)}, u32[]{:S(2)}) collective-permute-start(bf16[256,256]{1,0:T(8,128)(2,1)} %get-tuple-element.121), channel_id=1, source_target_pairs={{0,3},{1,2},{2,1},{3,0},{4,7},{5,6},{6,5},{7,4},{8,11},{9,10},{10,... | collective-permute-start | bytes 393224 | tf_op jit(solution)/shard_map/ppermute | solution.py:66
  110.7 20.7 %collective-permute-start.24 = (bf16[256,1024]{1,0:T(8,128)(2,1)}, bf16[256,1024]{1,0:T(8,128)(2,1)S(1)}, u32[]{:S(2)}, u32[]{:S(2)}) collective-permute-start(bf16[256,1024]{1,0:T(8,128)(2,1)} %get-tuple-element.129.refs_0_.refs_3_), channel_id=1, source_target_pairs={{0,1},{1,0},{2,3},{3,2},{4,5},{5,4},{6,7},{7,6},{8,9},{9,8},{10,11... | collective-permute-start | bytes 1572872 | tf_op jit(solution)/shard_map/ppermute | solution.py:66
  111.3 22.0 %collective-permute-start.25 = (bf16[256,1024]{1,0:T(8,128)(2,1)}, bf16[256,1024]{1,0:T(8,128)(2,1)S(1)}, u32[]{:S(2)}, u32[]{:S(2)}) collective-permute-start(bf16[256,1024]{1,0:T(8,128)(2,1)} %get-tuple-element.129.refs_0_.refs_3_), channel_id=1, source_target_pairs={{0,2},{1,3},{2,0},{3,1},{4,6},{5,7},{6,4},{7,5},{8,10},{9,11},{10,... | collective-permute-start | bytes 1572872 | tf_op jit(solution)/shard_map/ppermute | solution.py:66
  131.4 13.5 %copy-start.41 = (bf16[256,1024]{1,0:T(8,128)(2,1)}, bf16[256,1024]{1,0:T(8,128)(2,1)S(1)}, u32[]{:S(2)}) copy-start(bf16[256,1024]{1,0:T(8,128)(2,1)S(1)} %collective-permute-done.24.refs_1_.refs_4_) | copy-start | bytes 1572868
  133.3 11.6 %collective-permute-start.26 = (bf16[256,1024]{1,0:T(8,128)(2,1)S(1)}, bf16[256,1024]{1,0:T(8,128)(2,1)S(1)}, u32[]{:S(2)}, u32[]{:S(2)}) collective-permute-start(bf16[256,1024]{1,0:T(8,128)(2,1)S(1)} %collective-permute-done.25.refs_2_.refs_5_), channel_id=1, source_target_pairs={{0,1},{1,0},{2,3},{3,2},{4,5},{5,4},{6,7},{7,6},{8,9},{9,8},{10,11... | collective-permute-start | bytes 1572872 | tf_op jit(solution)/shard_map/ppermute | solution.py:66
  197.4 13.4 %copy-start.44 = (bf16[256,1024]{1,0:T(8,128)(2,1)S(1)}, bf16[256,1024]{1,0:T(8,128)(2,1)}, u32[]{:S(2)}) copy-start(bf16[256,1024]{1,0:T(8,128)(2,1)} %get-tuple-element.148) | copy-start | bytes 1572868
  197.4 12.5 %collective-permute-start.27 = (bf16[256,1024]{1,0:T(8,128)(2,1)}, bf16[256,1024]{1,0:T(8,128)(2,1)S(1)}, u32[]{:S(2)}, u32[]{:S(2)}) collective-permute-start(bf16[256,1024]{1,0:T(8,128)(2,1)} %get-tuple-element.143), channel_id=1, source_target_pairs={{0,1},{1,0},{2,3},{3,2},{4,5},{5,4},{6,7},{7,6},{8,9},{9,8},{10,11... | collective-permute-start | bytes 1572872 | tf_op jit(solution)/shard_map/ppermute | solution.py:66
  210.2 27.4 %collective-permute-start.29 = (bf16[256,1024]{1,0:T(8,128)(2,1)S(1)}, bf16[256,1024]{1,0:T(8,128)(2,1)S(1)}, u32[]{:S(2)}, u32[]{:S(2)}) collective-permute-start(bf16[256,1024]{1,0:T(8,128)(2,1)S(1)} %add_convert_fusion.6), channel_id=1, source_target_pairs={{0,2},{1,3},{2,0},{3,1},{4,6},{5,7},{6,4},{7,5},{8,10},{9,11},{10,... | collective-permute-start | bytes 1572872 | tf_op jit(solution)/shard_map/ppermute | solution.py:66
  210.8 26.8 %collective-permute-start.28 = (bf16[256,1024]{1,0:T(8,128)(2,1)S(1)}, bf16[256,1024]{1,0:T(8,128)(2,1)S(1)}, u32[]{:S(2)}, u32[]{:S(2)}) collective-permute-start(bf16[256,1024]{1,0:T(8,128)(2,1)S(1)} %copy-done.44), channel_id=1, source_target_pairs={{0,1},{1,0},{2,3},{3,2},{4,5},{5,4},{6,7},{7,6},{8,9},{9,8},{10,11... | collective-permute-start | bytes 1572872 | tf_op jit(solution)/shard_map/ppermute | solution.py:66
  243.4 13.8 %copy-start.9 = (bf16[256,1024]{1,0:T(8,128)(2,1)S(1)}, bf16[256,1024]{1,0:T(8,128)(2,1)}, u32[]{:S(2)}) copy-start(bf16[256,1024]{1,0:T(8,128)(2,1)} %get-tuple-element.140) | copy-start | bytes 1572868
  243.4 13.7 %collective-permute-start.30 = (bf16[256,1024]{1,0:T(8,128)(2,1)S(1)}, bf16[256,1024]{1,0:T(8,128)(2,1)S(1)}, u32[]{:S(2)}, u32[]{:S(2)}) collective-permute-start(bf16[256,1024]{1,0:T(8,128)(2,1)S(1)} %copy-done.40), channel_id=1, source_target_pairs={{0,1},{1,0},{2,3},{3,2},{4,5},{5,4},{6,7},{7,6},{8,9},{9,8},{10,11... | collective-permute-start | bytes 1572872 | tf_op jit(solution)/shard_map/ppermute | solution.py:66
  244.3 14.3 %collective-permute-start.33 = (bf16[256,256]{1,0:T(8,128)(2,1)}, bf16[256,256]{1,0:T(8,128)(2,1)S(1)}, u32[]{:S(2)}, u32[]{:S(2)}) collective-permute-start(bf16[256,256]{1,0:T(8,128)(2,1)} %get-tuple-element.155), channel_id=1, source_target_pairs={{0,1},{1,0},{2,3},{3,2},{4,5},{5,4},{6,7},{7,6},{8,9},{9,8},{10,11... | collective-permute-start | bytes 393224 | tf_op jit(solution)/shard_map/ppermute | solution.py:66
  246.0 14.5 %collective-permute-start.34 = (bf16[256,256]{1,0:T(8,128)(2,1)}, bf16[256,256]{1,0:T(8,128)(2,1)S(1)}, u32[]{:S(2)}, u32[]{:S(2)}) collective-permute-start(bf16[256,256]{1,0:T(8,128)(2,1)} %get-tuple-element.156), channel_id=1, source_target_pairs={{0,2},{1,3},{2,0},{3,1},{4,6},{5,7},{6,4},{7,5},{8,10},{9,11},{10,... | collective-permute-start | bytes 393224 | tf_op jit(solution)/shard_map/ppermute | solution.py:66
  246.7 13.8 %collective-permute-start.35 = (bf16[256,256]{1,0:T(8,128)(2,1)}, bf16[256,256]{1,0:T(8,128)(2,1)S(1)}, u32[]{:S(2)}, u32[]{:S(2)}) collective-permute-start(bf16[256,256]{1,0:T(8,128)(2,1)} %get-tuple-element.157), channel_id=1, source_target_pairs={{0,3},{1,2},{2,1},{3,0},{4,7},{5,6},{6,5},{7,4},{8,11},{9,10},{10,... | collective-permute-start | bytes 393224 | tf_op jit(solution)/shard_map/ppermute | solution.py:66
  260.5 3.8 %collective-permute-start.36 = (bf16[4,1024,128]{2,1,0:T(8,128)(2,1)}, bf16[4,1024,128]{2,1,0:T(8,128)(2,1)S(1)}, u32[]{:S(2)}, u32[]{:S(2)}) collective-permute-start(bf16[4,1024,128]{2,1,0:T(8,128)(2,1)} %get-tuple-element.164), channel_id=1, source_target_pairs={{0,4},{4,0},{8,12},{12,8},{16,20},{20,16},{24,28},{28,24},{1,5},{5... | collective-permute-start | bytes 3145736 | tf_op jit(solution)/shard_map/ppermute | solution.py:100
  260.6 26.2 %collective-permute-start.32 = (bf16[256,1024]{1,0:T(8,128)(2,1)}, bf16[256,1024]{1,0:T(8,128)(2,1)}, u32[]{:S(2)}, u32[]{:S(2)}) collective-permute-start(bf16[256,1024]{1,0:T(8,128)(2,1)} %add_convert_fusion.5), channel_id=1, source_target_pairs={{0,2},{1,3},{2,0},{3,1},{4,6},{5,7},{6,4},{7,5},{8,10},{9,11},{10,... | collective-permute-start | bytes 1572872 | tf_op jit(solution)/shard_map/ppermute | solution.py:66
  263.7 23.8 %collective-permute-start.31 = (bf16[256,1024]{1,0:T(8,128)(2,1)}, bf16[256,1024]{1,0:T(8,128)(2,1)}, u32[]{:S(2)}, u32[]{:S(2)}) collective-permute-start(bf16[256,1024]{1,0:T(8,128)(2,1)} %get-tuple-element.151), channel_id=1, source_target_pairs={{0,1},{1,0},{2,3},{3,2},{4,5},{5,4},{6,7},{7,6},{8,9},{9,8},{10,11... | collective-permute-start | bytes 1572872 | tf_op jit(solution)/shard_map/ppermute | solution.py:66
  266.4 19.1 %collective-permute-start.37 = (bf16[2,1024,128]{2,1,0:T(8,128)(2,1)}, bf16[2,1024,128]{2,1,0:T(8,128)(2,1)}, u32[]{:S(2)}, u32[]{:S(2)}) collective-permute-start(bf16[2,1024,128]{2,1,0:T(8,128)(2,1)} %slice.171), channel_id=1, source_target_pairs={{0,8},{4,12},{8,0},{12,4},{16,24},{20,28},{24,16},{28,20},{1,9},{5... | collective-permute-start | bytes 1572872 | tf_op jit(solution)/shard_map/ppermute | solution.py:100
  267.3 18.2 %copy-start.5 = (bf16[4,1024,128]{2,1,0:T(8,128)(2,1)S(1)}, bf16[4,1024,128]{2,1,0:T(8,128)(2,1)}, u32[]{:S(2)}) copy-start(bf16[4,1024,128]{2,1,0:T(8,128)(2,1)} %copy-done.4) | copy-start | bytes 3145732
  287.6 16.6 %collective-permute-start.39 = (bf16[1,1024,128]{2,1,0:T(8,128)(2,1)S(1)}, bf16[1,1024,128]{2,1,0:T(8,128)(2,1)S(1)}, u32[]{:S(2)}, u32[]{:S(2)}) collective-permute-start(bf16[1,1024,128]{2,1,0:T(8,128)(2,1)S(1)} %slice.173), channel_id=1, source_target_pairs={{0,16},{4,20},{8,24},{12,28},{16,0},{20,4},{24,8},{28,12},{1,17},{... | collective-permute-start | bytes 786440 | tf_op jit(solution)/shard_map/ppermute | solution.py:100
  296.6 21.4 %collective-permute-start.38 = (bf16[256,1024]{1,0:T(8,128)(2,1)}, bf16[256,1024]{1,0:T(8,128)(2,1)S(1)}, u32[]{:S(2)}, u32[]{:S(2)}) collective-permute-start(bf16[256,1024]{1,0:T(8,128)(2,1)} %get-tuple-element.174), channel_id=1, source_target_pairs={{0,1},{1,0},{2,3},{3,2},{4,5},{5,4},{6,7},{7,6},{8,9},{9,8},{10,11... | collective-permute-start | bytes 1572872 | tf_op jit(solution)/shard_map/ppermute | solution.py:66
  300.7 10.3 %collective-permute-start.40 = (f32[8,1024]{1,0:T(8,128)}, f32[8,1024]{1,0:T(8,128)S(1)}, u32[]{:S(2)}, u32[]{:S(2)}) collective-permute-start(f32[8,1024]{1,0:T(8,128)} %get-tuple-element.177.refs_0_), channel_id=1, source_target_pairs={{0,1},{1,0},{2,3},{3,2},{4,5},{5,4},{6,7},{7,6},{8,9},{9,8},{10,11... | collective-permute-start | bytes 98312 | tf_op jit(solution)/shard_map/ppermute | solution.py:66
  300.7 10.8 %collective-permute-start.41 = (f32[8,1024]{1,0:T(8,128)}, f32[8,1024]{1,0:T(8,128)S(1)}, u32[]{:S(2)}, u32[]{:S(2)}) collective-permute-start(f32[8,1024]{1,0:T(8,128)} %get-tuple-element.177.refs_0_), channel_id=1, source_target_pairs={{0,2},{1,3},{2,0},{3,1},{4,6},{5,7},{6,4},{7,5},{8,10},{9,11},{10,... | collective-permute-start | bytes 98312 | tf_op jit(solution)/shard_map/ppermute | solution.py:66
  301.2 10.3 %collective-permute-start.42 = (f32[8,1024]{1,0:T(8,128)}, f32[8,1024]{1,0:T(8,128)S(1)}, u32[]{:S(2)}, u32[]{:S(2)}) collective-permute-start(f32[8,1024]{1,0:T(8,128)} %get-tuple-element.177.refs_0_), channel_id=1, source_target_pairs={{0,3},{1,2},{2,1},{3,0},{4,7},{5,6},{6,5},{7,4},{8,11},{9,10},{10,... | collective-permute-start | bytes 98312 | tf_op jit(solution)/shard_map/ppermute | solution.py:66
  304.3 13.7 %copy-start.10 = (bf16[256,1024]{1,0:T(8,128)(2,1)S(1)}, bf16[256,1024]{1,0:T(8,128)(2,1)}, u32[]{:S(2)}) copy-start(bf16[256,1024]{1,0:T(8,128)(2,1)} %get-tuple-element.173) | copy-start | bytes 1572868
  318.2 3.0 collective-permute-start.45
  318.3 30.8 %collective-permute-start.44 = (bf16[256,1024]{1,0:T(8,128)(2,1)S(1)}, bf16[256,1024]{1,0:T(8,128)(2,1)S(1)}, u32[]{:S(2)}, u32[]{:S(2)}) collective-permute-start(bf16[256,1024]{1,0:T(8,128)(2,1)S(1)} %add_convert_fusion.2), channel_id=1, source_target_pairs={{0,2},{1,3},{2,0},{3,1},{4,6},{5,7},{6,4},{7,5},{8,10},{9,11},{10,... | collective-permute-start | bytes 1572872 | tf_op jit(solution)/shard_map/ppermute | solution.py:66
  320.5 24.2 %collective-permute-start.43 = (bf16[256,1024]{1,0:T(8,128)(2,1)}, bf16[256,1024]{1,0:T(8,128)(2,1)S(1)}, u32[]{:S(2)}, u32[]{:S(2)}) collective-permute-start(bf16[256,1024]{1,0:T(8,128)(2,1)} %get-tuple-element.180), channel_id=1, source_target_pairs={{0,1},{1,0},{2,3},{3,2},{4,5},{5,4},{6,7},{7,6},{8,9},{9,8},{10,11... | collective-permute-start | bytes 1572872 | tf_op jit(solution)/shard_map/ppermute | solution.py:66
  322.7 30.8 %collective-permute-start.46 = (bf16[2,784,128]{2,1,0:T(8,128)(2,1)S(1)}, bf16[2,784,128]{2,1,0:T(8,128)(2,1)S(1)}, u32[]{:S(2)}, u32[]{:S(2)}) collective-permute-start(bf16[2,784,128]{2,1,0:T(8,128)(2,1)S(1)} %slice.175), channel_id=1, source_target_pairs={{0,8},{4,12},{8,0},{12,4},{16,24},{20,28},{24,16},{28,20},{1,9},{5... | collective-permute-start | bytes 1204232 | tf_op jit(solution)/shard_map/ppermute | solution.py:100
  344.8 8.9 %collective-permute-start.50 = (bf16[256,128]{1,0:T(8,128)(2,1)S(1)}, bf16[256,128]{1,0:T(8,128)(2,1)S(1)}, u32[]{:S(2)}, u32[]{:S(2)}) collective-permute-start(bf16[256,128]{1,0:T(8,128)(2,1)S(1)} %get-tuple-element.196), channel_id=1, source_target_pairs={{0,3},{1,2},{2,1},{3,0},{4,7},{5,6},{6,5},{7,4},{8,11},{9,10},{10,... | collective-permute-start | bytes 196616 | tf_op jit(solution)/shard_map/ppermute | solution.py:66
  345.5 8.2 %collective-permute-start.49 = (bf16[256,128]{1,0:T(8,128)(2,1)S(1)}, bf16[256,128]{1,0:T(8,128)(2,1)S(1)}, u32[]{:S(2)}, u32[]{:S(2)}) collective-permute-start(bf16[256,128]{1,0:T(8,128)(2,1)S(1)} %get-tuple-element.197), channel_id=1, source_target_pairs={{0,2},{1,3},{2,0},{3,1},{4,6},{5,7},{6,4},{7,5},{8,10},{9,11},{10,... | collective-permute-start | bytes 196616 | tf_op jit(solution)/shard_map/ppermute | solution.py:66
  349.1 4.6 %collective-permute-start.48 = (bf16[256,128]{1,0:T(8,128)(2,1)S(1)}, bf16[256,128]{1,0:T(8,128)(2,1)S(1)}, u32[]{:S(2)}, u32[]{:S(2)}) collective-permute-start(bf16[256,128]{1,0:T(8,128)(2,1)S(1)} %get-tuple-element.195), channel_id=1, source_target_pairs={{0,1},{1,0},{2,3},{3,2},{4,5},{5,4},{6,7},{7,6},{8,9},{9,8},{10,11... | collective-permute-start | bytes 196616 | tf_op jit(solution)/shard_map/ppermute | solution.py:66
  353.6 11.2 %collective-permute-start.47 = (bf16[1,784,128]{2,1,0:T(8,128)(2,1)S(1)}, bf16[1,784,128]{2,1,0:T(8,128)(2,1)S(1)}, u32[]{:S(2)}, u32[]{:S(2)}) collective-permute-start(bf16[1,784,128]{2,1,0:T(8,128)(2,1)S(1)} %slice.144), channel_id=1, source_target_pairs={{0,16},{4,20},{8,24},{12,28},{16,0},{20,4},{24,8},{28,12},{1,17},{... | collective-permute-start | bytes 602120 | tf_op jit(solution)/shard_map/ppermute | solution.py:100
  (40 other events, 196.3 us)
Sparse Core Ops, SparseCore 0:
  10.6 102.8 all-gather.2
  237.8 131.0 reduce-scatter.1

commit v3 on v2

--- a/solution.py
+++ b/solution.py
@@ -914,7 +914,7 @@
         expert_grads = lax.psum_scatter(weight_grads, "dp", scatter_dimension=0, tiled=False)
     else:
         expert_grads = lax.psum_scatter(weight_grads[0], "dp", scatter_dimension=2, tiled=True)
-    out_passed = z_swap(after(outs[3], aog), 1, z_size)
+    out_passed = z_swap(after(outs[3], far), 1, z_size)
     dos = z_direct(resid[3:], z_size)
     wo_keep, wo_send = wo_grad_call(slots, atts, aog, count)
     out_both = (outs[2].astype(F32) + out_passed.astype(F32)).astype(BF)

time: 383 us -> 381 us (level)
    ppermute x6, waiting for transfers between devices: 15.2 us -> 10.7 us  [dp_fold(): other = lax.ppermute(send, 'dp', [(i, i ^ bit) for i in range(8)])]
  transfers between devices with their start and end apart: 53 -> 53, of which waited for: 23 -> 24; matrix products, arithmetic and copies ran while one was open for 6% -> 6% of each run, Pallas kernels for 26% -> 26%
where the time goes in v3:
time: 381 us; the launch traced here: 377 us
  Pallas kernels  150 us (39%)
  waiting for transfers between devices  118 us (31%)
  starting transfers between devices  57.2 us (15%)
  local copies, waits for them, and re-layouts  19.9 us (5%)
  other arithmetic  16.9 us (4%)
  between operations  14.9 us (4%)
    ppermute x33, waiting for transfers between devices, z_swap(): return lax.ppermute(x, 'tensor', [(i, i ^ mask) for i in range(size)])  98.8 us
    ppermute x33, starting transfers between devices, z_swap(): return lax.ppermute(x, 'tensor', [(i, i ^ mask) for i in range(size)])  44.2 us
    pallas_call x1, Pallas kernels, units_call(): pl.pallas_call(functools.partial(units_body, chunks, unit), grid=(ff // B...  32 us
    pallas_call x2, Pallas kernels, product_call(): pl.pallas_call(functools.partial(product_body, len(xs), chunks, bool(extr...  30.2 us
    pallas_call x1, Pallas kernels, wgrad_call(): pl.pallas_call(functools.partial(wgrad_body, count, chunks), grid=(ff //...  25 us
    pallas_call x1, Pallas kernels, attn_bwd(): pl.pallas_call(functools.partial(bwd_body, total, chunks), grid=(heads,),...  14.8 us
    pallas_call x1, Pallas kernels, attn_fwd(): pl.pallas_call(functools.partial(fwd_body, total, chunks), grid=(heads,),...  13.7 us
    unnamed x114, local copies, waits for them, and re-layouts  10.8 us
  transfers between devices with their start and end apart: 53, of which 24 were waited for; matrix products, arithmetic and copies ran while one was open for 6% of the time, Pallas kernels for 26%

profile of v3, /device:TPU:14, one launch (start us, length us, event | category | flops | bytes accessed | tf_op | source)
XLA Modules:
  0.0 377.1 jit_solution(294738728523073611)
XLA Ops:
  7.2 3.1 pad_maximum_fusion
  11.9 2.6 collective-permute-start.1
  16.0 2.3 reduce-window.6
  19.1 1.6 fusion.2.refs_8_
  21.7 15.8 %collective-permute-done.1.refs_2_ = bf16[256,1024]{1,0:T(8,128)(2,1)S(1)} collective-permute-done((bf16[256,1024]{1,0:T(8,128)(2,1)S(1)}, bf16[256,1024]{1,0:T(8,128)(2,1)S(1)}, u32[]{:S(2)}, u32[]{:S(2)}) %collective-permute-start.1) | collective-permute-done | bytes 524320 | tf_op jit(solution)/shard_map/ppermute | solution.py:66
  37.9 3.5 collective-permute-start.6
  41.5 2.0 collective-permute-start.2
  44.6 1.2 collective-permute-done.6
  45.7 1.5 collective-permute-done.5
  48.5 4.3 %collective-permute-done.8 = bf16[1,4,128,128]{3,2,1,0:T(8,128)(2,1)S(1)} collective-permute-done((bf16[1,4,128,128]{3,2,1,0:T(8,128)(2,1)S(1)}, bf16[1,4,128,128]{3,2,1,0:T(8,128)(2,1)S(1)}, u32[]{:S(2)}, u32[]{:S(2)}) %collective-permute-start.8) | collective-permute-done | bytes 131104 | tf_op jit(solution)/shard_map/ppermute | solution.py:95
  52.9 1.5 collective-permute-done.9
  56.6 1.1 collective-permute-start.14
  57.7 1.4 collective-permute-start.15
  61.2 6.6 %norm_qkv.1 = (bf16[1024,1024]{1,0:T(8,128)(2,1)}, bf16[1024,256]{1,0:T(8,128)(2,1)}, bf16[1024,256]{1,0:T(8,128)(2,1)}, bf16[1024,256]{1,0:T(8,128)(2,1)}, bf16...) custom-call(s32[16]{0:T(128)} %pad_add_fusion.index_ref, ...), custom_call_target="tpu_custom_call" | custom-call | flops 1610612736 | bytes 8388608 | tf_op jit(solution)/shard_map/norm_qkv/pallas_call | solution.py:168
  67.8 1.5 collective-permute-start.20
  69.9 13.7 %attn_forward.1 = (bf16[4,1024,1024]{2,1,0:T(8,128)(2,1)}, f32[256,1024]{1,0:T(8,128)}, bf16[256,256]{1,0:T(8,128)(2,1)}, bf16[256,256]{1,0:T(8,128)(2,1)}, bf16...) custom-call(s32[1,2]{1,0:T(1,128)} %starts_ref.1, s32[4]{0:T(128)} %iota_xor_fusion.place_ref, ...), custom_call_target="tpu_custom_call" | custom-call | flops 4294967296 | bytes 10485760 | tf_op jit(solution)/shard_map/attn_forward/pallas_call | solution.py:261
  83.6 1.7 collective-permute-start.17
  85.8 4.6 %collective-permute-done.17.refs_1_ = bf16[256,256]{1,0:T(8,128)(2,1)S(1)} collective-permute-done((bf16[256,256]{1,0:T(8,128)(2,1)}, bf16[256,256]{1,0:T(8,128)(2,1)S(1)}, u32[]{:S(2)}, u32[]{:S(2)}) %collective-permute-start.17) | collective-permute-done | bytes 131104 | tf_op jit(solution)/shard_map/ppermute | solution.py:66
  91.0 1.3 collective-permute-start.18
  92.3 1.8 collective-permute-start.19
  94.1 8.5 %collective-permute-done.16.refs_7_.refs_10_ = bf16[256,1024]{1,0:T(8,128)(2,1)S(1)} collective-permute-done((bf16[256,1024]{1,0:T(8,128)(2,1)S(1)}, bf16[256,1024]{1,0:T(8,128)(2,1)S(1)}, u32[]{:S(2)}, u32[]{:S(2)}) %collective-permute-start.16) | collective-permute-done | bytes 524320 | tf_op jit(solution)/shard_map/ppermute | solution.py:66
  102.9 1.1 collective-permute-done.18.refs_2_
  104.0 2.2 collective-permute-done.19.refs_3_
  106.8 3.8 %out_projection_norm.1 = (f32[256,1024]{1,0:T(8,128)}, bf16[256,1024]{1,0:T(8,128)(2,1)}) custom-call(s32[16]{0:T(128)} %pad_add_fusion.index_ref, bf16[256,256]{1,0:T(8,128)(2,1)} %get-tuple-element.115.refs_0_, bf16[256,256]{1,0:T(8,128)(2,1)} %copy-done.22, bf16[256,256]{1,0:T(8,128)(2,1)} %copy-done.23, bf16[256,256]{1,0:T(8,128)(2,1)} %copy-done.24, ...), custom_call_target="tpu_custom_call" | custom-call | flops 536870912 | bytes 4194304 | tf_op jit(solution)/shard_map/out_projection_norm/pallas_call | solution.py:427
  112.1 19.3 %collective-permute-done.24.refs_1_.refs_4_ = bf16[256,1024]{1,0:T(8,128)(2,1)S(1)} collective-permute-done((bf16[256,1024]{1,0:T(8,128)(2,1)}, bf16[256,1024]{1,0:T(8,128)(2,1)S(1)}, u32[]{:S(2)}, u32[]{:S(2)}) %collective-permute-start.24) | collective-permute-done | bytes 524320 | tf_op jit(solution)/shard_map/ppermute | solution.py:66
  131.4 1.9 collective-permute-done.25.refs_2_.refs_5_
  133.3 2.3 collective-permute-start.26
  135.7 9.2 %collective-permute-done.26.refs_3_.refs_6_ = bf16[256,1024]{1,0:T(8,128)(2,1)S(1)} collective-permute-done((bf16[256,1024]{1,0:T(8,128)(2,1)S(1)}, bf16[256,1024]{1,0:T(8,128)(2,1)S(1)}, u32[]{:S(2)}, u32[]{:S(2)}) %collective-permute-start.26) | collective-permute-done | bytes 524320 | tf_op jit(solution)/shard_map/ppermute | solution.py:66
  145.7 32.0 %expert_units.1 = (bf16[1024,2816]{1,0:T(8,128)(2,1)}, bf16[1024,2816]{1,0:T(8,128)(2,1)}, bf16[1024,2816]{1,0:T(8,128)(2,1)}, f32[1024,128]{1,0:T(8,128)}, f32[8,1024]{1,0:T(8,128)}) custom-call(s32[4]{0:T(128)} %iota_xor_fusion.place_ref, bf16[256,1024]{1,0:T(8,128)(2,1)} %get-tuple-element.129.refs_0_.refs_3_, bf16[256,1024]{1,0:T(8,128)(2,1)} %copy-done.41, ...), custom_call_target="tpu_custom_call" | custom-call | flops 17716740096 | bytes 29884416 | tf_op jit(solution)/shard_map/expert_units/pallas_call | solution.py:530
  177.8 19.7 %normed_two_grads.1 = (bf16[256,1024]{1,0:T(8,128)(2,1)}, bf16[256,1024]{1,0:T(8,128)(2,1)}, bf16[256,1024]{1,0:T(8,128)(2,1)}, bf16[256,1024]{1,0:T(8,128)(2,1)}) custom-call(bf16[1024,2816]{1,0:T(8,128)(2,1)} %get-tuple-element.133.refs_0_.refs_1_, bf16[1024,2816]{1,0:T(8,128)(2,1)} %get-tuple-element.134.refs_1_.refs_2_, ...), custom_call_target="tpu_custom_call" | custom-call | flops 11811160064 | bytes 23068672 | tf_op jit(solution)/shard_map/normed_two_grads/pallas_call | solution.py:580
  197.5 2.1 collective-permute-start.27
  199.5 10.5 %expert_out.1 = (bf16[256,1024]{1,0:T(8,128)(2,1)}, bf16[256,1024]{1,0:T(8,128)(2,1)}, bf16[256,1024]{1,0:T(8,128)(2,1)}, bf16[256,1024]{1,0:T(8,128)(2,1)}) custom-call(bf16[1024,2816]{1,0:T(8,128)(2,1)} %get-tuple-element.147.refs_0_, bf16[8,3,2816,128]{3,2,1,0:T(8,128)(2,1)} %bitcast.81), custom_call_target="tpu_custom_call" | custom-call | flops 5905580032 | bytes 11534336 | tf_op jit(solution)/shard_map/expert_out/pallas_call | solution.py:580
  210.9 1.8 collective-permute-start.32
  212.6 25.0 %expert_weight_grads.1 = bf16[8,3,2816,128]{3,2,1,0:T(8,128)(2,1)} custom-call(bf16[1024,2816]{1,0:T(8,128)(2,1)} %get-tuple-element.147.refs_0_, bf16[1024,2816]{1,0:T(8,128)(2,1)} %get-tuple-element.133.refs_0_.refs_1_, bf16[1024,2816]{1,0:T(8,128)(2,1)} %get-tuple-element.134.refs_1_.refs_2_, bf16[256,1024]{1,0:T(8,128)(2,1)} %get-tuple-element.129.refs_0_.refs_3_, ...), custom_call_target="tpu_custom_call" | custom-call | flops 17716740096 | bytes 34603008 | tf_op jit(solution)/shard_map/expert_weight_grads/pallas_call | solution.py:620
  239.8 4.8 %resid_grad.1 = (f32[256,1024]{1,0:T(8,128)}, bf16[256,1024]{1,0:T(8,128)(2,1)}, f32[8,1024]{1,0:T(8,128)}, bf16[256,256]{1,0:T(8,128)(2,1)}, bf16[256,256]{1,0:...) custom-call(s32[16]{0:T(128)} %pad_add_fusion.index_ref, ...), custom_call_target="tpu_custom_call" | custom-call | flops 536870912 | bytes 4194304 | tf_op jit(solution)/shard_map/resid_grad/pallas_call | solution.py:661
  244.6 1.8 collective-permute-start.33
  247.0 1.1 collective-permute-start.35
  248.1 3.9 %w_output_grad.1 = (bf16[4,1024,128]{2,1,0:T(8,128)(2,1)}, bf16[4,1024,128]{2,1,0:T(8,128)(2,1)}) custom-call(s32[8]{0:T(128)} %fusion.17.slot_ref, bf16[256,256]{1,0:T(8,128)(2,1)} %get-tuple-element.115.refs_0_, bf16[256,256]{1,0:T(8,128)(2,1)} %copy-done.22, bf16[256,256]{1,0:T(8,128)(2,1)} %copy-done.23, bf16[256,256]{1,0:T(8,128)(2,1)} %copy-done.24, ...), custom_call_target="tpu_custom_call" | custom-call | flops 536870912 | bytes 4194304 | tf_op jit(solution)/shard_map/w_output_grad/pallas_call | solution.py:783
  252.7 1.0 add_convert_fusion.5
  254.1 1.9 collective-permute-done.34.refs_2_
  256.1 3.2 collective-permute-start.31
  261.4 2.1 collective-permute-start.37
  263.5 14.8 %attn_backward.1 = (bf16[1024,256]{1,0:T(8,128)(2,1)}, bf16[1024,256]{1,0:T(8,128)(2,1)}, bf16[1024,256]{1,0:T(8,128)(2,1)}, f32[4,5,512]{2,1,0:T(8,128)}) custom-call(s32[4]{0:T(128)} %iota_xor_fusion.place_ref, bf16[256,256]{1,0:T(8,128)(2,1)} %get-tuple-element.154.refs_0_, bf16[256,256]{1,0:T(8,128)(2,1)} %copy-done.45, bf16[256,256]{1,0:T(8,128)(2,1)} %copy-done.46, ...), custom_call_target="tpu_custom_call" | custom-call | flops 171798691840 | bytes 10485760 | tf_op jit(solution)/shard_map/attn_backward/pallas_call | solution.py:382
  278.4 1.2 add_convert_fusion.3
  279.6 2.4 collective-permute-done.31
  283.1 2.0 collective-permute-start.39
  285.1 5.9 %projection_grads.1 = (bf16[256,1024]{1,0:T(8,128)(2,1)}, bf16[256,1024]{1,0:T(8,128)(2,1)}, bf16[256,1024]{1,0:T(8,128)(2,1)}, bf16[256,1024]{1,0:T(8,128)(2,1)}, f32[8,1024]{1,0:T(8,128)}) custom-call(s32[16]{0:T(128)} %pad_add_fusion.index_ref, s32[4]{0:T(128)} %iota_xor_fusion.place_ref, bf16[1024,256]{1,0:T(8,128)(2,1)} %get-tuple-element.166.dq_ref, ...), custom_call_target="tpu_custom_call" | custom-call | flops 1610612736 | bytes 8388608 | tf_op jit(solution)/shard_map/projection_grads/pallas_call | solution.py:720
  291.0 2.5 collective-permute-start.38
  294.6 2.2 collective-permute-start.41
  296.8 1.3 collective-permute-start.42
  298.1 8.0 %collective-permute-done.40.refs_1_ = f32[8,1024]{1,0:T(8,128)S(1)} collective-permute-done((f32[8,1024]{1,0:T(8,128)}, f32[8,1024]{1,0:T(8,128)S(1)}, u32[]{:S(2)}, u32[]{:S(2)}) %collective-permute-start.40) | collective-permute-done | bytes 32800 | tf_op jit(solution)/shard_map/ppermute | solution.py:66
  308.3 5.3 %attn_weight_grads.1 = (bf16[4,784,128]{2,1,0:T(8,128)(2,1)}, bf16[4,784,128]{2,1,0:T(8,128)(2,1)}) custom-call(s32[8]{0:T(128)} %fusion.17.slot_ref, bf16[1024,1024]{1,0:T(8,128)(2,1)} %get-tuple-element.122.n1_ref, bf16[1024,256]{1,0:T(8,128)(2,1)} %get-tuple-element.166.dq_ref, bf16[1024,256]{1,0:T(8,128)(2,1)} %get-tuple-element.167.dk_ref, ...), custom_call_target="tpu_custom_call" | custom-call | flops 1610612736 | bytes 8388608 | tf_op jit(solution)/shard_map/attn_weight_grads/pallas_call | solution.py:756
  313.9 1.8 collective-permute-start.44
  316.4 1.4 add_convert_fusion.1
  317.8 2.0 collective-permute-start.46
  319.8 2.3 add_convert_fusion.4
  322.2 17.6 %collective-permute-done.43.refs_1_ = bf16[256,1024]{1,0:T(8,128)(2,1)S(1)} collective-permute-done((bf16[256,1024]{1,0:T(8,128)(2,1)}, bf16[256,1024]{1,0:T(8,128)(2,1)S(1)}, u32[]{:S(2)}, u32[]{:S(2)}) %collective-permute-start.43) | collective-permute-done | bytes 524320 | tf_op jit(solution)/shard_map/ppermute | solution.py:66
  339.7 1.3 collective-permute-start.50
  341.0 1.3 collective-permute-start.49
  342.3 1.4 collective-permute-start.48
  344.5 3.6 in_grad.1
  349.1 10.5 %collective-permute-done.47 = bf16[1,784,128]{2,1,0:T(8,128)(2,1)S(1)} collective-permute-done((bf16[1,784,128]{2,1,0:T(8,128)(2,1)S(1)}, bf16[1,784,128]{2,1,0:T(8,128)(2,1)S(1)}, u32[]{:S(2)}, u32[]{:S(2)}) %collective-permute-start.47) | collective-permute-done | bytes 200736 | tf_op jit(solution)/shard_map/ppermute | solution.py:100
  363.9 2.6 reduce-scatter.2.cloned.1.call-done
  366.5 3.7 fusion.19
  (243 shorter events, 34.9 us)
Async XLA Ops:
  7.2 13.6 %copy-start = (f32[4,32]{1,0:T(4,128)S(1)}, f32[4,32]{1,0:T(4,128)}, u32[]{:S(2)}) copy-start(f32[4,32]{1,0:T(4,128)} %param.24) | copy-start | bytes 1540
  7.2 137.7 %all-gather.3.cloned.1.call-start = ((), (), s32[]{:S(2)}) async-start(), calls=%async_computation.2 | async-start | bytes 19464192 | tf_op jit(solution)/shard_map/all_gather | solution.py:882
  10.4 27.0 %copy-start.28 = (bf16[256,128]{1,0:T(8,128)(2,1)S(1)}, bf16[256,128]{1,0:T(8,128)(2,1)}, u32[]{:S(2)}) copy-start(bf16[256,128]{1,0:T(8,128)(2,1)} %param.23) | copy-start | bytes 196612
  10.5 356.0 %reduce-scatter.2.cloned.1.call-start = ((), (), s32[]{:S(2)}) async-start(), calls=%async_computation.1 | async-start | bytes 19464192 | tf_op jit(solution)/shard_map/reduce_scatter | solution.py:914
  11.4 30.1 %collective-permute-start = (bf16[256,1024]{1,0:T(8,128)(2,1)S(1)}, bf16[256,1024]{1,0:T(8,128)(2,1)S(1)}, u32[]{:S(2)}, u32[]{:S(2)}) collective-permute-start(bf16[256,1024]{1,0:T(8,128)(2,1)S(1)} %copy-done.7), channel_id=1, source_target_pairs={{0,1},{1,0},{2,3},{3,2},{4,5},{5,4},{6,7},{7,6},{8,9},{9,8},{10,11... | collective-permute-start | bytes 1572872 | tf_op jit(solution)/shard_map/ppermute | solution.py:66
  11.9 25.6 %collective-permute-start.1 = (bf16[256,1024]{1,0:T(8,128)(2,1)S(1)}, bf16[256,1024]{1,0:T(8,128)(2,1)S(1)}, u32[]{:S(2)}, u32[]{:S(2)}) collective-permute-start(bf16[256,1024]{1,0:T(8,128)(2,1)S(1)} %copy-done.7), channel_id=1, source_target_pairs={{0,2},{1,3},{2,0},{3,1},{4,6},{5,7},{6,4},{7,5},{8,10},{9,11},{10,... | collective-permute-start | bytes 1572872 | tf_op jit(solution)/shard_map/ppermute | solution.py:66
  14.5 27.0 %collective-permute-start.3 = (bf16[1,80,768]{2,1,0:T(8,128)(2,1)S(1)}, bf16[1,80,768]{2,1,0:T(8,128)(2,1)S(1)}, u32[]{:S(2)}, u32[]{:S(2)}) collective-permute-start(bf16[1,80,768]{2,1,0:T(8,128)(2,1)S(1)} %slice_bitcast_fusion), channel_id=1, source_target_pairs={{0,8},{4,12},{8,0},{12,4},{16,24},{20,28},{24,16},{28,20},{1,9},{5... | collective-permute-start | bytes 368648 | tf_op jit(solution)/shard_map/ppermute | solution.py:95
  15.4 6.3 %collective-permute-start.11 = (bf16[1,64,768]{2,1,0:T(8,128)(2,1)S(1)}, bf16[1,64,768]{2,1,0:T(8,128)(2,1)S(1)}, u32[]{:S(2)}, u32[]{:S(2)}) collective-permute-start(bf16[1,64,768]{2,1,0:T(8,128)(2,1)S(1)} %maximum_bitcast_fusion.1), channel_id=1, source_target_pairs={{0,16},{4,20},{8,24},{12,28},{16,0},{20,4},{24,8},{28,12},{1,17},{... | collective-permute-start | bytes 294920 | tf_op jit(solution)/shard_map/ppermute | solution.py:95
  21.7 35.0 %copy-start.13 = (bf16[256,1024]{1,0:T(8,128)(2,1)S(1)}, bf16[256,1024]{1,0:T(8,128)(2,1)}, u32[]{:S(2)}) copy-start(bf16[256,1024]{1,0:T(8,128)(2,1)} %refs_4_.3) | copy-start | bytes 1572868
  37.4 17.1 %copy-start.35 = (bf16[256,1024]{1,0:T(8,128)(2,1)}, bf16[256,1024]{1,0:T(8,128)(2,1)S(1)}, u32[]{:S(2)}) copy-start(bf16[256,1024]{1,0:T(8,128)(2,1)S(1)} %collective-permute-done.1.refs_2_) | copy-start | bytes 1572868
  37.4 6.6 %collective-permute-start.7 = (bf16[256,128]{1,0:T(8,128)(2,1)S(1)}, bf16[256,128]{1,0:T(8,128)(2,1)S(1)}, u32[]{:S(2)}, u32[]{:S(2)}) collective-permute-start(bf16[256,128]{1,0:T(8,128)(2,1)S(1)} %copy-done.28), channel_id=1, source_target_pairs={{0,3},{1,2},{2,1},{3,0},{4,7},{5,6},{6,5},{7,4},{8,11},{9,10},{10,... | collective-permute-start | bytes 196616 | tf_op jit(solution)/shard_map/ppermute | solution.py:66
  37.9 7.9 %collective-permute-start.6 = (bf16[256,128]{1,0:T(8,128)(2,1)S(1)}, bf16[256,128]{1,0:T(8,128)(2,1)S(1)}, u32[]{:S(2)}, u32[]{:S(2)}) collective-permute-start(bf16[256,128]{1,0:T(8,128)(2,1)S(1)} %copy-done.28), channel_id=1, source_target_pairs={{0,2},{1,3},{2,0},{3,1},{4,6},{5,7},{6,4},{7,5},{8,10},{9,11},{10,... | collective-permute-start | bytes 196616 | tf_op jit(solution)/shard_map/ppermute | solution.py:66
  41.4 5.9 %collective-permute-start.5 = (bf16[256,128]{1,0:T(8,128)(2,1)S(1)}, bf16[256,128]{1,0:T(8,128)(2,1)S(1)}, u32[]{:S(2)}, u32[]{:S(2)}) collective-permute-start(bf16[256,128]{1,0:T(8,128)(2,1)S(1)} %copy-done.28), channel_id=1, source_target_pairs={{0,1},{1,0},{2,3},{3,2},{4,5},{5,4},{6,7},{7,6},{8,9},{9,8},{10,11... | collective-permute-start | bytes 196616 | tf_op jit(solution)/shard_map/ppermute | solution.py:66
  41.5 17.7 %copy-start.34 = (bf16[256,1024]{1,0:T(8,128)(2,1)}, bf16[256,1024]{1,0:T(8,128)(2,1)S(1)}, u32[]{:S(2)}) copy-start(bf16[256,1024]{1,0:T(8,128)(2,1)S(1)} %collective-permute-done.refs_1_) | copy-start | bytes 1572868
  41.5 13.5 %collective-permute-start.2 = (bf16[256,1024]{1,0:T(8,128)(2,1)S(1)}, bf16[256,1024]{1,0:T(8,128)(2,1)S(1)}, u32[]{:S(2)}, u32[]{:S(2)}) collective-permute-start(bf16[256,1024]{1,0:T(8,128)(2,1)S(1)} %collective-permute-done.1.refs_2_), channel_id=1, source_target_pairs={{0,1},{1,0},{2,3},{3,2},{4,5},{5,4},{6,7},{7,6},{8,9},{9,8},{10,11... | collective-permute-start | bytes 1572872 | tf_op jit(solution)/shard_map/ppermute | solution.py:66
  43.5 11.0 %collective-permute-start.4 = (bf16[2,80,768]{2,1,0:T(8,128)(2,1)S(1)}, bf16[2,80,768]{2,1,0:T(8,128)(2,1)S(1)}, u32[]{:S(2)}, u32[]{:S(2)}) collective-permute-start(bf16[2,80,768]{2,1,0:T(8,128)(2,1)S(1)} %pad_maximum_fusion.5), channel_id=1, source_target_pairs={{0,16},{4,20},{8,24},{12,28},{16,0},{20,4},{24,8},{28,12},{1,17},{... | collective-permute-start | bytes 737288 | tf_op jit(solution)/shard_map/ppermute | solution.py:95
  44.0 10.4 %collective-permute-start.12 = (bf16[2,64,768]{2,1,0:T(8,128)(2,1)S(1)}, bf16[2,64,768]{2,1,0:T(8,128)(2,1)S(1)}, u32[]{:S(2)}, u32[]{:S(2)}) collective-permute-start(bf16[2,64,768]{2,1,0:T(8,128)(2,1)S(1)} %pad_maximum_fusion.6), channel_id=1, source_target_pairs={{0,8},{4,12},{8,0},{12,4},{16,24},{20,28},{24,16},{28,20},{1,9},{5... | collective-permute-start | bytes 589832 | tf_op jit(solution)/shard_map/ppermute | solution.py:95
  47.3 5.5 %collective-permute-start.8 = (bf16[1,4,128,128]{3,2,1,0:T(8,128)(2,1)S(1)}, bf16[1,4,128,128]{3,2,1,0:T(8,128)(2,1)S(1)}, u32[]{:S(2)}, u32[]{:S(2)}) collective-permute-start(bf16[1,4,128,128]{3,2,1,0:T(8,128)(2,1)S(1)} %get-tuple-element.103), channel_id=1, source_target_pairs={{0,8},{4,12},{8,0},{12,4},{16,24},{20,28},{24,16},{28,20},{1,9},{5... | collective-permute-start | bytes 393224 | tf_op jit(solution)/shard_map/ppermute | solution.py:95
  47.9 6.5 %collective-permute-start.9 = (bf16[1,4,128,128]{3,2,1,0:T(8,128)(2,1)S(1)}, bf16[1,4,128,128]{3,2,1,0:T(8,128)(2,1)S(1)}, u32[]{:S(2)}, u32[]{:S(2)}) collective-permute-start(bf16[1,4,128,128]{3,2,1,0:T(8,128)(2,1)S(1)} %get-tuple-element.104), channel_id=1, source_target_pairs={{0,16},{4,20},{8,24},{12,28},{16,0},{20,4},{24,8},{28,12},{1,17},{... | collective-permute-start | bytes 393224 | tf_op jit(solution)/shard_map/ppermute | solution.py:95
  55.0 4.3 %collective-permute-start.10 = (bf16[4,80,768]{2,1,0:T(8,128)(2,1)S(1)}, bf16[4,80,768]{2,1,0:T(8,128)(2,1)S(1)}, u32[]{:S(2)}, u32[]{:S(2)}) collective-permute-start(bf16[4,80,768]{2,1,0:T(8,128)(2,1)S(1)} %pad_maximum_fusion.3), channel_id=1, source_target_pairs={{0,4},{4,0},{8,12},{12,8},{16,20},{20,16},{24,28},{28,24},{1,5},{5... | collective-permute-start | bytes 1474568 | tf_op jit(solution)/shard_map/ppermute | solution.py:95
  55.0 4.2 %collective-permute-start.13 = (bf16[4,64,768]{2,1,0:T(8,128)(2,1)S(1)}, bf16[4,64,768]{2,1,0:T(8,128)(2,1)S(1)}, u32[]{:S(2)}, u32[]{:S(2)}) collective-permute-start(bf16[4,64,768]{2,1,0:T(8,128)(2,1)S(1)} %pad_maximum_fusion.4), channel_id=1, source_target_pairs={{0,4},{4,0},{8,12},{12,8},{16,20},{20,16},{24,28},{28,24},{1,5},{5... | collective-permute-start | bytes 1179656 | tf_op jit(solution)/shard_map/ppermute | solution.py:95
  56.6 26.9 %collective-permute-start.14 = (bf16[256,1024]{1,0:T(8,128)(2,1)S(1)}, bf16[256,1024]{1,0:T(8,128)(2,1)S(1)}, u32[]{:S(2)}, u32[]{:S(2)}) collective-permute-start(bf16[256,1024]{1,0:T(8,128)(2,1)S(1)} %copy-done.13), channel_id=1, source_target_pairs={{0,1},{1,0},{2,3},{3,2},{4,5},{5,4},{6,7},{7,6},{8,9},{9,8},{10,11... | collective-permute-start | bytes 1572872 | tf_op jit(solution)/shard_map/ppermute | solution.py:66
  57.7 25.9 %collective-permute-start.15 = (bf16[256,1024]{1,0:T(8,128)(2,1)S(1)}, bf16[256,1024]{1,0:T(8,128)(2,1)S(1)}, u32[]{:S(2)}, u32[]{:S(2)}) collective-permute-start(bf16[256,1024]{1,0:T(8,128)(2,1)S(1)} %copy-done.13), channel_id=1, source_target_pairs={{0,2},{1,3},{2,0},{3,1},{4,6},{5,7},{6,4},{7,5},{8,10},{9,11},{10,... | collective-permute-start | bytes 1572872 | tf_op jit(solution)/shard_map/ppermute | solution.py:66
  67.8 17.9 %collective-permute-start.20 = (bf16[2,4,128,128]{3,2,1,0:T(8,128)(2,1)S(1)}, bf16[2,4,128,128]{3,2,1,0:T(8,128)(2,1)S(1)}, u32[]{:S(2)}, u32[]{:S(2)}) collective-permute-start(bf16[2,4,128,128]{3,2,1,0:T(8,128)(2,1)S(1)} %constant_dynamic-update-slice_fusion.3), channel_id=1, source_target_pairs={{0,16},{4,20},{8,24},{12,28},{16,0},{20,4},{24,8},{28,12},{1,17},{... | collective-permute-start | bytes 786440 | tf_op jit(solution)/shard_map/ppermute | solution.py:95
  69.3 21.1 %collective-permute-start.22 = (bf16[2,4,128,128]{3,2,1,0:T(8,128)(2,1)S(1)}, bf16[2,4,128,128]{3,2,1,0:T(8,128)(2,1)S(1)}, u32[]{:S(2)}, u32[]{:S(2)}) collective-permute-start(bf16[2,4,128,128]{3,2,1,0:T(8,128)(2,1)S(1)} %constant_dynamic-update-slice_fusion.5), channel_id=1, source_target_pairs={{0,8},{4,12},{8,0},{12,4},{16,24},{20,28},{24,16},{28,20},{1,9},{5... | collective-permute-start | bytes 786440 | tf_op jit(solution)/shard_map/ppermute | solution.py:95
  83.6 19.2 %copy-start.38 = (bf16[256,1024]{1,0:T(8,128)(2,1)}, bf16[256,1024]{1,0:T(8,128)(2,1)S(1)}, u32[]{:S(2)}) copy-start(bf16[256,1024]{1,0:T(8,128)(2,1)S(1)} %collective-permute-done.15.refs_6_.refs_9_) | copy-start | bytes 1572868
  83.6 6.7 %collective-permute-start.17 = (bf16[256,256]{1,0:T(8,128)(2,1)}, bf16[256,256]{1,0:T(8,128)(2,1)S(1)}, u32[]{:S(2)}, u32[]{:S(2)}) collective-permute-start(bf16[256,256]{1,0:T(8,128)(2,1)} %get-tuple-element.117), channel_id=1, source_target_pairs={{0,1},{1,0},{2,3},{3,2},{4,5},{5,4},{6,7},{7,6},{8,9},{9,8},{10,11... | collective-permute-start | bytes 393224 | tf_op jit(solution)/shard_map/ppermute | solution.py:66
  85.3 17.4 %collective-permute-start.16 = (bf16[256,1024]{1,0:T(8,128)(2,1)S(1)}, bf16[256,1024]{1,0:T(8,128)(2,1)S(1)}, u32[]{:S(2)}, u32[]{:S(2)}) collective-permute-start(bf16[256,1024]{1,0:T(8,128)(2,1)S(1)} %collective-permute-done.15.refs_6_.refs_9_), channel_id=1, source_target_pairs={{0,1},{1,0},{2,3},{3,2},{4,5},{5,4},{6,7},{7,6},{8,9},{9,8},{10,11... | collective-permute-start | bytes 1572872 | tf_op jit(solution)/shard_map/ppermute | solution.py:66
  90.3 12.3 %collective-permute-start.21 = (bf16[4,4,128,128]{3,2,1,0:T(8,128)(2,1)S(1)}, bf16[4,4,128,128]{3,2,1,0:T(8,128)(2,1)S(1)}, u32[]{:S(2)}, u32[]{:S(2)}) collective-permute-start(bf16[4,4,128,128]{3,2,1,0:T(8,128)(2,1)S(1)} %pad_maximum_fusion.1), channel_id=1, source_target_pairs={{0,4},{4,0},{8,12},{12,8},{16,20},{20,16},{24,28},{28,24},{1,5},{5... | collective-permute-start | bytes 1572872 | tf_op jit(solution)/shard_map/ppermute | solution.py:95
  90.4 12.4 %collective-permute-start.23 = (bf16[4,4,128,128]{3,2,1,0:T(8,128)(2,1)S(1)}, bf16[4,4,128,128]{3,2,1,0:T(8,128)(2,1)S(1)}, u32[]{:S(2)}, u32[]{:S(2)}) collective-permute-start(bf16[4,4,128,128]{3,2,1,0:T(8,128)(2,1)S(1)} %pad_maximum_fusion.2), channel_id=1, source_target_pairs={{0,4},{4,0},{8,12},{12,8},{16,20},{20,16},{24,28},{28,24},{1,5},{5... | collective-permute-start | bytes 1572872 | tf_op jit(solution)/shard_map/ppermute | solution.py:95
  91.0 13.0 %collective-permute-start.18 = (bf16[256,256]{1,0:T(8,128)(2,1)}, bf16[256,256]{1,0:T(8,128)(2,1)S(1)}, u32[]{:S(2)}, u32[]{:S(2)}) collective-permute-start(bf16[256,256]{1,0:T(8,128)(2,1)} %get-tuple-element.119), channel_id=1, source_target_pairs={{0,2},{1,3},{2,0},{3,1},{4,6},{5,7},{6,4},{7,5},{8,10},{9,11},{10,... | collective-permute-start | bytes 393224 | tf_op jit(solution)/shard_map/ppermute | solution.py:66
  92.3 13.9 %collective-permute-start.19 = (bf16[256,256]{1,0:T(8,128)(2,1)}, bf16[256,256]{1,0:T(8,128)(2,1)S(1)}, u32[]{:S(2)}, u32[]{:S(2)}) collective-permute-start(bf16[256,256]{1,0:T(8,128)(2,1)} %get-tuple-element.121), channel_id=1, source_target_pairs={{0,3},{1,2},{2,1},{3,0},{4,7},{5,6},{6,5},{7,4},{8,11},{9,10},{10,... | collective-permute-start | bytes 393224 | tf_op jit(solution)/shard_map/ppermute | solution.py:66
  110.7 20.7 %collective-permute-start.24 = (bf16[256,1024]{1,0:T(8,128)(2,1)}, bf16[256,1024]{1,0:T(8,128)(2,1)S(1)}, u32[]{:S(2)}, u32[]{:S(2)}) collective-permute-start(bf16[256,1024]{1,0:T(8,128)(2,1)} %get-tuple-element.129.refs_0_.refs_3_), channel_id=1, source_target_pairs={{0,1},{1,0},{2,3},{3,2},{4,5},{5,4},{6,7},{7,6},{8,9},{9,8},{10,11... | collective-permute-start | bytes 1572872 | tf_op jit(solution)/shard_map/ppermute | solution.py:66
  111.3 22.0 %collective-permute-start.25 = (bf16[256,1024]{1,0:T(8,128)(2,1)}, bf16[256,1024]{1,0:T(8,128)(2,1)S(1)}, u32[]{:S(2)}, u32[]{:S(2)}) collective-permute-start(bf16[256,1024]{1,0:T(8,128)(2,1)} %get-tuple-element.129.refs_0_.refs_3_), channel_id=1, source_target_pairs={{0,2},{1,3},{2,0},{3,1},{4,6},{5,7},{6,4},{7,5},{8,10},{9,11},{10,... | collective-permute-start | bytes 1572872 | tf_op jit(solution)/shard_map/ppermute | solution.py:66
  131.4 13.5 %copy-start.41 = (bf16[256,1024]{1,0:T(8,128)(2,1)}, bf16[256,1024]{1,0:T(8,128)(2,1)S(1)}, u32[]{:S(2)}) copy-start(bf16[256,1024]{1,0:T(8,128)(2,1)S(1)} %collective-permute-done.24.refs_1_.refs_4_) | copy-start | bytes 1572868
  133.3 11.6 %collective-permute-start.26 = (bf16[256,1024]{1,0:T(8,128)(2,1)S(1)}, bf16[256,1024]{1,0:T(8,128)(2,1)S(1)}, u32[]{:S(2)}, u32[]{:S(2)}) collective-permute-start(bf16[256,1024]{1,0:T(8,128)(2,1)S(1)} %collective-permute-done.25.refs_2_.refs_5_), channel_id=1, source_target_pairs={{0,1},{1,0},{2,3},{3,2},{4,5},{5,4},{6,7},{7,6},{8,9},{9,8},{10,11... | collective-permute-start | bytes 1572872 | tf_op jit(solution)/shard_map/ppermute | solution.py:66
  197.5 12.5 %copy-start.11 = (bf16[256,1024]{1,0:T(8,128)(2,1)S(1)}, bf16[256,1024]{1,0:T(8,128)(2,1)}, u32[]{:S(2)}) copy-start(bf16[256,1024]{1,0:T(8,128)(2,1)} %get-tuple-element.142) | copy-start | bytes 1572868
  197.5 13.4 %copy-start.44 = (bf16[256,1024]{1,0:T(8,128)(2,1)S(1)}, bf16[256,1024]{1,0:T(8,128)(2,1)}, u32[]{:S(2)}) copy-start(bf16[256,1024]{1,0:T(8,128)(2,1)} %get-tuple-element.150) | copy-start | bytes 1572868
  197.5 12.5 %collective-permute-start.27 = (bf16[256,1024]{1,0:T(8,128)(2,1)}, bf16[256,1024]{1,0:T(8,128)(2,1)S(1)}, u32[]{:S(2)}, u32[]{:S(2)}) collective-permute-start(bf16[256,1024]{1,0:T(8,128)(2,1)} %get-tuple-element.143), channel_id=1, source_target_pairs={{0,1},{1,0},{2,3},{3,2},{4,5},{5,4},{6,7},{7,6},{8,9},{9,8},{10,11... | collective-permute-start | bytes 1572872 | tf_op jit(solution)/shard_map/ppermute | solution.py:66
  210.2 27.4 %collective-permute-start.28 = (bf16[256,1024]{1,0:T(8,128)(2,1)S(1)}, bf16[256,1024]{1,0:T(8,128)(2,1)S(1)}, u32[]{:S(2)}, u32[]{:S(2)}) collective-permute-start(bf16[256,1024]{1,0:T(8,128)(2,1)S(1)} %add_convert_fusion.6), channel_id=1, source_target_pairs={{0,2},{1,3},{2,0},{3,1},{4,6},{5,7},{6,4},{7,5},{8,10},{9,11},{10,... | collective-permute-start | bytes 1572872 | tf_op jit(solution)/shard_map/ppermute | solution.py:66
  210.9 26.8 %collective-permute-start.32 = (bf16[256,1024]{1,0:T(8,128)(2,1)S(1)}, bf16[256,1024]{1,0:T(8,128)(2,1)S(1)}, u32[]{:S(2)}, u32[]{:S(2)}) collective-permute-start(bf16[256,1024]{1,0:T(8,128)(2,1)S(1)} %copy-done.44), channel_id=1, source_target_pairs={{0,1},{1,0},{2,3},{3,2},{4,5},{5,4},{6,7},{7,6},{8,9},{9,8},{10,11... | collective-permute-start | bytes 1572872 | tf_op jit(solution)/shard_map/ppermute | solution.py:66
  239.0 13.7 %collective-permute-start.29 = (bf16[256,1024]{1,0:T(8,128)(2,1)S(1)}, bf16[256,1024]{1,0:T(8,128)(2,1)S(1)}, u32[]{:S(2)}, u32[]{:S(2)}) collective-permute-start(bf16[256,1024]{1,0:T(8,128)(2,1)S(1)} %copy-done.40), channel_id=1, source_target_pairs={{0,1},{1,0},{2,3},{3,2},{4,5},{5,4},{6,7},{7,6},{8,9},{9,8},{10,11... | collective-permute-start | bytes 1572872 | tf_op jit(solution)/shard_map/ppermute | solution.py:66
  244.6 9.5 %collective-permute-start.33 = (bf16[256,256]{1,0:T(8,128)(2,1)}, bf16[256,256]{1,0:T(8,128)(2,1)S(1)}, u32[]{:S(2)}, u32[]{:S(2)}) collective-permute-start(bf16[256,256]{1,0:T(8,128)(2,1)} %get-tuple-element.155), channel_id=1, source_target_pairs={{0,1},{1,0},{2,3},{3,2},{4,5},{5,4},{6,7},{7,6},{8,9},{9,8},{10,11... | collective-permute-start | bytes 393224 | tf_op jit(solution)/shard_map/ppermute | solution.py:66
  246.4 9.7 %collective-permute-start.34 = (bf16[256,256]{1,0:T(8,128)(2,1)}, bf16[256,256]{1,0:T(8,128)(2,1)S(1)}, u32[]{:S(2)}, u32[]{:S(2)}) collective-permute-start(bf16[256,256]{1,0:T(8,128)(2,1)} %get-tuple-element.156), channel_id=1, source_target_pairs={{0,2},{1,3},{2,0},{3,1},{4,6},{5,7},{6,4},{7,5},{8,10},{9,11},{10,... | collective-permute-start | bytes 393224 | tf_op jit(solution)/shard_map/ppermute | solution.py:66
  247.0 9.0 %collective-permute-start.35 = (bf16[256,256]{1,0:T(8,128)(2,1)}, bf16[256,256]{1,0:T(8,128)(2,1)S(1)}, u32[]{:S(2)}, u32[]{:S(2)}) collective-permute-start(bf16[256,256]{1,0:T(8,128)(2,1)} %get-tuple-element.157), channel_id=1, source_target_pairs={{0,3},{1,2},{2,1},{3,0},{4,7},{5,6},{6,5},{7,4},{8,11},{9,10},{10,... | collective-permute-start | bytes 393224 | tf_op jit(solution)/shard_map/ppermute | solution.py:66
  256.0 3.2 collective-permute-start.36
  256.1 26.0 %collective-permute-start.31 = (bf16[256,1024]{1,0:T(8,128)(2,1)}, bf16[256,1024]{1,0:T(8,128)(2,1)}, u32[]{:S(2)}, u32[]{:S(2)}) collective-permute-start(bf16[256,1024]{1,0:T(8,128)(2,1)} %add_convert_fusion.5), channel_id=1, source_target_pairs={{0,2},{1,3},{2,0},{3,1},{4,6},{5,7},{6,4},{7,5},{8,10},{9,11},{10,... | collective-permute-start | bytes 1572872 | tf_op jit(solution)/shard_map/ppermute | solution.py:66
  259.3 23.8 %collective-permute-start.30 = (bf16[256,1024]{1,0:T(8,128)(2,1)}, bf16[256,1024]{1,0:T(8,128)(2,1)}, u32[]{:S(2)}, u32[]{:S(2)}) collective-permute-start(bf16[256,1024]{1,0:T(8,128)(2,1)} %get-tuple-element.146), channel_id=1, source_target_pairs={{0,1},{1,0},{2,3},{3,2},{4,5},{5,4},{6,7},{7,6},{8,9},{9,8},{10,11... | collective-permute-start | bytes 1572872 | tf_op jit(solution)/shard_map/ppermute | solution.py:66
  261.4 17.0 %collective-permute-start.37 = (bf16[2,1024,128]{2,1,0:T(8,128)(2,1)}, bf16[2,1024,128]{2,1,0:T(8,128)(2,1)}, u32[]{:S(2)}, u32[]{:S(2)}) collective-permute-start(bf16[2,1024,128]{2,1,0:T(8,128)(2,1)} %slice.171), channel_id=1, source_target_pairs={{0,8},{4,12},{8,0},{12,4},{16,24},{20,28},{24,16},{28,20},{1,9},{5... | collective-permute-start | bytes 1572872 | tf_op jit(solution)/shard_map/ppermute | solution.py:100
  263.5 14.9 %copy-start.5 = (bf16[4,1024,128]{2,1,0:T(8,128)(2,1)S(1)}, bf16[4,1024,128]{2,1,0:T(8,128)(2,1)}, u32[]{:S(2)}) copy-start(bf16[4,1024,128]{2,1,0:T(8,128)(2,1)} %copy-done.4) | copy-start | bytes 3145732
  283.1 14.9 %collective-permute-start.39 = (bf16[1,1024,128]{2,1,0:T(8,128)(2,1)S(1)}, bf16[1,1024,128]{2,1,0:T(8,128)(2,1)S(1)}, u32[]{:S(2)}, u32[]{:S(2)}) collective-permute-start(bf16[1,1024,128]{2,1,0:T(8,128)(2,1)S(1)} %slice.173), channel_id=1, source_target_pairs={{0,16},{4,20},{8,24},{12,28},{16,0},{20,4},{24,8},{28,12},{1,17},{... | collective-permute-start | bytes 786440 | tf_op jit(solution)/shard_map/ppermute | solution.py:100
  291.0 22.5 %collective-permute-start.38 = (bf16[256,1024]{1,0:T(8,128)(2,1)}, bf16[256,1024]{1,0:T(8,128)(2,1)S(1)}, u32[]{:S(2)}, u32[]{:S(2)}) collective-permute-start(bf16[256,1024]{1,0:T(8,128)(2,1)} %get-tuple-element.174), channel_id=1, source_target_pairs={{0,1},{1,0},{2,3},{3,2},{4,5},{5,4},{6,7},{7,6},{8,9},{9,8},{10,11... | collective-permute-start | bytes 1572872 | tf_op jit(solution)/shard_map/ppermute | solution.py:66
  294.6 11.6 %collective-permute-start.40 = (f32[8,1024]{1,0:T(8,128)}, f32[8,1024]{1,0:T(8,128)S(1)}, u32[]{:S(2)}, u32[]{:S(2)}) collective-permute-start(f32[8,1024]{1,0:T(8,128)} %get-tuple-element.177.refs_0_), channel_id=1, source_target_pairs={{0,1},{1,0},{2,3},{3,2},{4,5},{5,4},{6,7},{7,6},{8,9},{9,8},{10,11... | collective-permute-start | bytes 98312 | tf_op jit(solution)/shard_map/ppermute | solution.py:66
  294.6 12.5 %collective-permute-start.41 = (f32[8,1024]{1,0:T(8,128)}, f32[8,1024]{1,0:T(8,128)S(1)}, u32[]{:S(2)}, u32[]{:S(2)}) collective-permute-start(f32[8,1024]{1,0:T(8,128)} %get-tuple-element.177.refs_0_), channel_id=1, source_target_pairs={{0,2},{1,3},{2,0},{3,1},{4,6},{5,7},{6,4},{7,5},{8,10},{9,11},{10,... | collective-permute-start | bytes 98312 | tf_op jit(solution)/shard_map/ppermute | solution.py:66
  296.8 10.3 %collective-permute-start.42 = (f32[8,1024]{1,0:T(8,128)}, f32[8,1024]{1,0:T(8,128)S(1)}, u32[]{:S(2)}, u32[]{:S(2)}) collective-permute-start(f32[8,1024]{1,0:T(8,128)} %get-tuple-element.177.refs_0_), channel_id=1, source_target_pairs={{0,3},{1,2},{2,1},{3,0},{4,7},{5,6},{6,5},{7,4},{8,11},{9,10},{10,... | collective-permute-start | bytes 98312 | tf_op jit(solution)/shard_map/ppermute | solution.py:66
  298.1 15.4 %copy-start.10 = (bf16[256,1024]{1,0:T(8,128)(2,1)S(1)}, bf16[256,1024]{1,0:T(8,128)(2,1)}, u32[]{:S(2)}) copy-start(bf16[256,1024]{1,0:T(8,128)(2,1)} %get-tuple-element.173) | copy-start | bytes 1572868
  313.8 2.6 collective-permute-start.45
  313.9 29.9 %collective-permute-start.44 = (bf16[256,1024]{1,0:T(8,128)(2,1)S(1)}, bf16[256,1024]{1,0:T(8,128)(2,1)S(1)}, u32[]{:S(2)}, u32[]{:S(2)}) collective-permute-start(bf16[256,1024]{1,0:T(8,128)(2,1)S(1)} %add_convert_fusion.2), channel_id=1, source_target_pairs={{0,2},{1,3},{2,0},{3,1},{4,6},{5,7},{6,4},{7,5},{8,10},{9,11},{10,... | collective-permute-start | bytes 1572872 | tf_op jit(solution)/shard_map/ppermute | solution.py:66
  315.6 24.1 %collective-permute-start.43 = (bf16[256,1024]{1,0:T(8,128)(2,1)}, bf16[256,1024]{1,0:T(8,128)(2,1)S(1)}, u32[]{:S(2)}, u32[]{:S(2)}) collective-permute-start(bf16[256,1024]{1,0:T(8,128)(2,1)} %get-tuple-element.180), channel_id=1, source_target_pairs={{0,1},{1,0},{2,3},{3,2},{4,5},{5,4},{6,7},{7,6},{8,9},{9,8},{10,11... | collective-permute-start | bytes 1572872 | tf_op jit(solution)/shard_map/ppermute | solution.py:66
  317.8 30.4 %collective-permute-start.46 = (bf16[2,784,128]{2,1,0:T(8,128)(2,1)S(1)}, bf16[2,784,128]{2,1,0:T(8,128)(2,1)S(1)}, u32[]{:S(2)}, u32[]{:S(2)}) collective-permute-start(bf16[2,784,128]{2,1,0:T(8,128)(2,1)S(1)} %slice.175), channel_id=1, source_target_pairs={{0,8},{4,12},{8,0},{12,4},{16,24},{20,28},{24,16},{28,20},{1,9},{5... | collective-permute-start | bytes 1204232 | tf_op jit(solution)/shard_map/ppermute | solution.py:100
  339.7 8.6 %collective-permute-start.50 = (bf16[256,128]{1,0:T(8,128)(2,1)S(1)}, bf16[256,128]{1,0:T(8,128)(2,1)S(1)}, u32[]{:S(2)}, u32[]{:S(2)}) collective-permute-start(bf16[256,128]{1,0:T(8,128)(2,1)S(1)} %get-tuple-element.196), channel_id=1, source_target_pairs={{0,3},{1,2},{2,1},{3,0},{4,7},{5,6},{6,5},{7,4},{8,11},{9,10},{10,... | collective-permute-start | bytes 196616 | tf_op jit(solution)/shard_map/ppermute | solution.py:66
  341.0 7.3 %collective-permute-start.49 = (bf16[256,128]{1,0:T(8,128)(2,1)S(1)}, bf16[256,128]{1,0:T(8,128)(2,1)S(1)}, u32[]{:S(2)}, u32[]{:S(2)}) collective-permute-start(bf16[256,128]{1,0:T(8,128)(2,1)S(1)} %get-tuple-element.197), channel_id=1, source_target_pairs={{0,2},{1,3},{2,0},{3,1},{4,6},{5,7},{6,4},{7,5},{8,10},{9,11},{10,... | collective-permute-start | bytes 196616 | tf_op jit(solution)/shard_map/ppermute | solution.py:66
  342.3 6.0 %collective-permute-start.48 = (bf16[256,128]{1,0:T(8,128)(2,1)S(1)}, bf16[256,128]{1,0:T(8,128)(2,1)S(1)}, u32[]{:S(2)}, u32[]{:S(2)}) collective-permute-start(bf16[256,128]{1,0:T(8,128)(2,1)S(1)} %get-tuple-element.195), channel_id=1, source_target_pairs={{0,1},{1,0},{2,3},{3,2},{4,5},{5,4},{6,7},{7,6},{8,9},{9,8},{10,11... | collective-permute-start | bytes 196616 | tf_op jit(solution)/shard_map/ppermute | solution.py:66
  348.3 11.3 %collective-permute-start.47 = (bf16[1,784,128]{2,1,0:T(8,128)(2,1)S(1)}, bf16[1,784,128]{2,1,0:T(8,128)(2,1)S(1)}, u32[]{:S(2)}, u32[]{:S(2)}) collective-permute-start(bf16[1,784,128]{2,1,0:T(8,128)(2,1)S(1)} %slice.144), channel_id=1, source_target_pairs={{0,16},{4,20},{8,24},{12,28},{16,0},{20,4},{24,8},{28,12},{1,17},{... | collective-permute-start | bytes 602120 | tf_op jit(solution)/shard_map/ppermute | solution.py:100
  (40 other events, 184.8 us)
Sparse Core Ops, SparseCore 0:
  10.6 102.8 all-gather.2
  237.8 128.6 reduce-scatter.1

commit v4 on v3

--- a/solution.py
+++ b/solution.py
@@ -135,7 +135,7 @@
         small = [small_ref[r : r + 1, :] for r in range(2 + EXPERTS)]
     else:
         row = depth - first_ref.shape[1]
-        lines = [small_ref[index_ref[count + d], row : row + 1, :].astype(F32) for d in range(count)]
+        lines = [small_ref[index_ref[count + d], row : row + 16, :].astype(F32)[0:1] for d in range(count)]
         small = [
             jnp.concatenate([x[:, depth * r : depth * (r + 1)] for x in lines], 1) for r in range(2 + EXPERTS)
         ]
@@ -493,13 +493,12 @@
     e_low = (step * width) // unit
     e_high = (step * width + width - 1) // unit
     bound = jnp.where(e_high > e_low, unit * e_high - step * width, width)
-    lows, highs = [], []
+    lows = []
     for m in range(width // 128):
         is_low = lane + 128 * m < bound
         part = slice(128 * m, 128 * (m + 1))
         gate = jnp.where(is_low, gate_ref[e_low], gate_ref[e_high])
         lows.append(jnp.where(is_low, prod[:, part], 0.0))
-        highs.append(prod[:, part] - lows[m])
         hg_ref[:, part] = (gate * hidden[:, part]).astype(BF)
         hidden_grad = gate * raw[:, part]
         gg_ref[:, part] = (hidden_grad * up_pre[:, part] * slope[:, part]).astype(BF)
@@ -508,7 +507,8 @@
 
     @pl.when(e_high > e_low)
     def _():
-        sum_ref[e_high] += functools.reduce(jnp.add, highs)
+        every = [prod[:, 128 * m : 128 * (m + 1)] - lows[m] for m in range(width // 128)]
+        sum_ref[e_high] += functools.reduce(jnp.add, every)
 
     @pl.when(step == steps - 1)
     def _():

time: 381 us -> 381 us (level)
  no operation moved by 1% of the time
where the time goes in v4:
time: 381 us; the launch traced here: 377 us
  Pallas kernels  150 us (39%)
  waiting for transfers between devices  118 us (31%)
  starting transfers between devices  56.9 us (15%)
  local copies, waits for them, and re-layouts  19.9 us (5%)
  other arithmetic  16.9 us (4%)
  between operations  14.9 us (4%)
    ppermute x33, waiting for transfers between devices, z_swap(): return lax.ppermute(x, 'tensor', [(i, i ^ mask) for i in range(size)])  99 us
    ppermute x33, starting transfers between devices, z_swap(): return lax.ppermute(x, 'tensor', [(i, i ^ mask) for i in range(size)])  44.3 us
    pallas_call x1, Pallas kernels, units_call(): pl.pallas_call(functools.partial(units_body, chunks, unit), grid=(ff // B...  32 us
    pallas_call x2, Pallas kernels, product_call(): pl.pallas_call(functools.partial(product_body, len(xs), chunks, bool(extr...  30.2 us
    pallas_call x1, Pallas kernels, wgrad_call(): pl.pallas_call(functools.partial(wgrad_body, count, chunks), grid=(ff //...  25 us
    pallas_call x1, Pallas kernels, attn_bwd(): pl.pallas_call(functools.partial(bwd_body, total, chunks), grid=(heads,),...  14.9 us
    pallas_call x1, Pallas kernels, attn_fwd(): pl.pallas_call(functools.partial(fwd_body, total, chunks), grid=(heads,),...  13.7 us
    unnamed x114, local copies, waits for them, and re-layouts  10.8 us
  transfers between devices with their start and end apart: 53, of which 24 were waited for; matrix products, arithmetic and copies ran while one was open for 6% of the time, Pallas kernels for 26%

profile of v4, /device:TPU:14, one launch (start us, length us, event | category | flops | bytes accessed | tf_op | source)
XLA Modules:
  0.0 377.0 jit_solution(4166266536863421377)
XLA Ops:
  7.2 3.1 pad_maximum_fusion
  11.9 2.6 collective-permute-start.1
  16.0 2.3 reduce-window.6
  19.1 1.6 fusion.2.refs_8_
  21.7 15.8 %collective-permute-done.1.refs_2_ = bf16[256,1024]{1,0:T(8,128)(2,1)S(1)} collective-permute-done((bf16[256,1024]{1,0:T(8,128)(2,1)S(1)}, bf16[256,1024]{1,0:T(8,128)(2,1)S(1)}, u32[]{:S(2)}, u32[]{:S(2)}) %collective-permute-start.1) | collective-permute-done | bytes 524320 | tf_op jit(solution)/shard_map/ppermute | solution.py:66
  37.9 3.5 collective-permute-start.6
  41.5 2.0 collective-permute-start.2
  44.6 1.2 collective-permute-done.6
  45.7 1.5 collective-permute-done.5
  48.5 4.3 %collective-permute-done.8 = bf16[1,4,128,128]{3,2,1,0:T(8,128)(2,1)S(1)} collective-permute-done((bf16[1,4,128,128]{3,2,1,0:T(8,128)(2,1)S(1)}, bf16[1,4,128,128]{3,2,1,0:T(8,128)(2,1)S(1)}, u32[]{:S(2)}, u32[]{:S(2)}) %collective-permute-start.8) | collective-permute-done | bytes 131104 | tf_op jit(solution)/shard_map/ppermute | solution.py:95
  52.9 1.5 collective-permute-done.9
  56.6 1.1 collective-permute-start.14
  57.7 1.4 collective-permute-start.15
  61.2 6.6 %norm_qkv.1 = (bf16[1024,1024]{1,0:T(8,128)(2,1)}, bf16[1024,256]{1,0:T(8,128)(2,1)}, bf16[1024,256]{1,0:T(8,128)(2,1)}, bf16[1024,256]{1,0:T(8,128)(2,1)}, bf16...) custom-call(s32[16]{0:T(128)} %pad_add_fusion.index_ref, ...), custom_call_target="tpu_custom_call" | custom-call | flops 1610612736 | bytes 8388608 | tf_op jit(solution)/shard_map/norm_qkv/pallas_call | solution.py:168
  67.8 1.5 collective-permute-start.20
  69.9 13.7 %attn_forward.1 = (bf16[4,1024,1024]{2,1,0:T(8,128)(2,1)}, f32[256,1024]{1,0:T(8,128)}, bf16[256,256]{1,0:T(8,128)(2,1)}, bf16[256,256]{1,0:T(8,128)(2,1)}, bf16...) custom-call(s32[1,2]{1,0:T(1,128)} %starts_ref.1, s32[4]{0:T(128)} %iota_xor_fusion.place_ref, ...), custom_call_target="tpu_custom_call" | custom-call | flops 4294967296 | bytes 10485760 | tf_op jit(solution)/shard_map/attn_forward/pallas_call | solution.py:261
  83.6 1.7 collective-permute-start.17
  85.8 4.6 %collective-permute-done.17.refs_1_ = bf16[256,256]{1,0:T(8,128)(2,1)S(1)} collective-permute-done((bf16[256,256]{1,0:T(8,128)(2,1)}, bf16[256,256]{1,0:T(8,128)(2,1)S(1)}, u32[]{:S(2)}, u32[]{:S(2)}) %collective-permute-start.17) | collective-permute-done | bytes 131104 | tf_op jit(solution)/shard_map/ppermute | solution.py:66
  91.0 1.3 collective-permute-start.18
  92.3 1.8 collective-permute-start.19
  94.1 8.5 %collective-permute-done.16.refs_7_.refs_10_ = bf16[256,1024]{1,0:T(8,128)(2,1)S(1)} collective-permute-done((bf16[256,1024]{1,0:T(8,128)(2,1)S(1)}, bf16[256,1024]{1,0:T(8,128)(2,1)S(1)}, u32[]{:S(2)}, u32[]{:S(2)}) %collective-permute-start.16) | collective-permute-done | bytes 524320 | tf_op jit(solution)/shard_map/ppermute | solution.py:66
  102.9 1.1 collective-permute-done.18.refs_2_
  104.0 2.2 collective-permute-done.19.refs_3_
  106.9 3.8 %out_projection_norm.1 = (f32[256,1024]{1,0:T(8,128)}, bf16[256,1024]{1,0:T(8,128)(2,1)}) custom-call(s32[16]{0:T(128)} %pad_add_fusion.index_ref, bf16[256,256]{1,0:T(8,128)(2,1)} %get-tuple-element.115.refs_0_, bf16[256,256]{1,0:T(8,128)(2,1)} %copy-done.22, bf16[256,256]{1,0:T(8,128)(2,1)} %copy-done.23, bf16[256,256]{1,0:T(8,128)(2,1)} %copy-done.24, ...), custom_call_target="tpu_custom_call" | custom-call | flops 536870912 | bytes 4194304 | tf_op jit(solution)/shard_map/out_projection_norm/pallas_call | solution.py:427
  112.1 19.3 %collective-permute-done.24.refs_1_.refs_4_ = bf16[256,1024]{1,0:T(8,128)(2,1)S(1)} collective-permute-done((bf16[256,1024]{1,0:T(8,128)(2,1)}, bf16[256,1024]{1,0:T(8,128)(2,1)S(1)}, u32[]{:S(2)}, u32[]{:S(2)}) %collective-permute-start.24) | collective-permute-done | bytes 524320 | tf_op jit(solution)/shard_map/ppermute | solution.py:66
  131.4 1.9 collective-permute-done.25.refs_2_.refs_5_
  133.3 2.4 collective-permute-start.26
  135.7 9.2 %collective-permute-done.26.refs_3_.refs_6_ = bf16[256,1024]{1,0:T(8,128)(2,1)S(1)} collective-permute-done((bf16[256,1024]{1,0:T(8,128)(2,1)S(1)}, bf16[256,1024]{1,0:T(8,128)(2,1)S(1)}, u32[]{:S(2)}, u32[]{:S(2)}) %collective-permute-start.26) | collective-permute-done | bytes 524320 | tf_op jit(solution)/shard_map/ppermute | solution.py:66
  145.7 32.0 %expert_units.1 = (bf16[1024,2816]{1,0:T(8,128)(2,1)}, bf16[1024,2816]{1,0:T(8,128)(2,1)}, bf16[1024,2816]{1,0:T(8,128)(2,1)}, f32[1024,128]{1,0:T(8,128)}, f32[8,1024]{1,0:T(8,128)}) custom-call(s32[4]{0:T(128)} %iota_xor_fusion.place_ref, bf16[256,1024]{1,0:T(8,128)(2,1)} %get-tuple-element.129.refs_0_.refs_3_, bf16[256,1024]{1,0:T(8,128)(2,1)} %copy-done.41, ...), custom_call_target="tpu_custom_call" | custom-call | flops 17716740096 | bytes 29884416 | tf_op jit(solution)/shard_map/expert_units/pallas_call | solution.py:530
  177.7 19.7 %normed_two_grads.1 = (bf16[256,1024]{1,0:T(8,128)(2,1)}, bf16[256,1024]{1,0:T(8,128)(2,1)}, bf16[256,1024]{1,0:T(8,128)(2,1)}, bf16[256,1024]{1,0:T(8,128)(2,1)}) custom-call(bf16[1024,2816]{1,0:T(8,128)(2,1)} %get-tuple-element.133.refs_0_.refs_1_, bf16[1024,2816]{1,0:T(8,128)(2,1)} %get-tuple-element.134.refs_1_.refs_2_, ...), custom_call_target="tpu_custom_call" | custom-call | flops 11811160064 | bytes 23068672 | tf_op jit(solution)/shard_map/normed_two_grads/pallas_call | solution.py:580
  197.4 2.1 collective-permute-start.27
  199.5 10.5 %expert_out.1 = (bf16[256,1024]{1,0:T(8,128)(2,1)}, bf16[256,1024]{1,0:T(8,128)(2,1)}, bf16[256,1024]{1,0:T(8,128)(2,1)}, bf16[256,1024]{1,0:T(8,128)(2,1)}) custom-call(bf16[1024,2816]{1,0:T(8,128)(2,1)} %get-tuple-element.147.refs_0_, bf16[8,3,2816,128]{3,2,1,0:T(8,128)(2,1)} %bitcast.81), custom_call_target="tpu_custom_call" | custom-call | flops 5905580032 | bytes 11534336 | tf_op jit(solution)/shard_map/expert_out/pallas_call | solution.py:580
  210.8 1.7 collective-permute-start.32
  212.6 25.0 %expert_weight_grads.1 = bf16[8,3,2816,128]{3,2,1,0:T(8,128)(2,1)} custom-call(bf16[1024,2816]{1,0:T(8,128)(2,1)} %get-tuple-element.147.refs_0_, bf16[1024,2816]{1,0:T(8,128)(2,1)} %get-tuple-element.133.refs_0_.refs_1_, bf16[1024,2816]{1,0:T(8,128)(2,1)} %get-tuple-element.134.refs_1_.refs_2_, bf16[256,1024]{1,0:T(8,128)(2,1)} %get-tuple-element.129.refs_0_.refs_3_, ...), custom_call_target="tpu_custom_call" | custom-call | flops 17716740096 | bytes 34603008 | tf_op jit(solution)/shard_map/expert_weight_grads/pallas_call | solution.py:620
  239.7 4.8 %resid_grad.1 = (f32[256,1024]{1,0:T(8,128)}, bf16[256,1024]{1,0:T(8,128)(2,1)}, f32[8,1024]{1,0:T(8,128)}, bf16[256,256]{1,0:T(8,128)(2,1)}, bf16[256,256]{1,0:...) custom-call(s32[16]{0:T(128)} %pad_add_fusion.index_ref, ...), custom_call_target="tpu_custom_call" | custom-call | flops 536870912 | bytes 4194304 | tf_op jit(solution)/shard_map/resid_grad/pallas_call | solution.py:661
  244.5 1.8 collective-permute-start.33
  247.0 1.1 collective-permute-start.35
  248.0 3.9 %w_output_grad.1 = (bf16[4,1024,128]{2,1,0:T(8,128)(2,1)}, bf16[4,1024,128]{2,1,0:T(8,128)(2,1)}) custom-call(s32[8]{0:T(128)} %fusion.17.slot_ref, bf16[256,256]{1,0:T(8,128)(2,1)} %get-tuple-element.115.refs_0_, bf16[256,256]{1,0:T(8,128)(2,1)} %copy-done.22, bf16[256,256]{1,0:T(8,128)(2,1)} %copy-done.23, bf16[256,256]{1,0:T(8,128)(2,1)} %copy-done.24, ...), custom_call_target="tpu_custom_call" | custom-call | flops 536870912 | bytes 4194304 | tf_op jit(solution)/shard_map/w_output_grad/pallas_call | solution.py:783
  252.6 1.0 add_convert_fusion.5
  254.0 1.9 collective-permute-done.34.refs_2_
  256.1 3.1 collective-permute-start.31
  261.3 1.8 collective-permute-start.37
  263.2 14.9 %attn_backward.1 = (bf16[1024,256]{1,0:T(8,128)(2,1)}, bf16[1024,256]{1,0:T(8,128)(2,1)}, bf16[1024,256]{1,0:T(8,128)(2,1)}, f32[4,5,512]{2,1,0:T(8,128)}) custom-call(s32[4]{0:T(128)} %iota_xor_fusion.place_ref, bf16[256,256]{1,0:T(8,128)(2,1)} %get-tuple-element.154.refs_0_, bf16[256,256]{1,0:T(8,128)(2,1)} %copy-done.45, bf16[256,256]{1,0:T(8,128)(2,1)} %copy-done.46, ...), custom_call_target="tpu_custom_call" | custom-call | flops 171798691840 | bytes 10485760 | tf_op jit(solution)/shard_map/attn_backward/pallas_call | solution.py:382
  278.1 1.2 add_convert_fusion.3
  279.4 2.7 collective-permute-done.31
  283.0 2.0 collective-permute-start.39
  285.1 5.9 %projection_grads.1 = (bf16[256,1024]{1,0:T(8,128)(2,1)}, bf16[256,1024]{1,0:T(8,128)(2,1)}, bf16[256,1024]{1,0:T(8,128)(2,1)}, bf16[256,1024]{1,0:T(8,128)(2,1)}, f32[8,1024]{1,0:T(8,128)}) custom-call(s32[16]{0:T(128)} %pad_add_fusion.index_ref, s32[4]{0:T(128)} %iota_xor_fusion.place_ref, bf16[1024,256]{1,0:T(8,128)(2,1)} %get-tuple-element.166.dq_ref, ...), custom_call_target="tpu_custom_call" | custom-call | flops 1610612736 | bytes 8388608 | tf_op jit(solution)/shard_map/projection_grads/pallas_call | solution.py:720
  291.0 2.5 collective-permute-start.38
  294.6 2.2 collective-permute-start.41
  296.8 1.3 collective-permute-start.42
  298.1 8.0 %collective-permute-done.40.refs_1_ = f32[8,1024]{1,0:T(8,128)S(1)} collective-permute-done((f32[8,1024]{1,0:T(8,128)}, f32[8,1024]{1,0:T(8,128)S(1)}, u32[]{:S(2)}, u32[]{:S(2)}) %collective-permute-start.40) | collective-permute-done | bytes 32800 | tf_op jit(solution)/shard_map/ppermute | solution.py:66
  308.3 5.3 %attn_weight_grads.1 = (bf16[4,784,128]{2,1,0:T(8,128)(2,1)}, bf16[4,784,128]{2,1,0:T(8,128)(2,1)}) custom-call(s32[8]{0:T(128)} %fusion.17.slot_ref, bf16[1024,1024]{1,0:T(8,128)(2,1)} %get-tuple-element.122.n1_ref, bf16[1024,256]{1,0:T(8,128)(2,1)} %get-tuple-element.166.dq_ref, bf16[1024,256]{1,0:T(8,128)(2,1)} %get-tuple-element.167.dk_ref, ...), custom_call_target="tpu_custom_call" | custom-call | flops 1610612736 | bytes 8388608 | tf_op jit(solution)/shard_map/attn_weight_grads/pallas_call | solution.py:756
  313.8 1.8 collective-permute-start.44
  316.3 1.4 add_convert_fusion.1
  317.8 2.0 collective-permute-start.46
  319.8 2.3 add_convert_fusion.4
  322.1 17.6 %collective-permute-done.43.refs_1_ = bf16[256,1024]{1,0:T(8,128)(2,1)S(1)} collective-permute-done((bf16[256,1024]{1,0:T(8,128)(2,1)}, bf16[256,1024]{1,0:T(8,128)(2,1)S(1)}, u32[]{:S(2)}, u32[]{:S(2)}) %collective-permute-start.43) | collective-permute-done | bytes 524320 | tf_op jit(solution)/shard_map/ppermute | solution.py:66
  339.7 1.3 collective-permute-start.50
  341.0 1.3 collective-permute-start.49
  342.3 1.4 collective-permute-start.48
  344.5 3.6 in_grad.1
  349.1 10.5 %collective-permute-done.47 = bf16[1,784,128]{2,1,0:T(8,128)(2,1)S(1)} collective-permute-done((bf16[1,784,128]{2,1,0:T(8,128)(2,1)S(1)}, bf16[1,784,128]{2,1,0:T(8,128)(2,1)S(1)}, u32[]{:S(2)}, u32[]{:S(2)}) %collective-permute-start.47) | collective-permute-done | bytes 200736 | tf_op jit(solution)/shard_map/ppermute | solution.py:100
  363.9 2.5 reduce-scatter.2.cloned.1.call-done
  366.5 3.7 fusion.19
  (243 shorter events, 34.8 us)
Async XLA Ops:
  7.2 13.6 %copy-start = (f32[4,32]{1,0:T(4,128)S(1)}, f32[4,32]{1,0:T(4,128)}, u32[]{:S(2)}) copy-start(f32[4,32]{1,0:T(4,128)} %param.24) | copy-start | bytes 1540
  7.2 137.7 %all-gather.3.cloned.1.call-start = ((), (), s32[]{:S(2)}) async-start(), calls=%async_computation.2 | async-start | bytes 19464192 | tf_op jit(solution)/shard_map/all_gather | solution.py:882
  10.4 27.0 %copy-start.28 = (bf16[256,128]{1,0:T(8,128)(2,1)S(1)}, bf16[256,128]{1,0:T(8,128)(2,1)}, u32[]{:S(2)}) copy-start(bf16[256,128]{1,0:T(8,128)(2,1)} %param.23) | copy-start | bytes 196612
  10.5 356.0 %reduce-scatter.2.cloned.1.call-start = ((), (), s32[]{:S(2)}) async-start(), calls=%async_computation.1 | async-start | bytes 19464192 | tf_op jit(solution)/shard_map/reduce_scatter | solution.py:914
  11.4 30.1 %collective-permute-start = (bf16[256,1024]{1,0:T(8,128)(2,1)S(1)}, bf16[256,1024]{1,0:T(8,128)(2,1)S(1)}, u32[]{:S(2)}, u32[]{:S(2)}) collective-permute-start(bf16[256,1024]{1,0:T(8,128)(2,1)S(1)} %copy-done.7), channel_id=1, source_target_pairs={{0,1},{1,0},{2,3},{3,2},{4,5},{5,4},{6,7},{7,6},{8,9},{9,8},{10,11... | collective-permute-start | bytes 1572872 | tf_op jit(solution)/shard_map/ppermute | solution.py:66
  11.9 25.6 %collective-permute-start.1 = (bf16[256,1024]{1,0:T(8,128)(2,1)S(1)}, bf16[256,1024]{1,0:T(8,128)(2,1)S(1)}, u32[]{:S(2)}, u32[]{:S(2)}) collective-permute-start(bf16[256,1024]{1,0:T(8,128)(2,1)S(1)} %copy-done.7), channel_id=1, source_target_pairs={{0,2},{1,3},{2,0},{3,1},{4,6},{5,7},{6,4},{7,5},{8,10},{9,11},{10,... | collective-permute-start | bytes 1572872 | tf_op jit(solution)/shard_map/ppermute | solution.py:66
  14.5 27.0 %collective-permute-start.3 = (bf16[1,80,768]{2,1,0:T(8,128)(2,1)S(1)}, bf16[1,80,768]{2,1,0:T(8,128)(2,1)S(1)}, u32[]{:S(2)}, u32[]{:S(2)}) collective-permute-start(bf16[1,80,768]{2,1,0:T(8,128)(2,1)S(1)} %slice_bitcast_fusion), channel_id=1, source_target_pairs={{0,8},{4,12},{8,0},{12,4},{16,24},{20,28},{24,16},{28,20},{1,9},{5... | collective-permute-start | bytes 368648 | tf_op jit(solution)/shard_map/ppermute | solution.py:95
  15.4 6.3 %collective-permute-start.11 = (bf16[1,64,768]{2,1,0:T(8,128)(2,1)S(1)}, bf16[1,64,768]{2,1,0:T(8,128)(2,1)S(1)}, u32[]{:S(2)}, u32[]{:S(2)}) collective-permute-start(bf16[1,64,768]{2,1,0:T(8,128)(2,1)S(1)} %maximum_bitcast_fusion.1), channel_id=1, source_target_pairs={{0,16},{4,20},{8,24},{12,28},{16,0},{20,4},{24,8},{28,12},{1,17},{... | collective-permute-start | bytes 294920 | tf_op jit(solution)/shard_map/ppermute | solution.py:95
  21.7 35.0 %copy-start.13 = (bf16[256,1024]{1,0:T(8,128)(2,1)S(1)}, bf16[256,1024]{1,0:T(8,128)(2,1)}, u32[]{:S(2)}) copy-start(bf16[256,1024]{1,0:T(8,128)(2,1)} %refs_4_.3) | copy-start | bytes 1572868
  37.4 17.1 %copy-start.35 = (bf16[256,1024]{1,0:T(8,128)(2,1)}, bf16[256,1024]{1,0:T(8,128)(2,1)S(1)}, u32[]{:S(2)}) copy-start(bf16[256,1024]{1,0:T(8,128)(2,1)S(1)} %collective-permute-done.1.refs_2_) | copy-start | bytes 1572868
  37.4 6.6 %collective-permute-start.7 = (bf16[256,128]{1,0:T(8,128)(2,1)S(1)}, bf16[256,128]{1,0:T(8,128)(2,1)S(1)}, u32[]{:S(2)}, u32[]{:S(2)}) collective-permute-start(bf16[256,128]{1,0:T(8,128)(2,1)S(1)} %copy-done.28), channel_id=1, source_target_pairs={{0,3},{1,2},{2,1},{3,0},{4,7},{5,6},{6,5},{7,4},{8,11},{9,10},{10,... | collective-permute-start | bytes 196616 | tf_op jit(solution)/shard_map/ppermute | solution.py:66
  37.9 7.9 %collective-permute-start.6 = (bf16[256,128]{1,0:T(8,128)(2,1)S(1)}, bf16[256,128]{1,0:T(8,128)(2,1)S(1)}, u32[]{:S(2)}, u32[]{:S(2)}) collective-permute-start(bf16[256,128]{1,0:T(8,128)(2,1)S(1)} %copy-done.28), channel_id=1, source_target_pairs={{0,2},{1,3},{2,0},{3,1},{4,6},{5,7},{6,4},{7,5},{8,10},{9,11},{10,... | collective-permute-start | bytes 196616 | tf_op jit(solution)/shard_map/ppermute | solution.py:66
  41.4 5.9 %collective-permute-start.5 = (bf16[256,128]{1,0:T(8,128)(2,1)S(1)}, bf16[256,128]{1,0:T(8,128)(2,1)S(1)}, u32[]{:S(2)}, u32[]{:S(2)}) collective-permute-start(bf16[256,128]{1,0:T(8,128)(2,1)S(1)} %copy-done.28), channel_id=1, source_target_pairs={{0,1},{1,0},{2,3},{3,2},{4,5},{5,4},{6,7},{7,6},{8,9},{9,8},{10,11... | collective-permute-start | bytes 196616 | tf_op jit(solution)/shard_map/ppermute | solution.py:66
  41.5 17.7 %copy-start.34 = (bf16[256,1024]{1,0:T(8,128)(2,1)}, bf16[256,1024]{1,0:T(8,128)(2,1)S(1)}, u32[]{:S(2)}) copy-start(bf16[256,1024]{1,0:T(8,128)(2,1)S(1)} %collective-permute-done.refs_1_) | copy-start | bytes 1572868
  41.5 13.5 %collective-permute-start.2 = (bf16[256,1024]{1,0:T(8,128)(2,1)S(1)}, bf16[256,1024]{1,0:T(8,128)(2,1)S(1)}, u32[]{:S(2)}, u32[]{:S(2)}) collective-permute-start(bf16[256,1024]{1,0:T(8,128)(2,1)S(1)} %collective-permute-done.1.refs_2_), channel_id=1, source_target_pairs={{0,1},{1,0},{2,3},{3,2},{4,5},{5,4},{6,7},{7,6},{8,9},{9,8},{10,11... | collective-permute-start | bytes 1572872 | tf_op jit(solution)/shard_map/ppermute | solution.py:66
  43.5 11.0 %collective-permute-start.4 = (bf16[2,80,768]{2,1,0:T(8,128)(2,1)S(1)}, bf16[2,80,768]{2,1,0:T(8,128)(2,1)S(1)}, u32[]{:S(2)}, u32[]{:S(2)}) collective-permute-start(bf16[2,80,768]{2,1,0:T(8,128)(2,1)S(1)} %pad_maximum_fusion.5), channel_id=1, source_target_pairs={{0,16},{4,20},{8,24},{12,28},{16,0},{20,4},{24,8},{28,12},{1,17},{... | collective-permute-start | bytes 737288 | tf_op jit(solution)/shard_map/ppermute | solution.py:95
  44.0 10.4 %collective-permute-start.12 = (bf16[2,64,768]{2,1,0:T(8,128)(2,1)S(1)}, bf16[2,64,768]{2,1,0:T(8,128)(2,1)S(1)}, u32[]{:S(2)}, u32[]{:S(2)}) collective-permute-start(bf16[2,64,768]{2,1,0:T(8,128)(2,1)S(1)} %pad_maximum_fusion.6), channel_id=1, source_target_pairs={{0,8},{4,12},{8,0},{12,4},{16,24},{20,28},{24,16},{28,20},{1,9},{5... | collective-permute-start | bytes 589832 | tf_op jit(solution)/shard_map/ppermute | solution.py:95
  47.3 5.5 %collective-permute-start.8 = (bf16[1,4,128,128]{3,2,1,0:T(8,128)(2,1)S(1)}, bf16[1,4,128,128]{3,2,1,0:T(8,128)(2,1)S(1)}, u32[]{:S(2)}, u32[]{:S(2)}) collective-permute-start(bf16[1,4,128,128]{3,2,1,0:T(8,128)(2,1)S(1)} %get-tuple-element.103), channel_id=1, source_target_pairs={{0,8},{4,12},{8,0},{12,4},{16,24},{20,28},{24,16},{28,20},{1,9},{5... | collective-permute-start | bytes 393224 | tf_op jit(solution)/shard_map/ppermute | solution.py:95
  47.9 6.5 %collective-permute-start.9 = (bf16[1,4,128,128]{3,2,1,0:T(8,128)(2,1)S(1)}, bf16[1,4,128,128]{3,2,1,0:T(8,128)(2,1)S(1)}, u32[]{:S(2)}, u32[]{:S(2)}) collective-permute-start(bf16[1,4,128,128]{3,2,1,0:T(8,128)(2,1)S(1)} %get-tuple-element.104), channel_id=1, source_target_pairs={{0,16},{4,20},{8,24},{12,28},{16,0},{20,4},{24,8},{28,12},{1,17},{... | collective-permute-start | bytes 393224 | tf_op jit(solution)/shard_map/ppermute | solution.py:95
  55.0 4.3 %collective-permute-start.10 = (bf16[4,80,768]{2,1,0:T(8,128)(2,1)S(1)}, bf16[4,80,768]{2,1,0:T(8,128)(2,1)S(1)}, u32[]{:S(2)}, u32[]{:S(2)}) collective-permute-start(bf16[4,80,768]{2,1,0:T(8,128)(2,1)S(1)} %pad_maximum_fusion.3), channel_id=1, source_target_pairs={{0,4},{4,0},{8,12},{12,8},{16,20},{20,16},{24,28},{28,24},{1,5},{5... | collective-permute-start | bytes 1474568 | tf_op jit(solution)/shard_map/ppermute | solution.py:95
  55.0 4.2 %collective-permute-start.13 = (bf16[4,64,768]{2,1,0:T(8,128)(2,1)S(1)}, bf16[4,64,768]{2,1,0:T(8,128)(2,1)S(1)}, u32[]{:S(2)}, u32[]{:S(2)}) collective-permute-start(bf16[4,64,768]{2,1,0:T(8,128)(2,1)S(1)} %pad_maximum_fusion.4), channel_id=1, source_target_pairs={{0,4},{4,0},{8,12},{12,8},{16,20},{20,16},{24,28},{28,24},{1,5},{5... | collective-permute-start | bytes 1179656 | tf_op jit(solution)/shard_map/ppermute | solution.py:95
  56.6 26.9 %collective-permute-start.14 = (bf16[256,1024]{1,0:T(8,128)(2,1)S(1)}, bf16[256,1024]{1,0:T(8,128)(2,1)S(1)}, u32[]{:S(2)}, u32[]{:S(2)}) collective-permute-start(bf16[256,1024]{1,0:T(8,128)(2,1)S(1)} %copy-done.13), channel_id=1, source_target_pairs={{0,1},{1,0},{2,3},{3,2},{4,5},{5,4},{6,7},{7,6},{8,9},{9,8},{10,11... | collective-permute-start | bytes 1572872 | tf_op jit(solution)/shard_map/ppermute | solution.py:66
  57.7 25.9 %collective-permute-start.15 = (bf16[256,1024]{1,0:T(8,128)(2,1)S(1)}, bf16[256,1024]{1,0:T(8,128)(2,1)S(1)}, u32[]{:S(2)}, u32[]{:S(2)}) collective-permute-start(bf16[256,1024]{1,0:T(8,128)(2,1)S(1)} %copy-done.13), channel_id=1, source_target_pairs={{0,2},{1,3},{2,0},{3,1},{4,6},{5,7},{6,4},{7,5},{8,10},{9,11},{10,... | collective-permute-start | bytes 1572872 | tf_op jit(solution)/shard_map/ppermute | solution.py:66
  67.8 17.9 %collective-permute-start.20 = (bf16[2,4,128,128]{3,2,1,0:T(8,128)(2,1)S(1)}, bf16[2,4,128,128]{3,2,1,0:T(8,128)(2,1)S(1)}, u32[]{:S(2)}, u32[]{:S(2)}) collective-permute-start(bf16[2,4,128,128]{3,2,1,0:T(8,128)(2,1)S(1)} %constant_dynamic-update-slice_fusion.3), channel_id=1, source_target_pairs={{0,16},{4,20},{8,24},{12,28},{16,0},{20,4},{24,8},{28,12},{1,17},{... | collective-permute-start | bytes 786440 | tf_op jit(solution)/shard_map/ppermute | solution.py:95
  69.3 21.1 %collective-permute-start.22 = (bf16[2,4,128,128]{3,2,1,0:T(8,128)(2,1)S(1)}, bf16[2,4,128,128]{3,2,1,0:T(8,128)(2,1)S(1)}, u32[]{:S(2)}, u32[]{:S(2)}) collective-permute-start(bf16[2,4,128,128]{3,2,1,0:T(8,128)(2,1)S(1)} %constant_dynamic-update-slice_fusion.5), channel_id=1, source_target_pairs={{0,8},{4,12},{8,0},{12,4},{16,24},{20,28},{24,16},{28,20},{1,9},{5... | collective-permute-start | bytes 786440 | tf_op jit(solution)/shard_map/ppermute | solution.py:95
  83.6 19.1 %copy-start.38 = (bf16[256,1024]{1,0:T(8,128)(2,1)}, bf16[256,1024]{1,0:T(8,128)(2,1)S(1)}, u32[]{:S(2)}) copy-start(bf16[256,1024]{1,0:T(8,128)(2,1)S(1)} %collective-permute-done.15.refs_6_.refs_9_) | copy-start | bytes 1572868
  83.6 6.7 %collective-permute-start.17 = (bf16[256,256]{1,0:T(8,128)(2,1)}, bf16[256,256]{1,0:T(8,128)(2,1)S(1)}, u32[]{:S(2)}, u32[]{:S(2)}) collective-permute-start(bf16[256,256]{1,0:T(8,128)(2,1)} %get-tuple-element.117), channel_id=1, source_target_pairs={{0,1},{1,0},{2,3},{3,2},{4,5},{5,4},{6,7},{7,6},{8,9},{9,8},{10,11... | collective-permute-start | bytes 393224 | tf_op jit(solution)/shard_map/ppermute | solution.py:66
  85.3 17.3 %collective-permute-start.16 = (bf16[256,1024]{1,0:T(8,128)(2,1)S(1)}, bf16[256,1024]{1,0:T(8,128)(2,1)S(1)}, u32[]{:S(2)}, u32[]{:S(2)}) collective-permute-start(bf16[256,1024]{1,0:T(8,128)(2,1)S(1)} %collective-permute-done.15.refs_6_.refs_9_), channel_id=1, source_target_pairs={{0,1},{1,0},{2,3},{3,2},{4,5},{5,4},{6,7},{7,6},{8,9},{9,8},{10,11... | collective-permute-start | bytes 1572872 | tf_op jit(solution)/shard_map/ppermute | solution.py:66
  90.3 12.3 %collective-permute-start.21 = (bf16[4,4,128,128]{3,2,1,0:T(8,128)(2,1)S(1)}, bf16[4,4,128,128]{3,2,1,0:T(8,128)(2,1)S(1)}, u32[]{:S(2)}, u32[]{:S(2)}) collective-permute-start(bf16[4,4,128,128]{3,2,1,0:T(8,128)(2,1)S(1)} %pad_maximum_fusion.1), channel_id=1, source_target_pairs={{0,4},{4,0},{8,12},{12,8},{16,20},{20,16},{24,28},{28,24},{1,5},{5... | collective-permute-start | bytes 1572872 | tf_op jit(solution)/shard_map/ppermute | solution.py:95
  90.4 12.4 %collective-permute-start.23 = (bf16[4,4,128,128]{3,2,1,0:T(8,128)(2,1)S(1)}, bf16[4,4,128,128]{3,2,1,0:T(8,128)(2,1)S(1)}, u32[]{:S(2)}, u32[]{:S(2)}) collective-permute-start(bf16[4,4,128,128]{3,2,1,0:T(8,128)(2,1)S(1)} %pad_maximum_fusion.2), channel_id=1, source_target_pairs={{0,4},{4,0},{8,12},{12,8},{16,20},{20,16},{24,28},{28,24},{1,5},{5... | collective-permute-start | bytes 1572872 | tf_op jit(solution)/shard_map/ppermute | solution.py:95
  91.0 13.0 %collective-permute-start.18 = (bf16[256,256]{1,0:T(8,128)(2,1)}, bf16[256,256]{1,0:T(8,128)(2,1)S(1)}, u32[]{:S(2)}, u32[]{:S(2)}) collective-permute-start(bf16[256,256]{1,0:T(8,128)(2,1)} %get-tuple-element.119), channel_id=1, source_target_pairs={{0,2},{1,3},{2,0},{3,1},{4,6},{5,7},{6,4},{7,5},{8,10},{9,11},{10,... | collective-permute-start | bytes 393224 | tf_op jit(solution)/shard_map/ppermute | solution.py:66
  92.3 13.9 %collective-permute-start.19 = (bf16[256,256]{1,0:T(8,128)(2,1)}, bf16[256,256]{1,0:T(8,128)(2,1)S(1)}, u32[]{:S(2)}, u32[]{:S(2)}) collective-permute-start(bf16[256,256]{1,0:T(8,128)(2,1)} %get-tuple-element.121), channel_id=1, source_target_pairs={{0,3},{1,2},{2,1},{3,0},{4,7},{5,6},{6,5},{7,4},{8,11},{9,10},{10,... | collective-permute-start | bytes 393224 | tf_op jit(solution)/shard_map/ppermute | solution.py:66
  110.7 20.7 %collective-permute-start.24 = (bf16[256,1024]{1,0:T(8,128)(2,1)}, bf16[256,1024]{1,0:T(8,128)(2,1)S(1)}, u32[]{:S(2)}, u32[]{:S(2)}) collective-permute-start(bf16[256,1024]{1,0:T(8,128)(2,1)} %get-tuple-element.129.refs_0_.refs_3_), channel_id=1, source_target_pairs={{0,1},{1,0},{2,3},{3,2},{4,5},{5,4},{6,7},{7,6},{8,9},{9,8},{10,11... | collective-permute-start | bytes 1572872 | tf_op jit(solution)/shard_map/ppermute | solution.py:66
  111.3 22.0 %collective-permute-start.25 = (bf16[256,1024]{1,0:T(8,128)(2,1)}, bf16[256,1024]{1,0:T(8,128)(2,1)S(1)}, u32[]{:S(2)}, u32[]{:S(2)}) collective-permute-start(bf16[256,1024]{1,0:T(8,128)(2,1)} %get-tuple-element.129.refs_0_.refs_3_), channel_id=1, source_target_pairs={{0,2},{1,3},{2,0},{3,1},{4,6},{5,7},{6,4},{7,5},{8,10},{9,11},{10,... | collective-permute-start | bytes 1572872 | tf_op jit(solution)/shard_map/ppermute | solution.py:66
  131.4 13.5 %copy-start.41 = (bf16[256,1024]{1,0:T(8,128)(2,1)}, bf16[256,1024]{1,0:T(8,128)(2,1)S(1)}, u32[]{:S(2)}) copy-start(bf16[256,1024]{1,0:T(8,128)(2,1)S(1)} %collective-permute-done.24.refs_1_.refs_4_) | copy-start | bytes 1572868
  133.3 11.6 %collective-permute-start.26 = (bf16[256,1024]{1,0:T(8,128)(2,1)S(1)}, bf16[256,1024]{1,0:T(8,128)(2,1)S(1)}, u32[]{:S(2)}, u32[]{:S(2)}) collective-permute-start(bf16[256,1024]{1,0:T(8,128)(2,1)S(1)} %collective-permute-done.25.refs_2_.refs_5_), channel_id=1, source_target_pairs={{0,1},{1,0},{2,3},{3,2},{4,5},{5,4},{6,7},{7,6},{8,9},{9,8},{10,11... | collective-permute-start | bytes 1572872 | tf_op jit(solution)/shard_map/ppermute | solution.py:66
  197.4 12.6 %copy-start.11 = (bf16[256,1024]{1,0:T(8,128)(2,1)S(1)}, bf16[256,1024]{1,0:T(8,128)(2,1)}, u32[]{:S(2)}) copy-start(bf16[256,1024]{1,0:T(8,128)(2,1)} %get-tuple-element.142) | copy-start | bytes 1572868
  197.4 13.4 %copy-start.44 = (bf16[256,1024]{1,0:T(8,128)(2,1)S(1)}, bf16[256,1024]{1,0:T(8,128)(2,1)}, u32[]{:S(2)}) copy-start(bf16[256,1024]{1,0:T(8,128)(2,1)} %get-tuple-element.150) | copy-start | bytes 1572868
  197.4 12.5 %collective-permute-start.27 = (bf16[256,1024]{1,0:T(8,128)(2,1)}, bf16[256,1024]{1,0:T(8,128)(2,1)S(1)}, u32[]{:S(2)}, u32[]{:S(2)}) collective-permute-start(bf16[256,1024]{1,0:T(8,128)(2,1)} %get-tuple-element.143), channel_id=1, source_target_pairs={{0,1},{1,0},{2,3},{3,2},{4,5},{5,4},{6,7},{7,6},{8,9},{9,8},{10,11... | collective-permute-start | bytes 1572872 | tf_op jit(solution)/shard_map/ppermute | solution.py:66
  210.2 27.4 %collective-permute-start.28 = (bf16[256,1024]{1,0:T(8,128)(2,1)S(1)}, bf16[256,1024]{1,0:T(8,128)(2,1)S(1)}, u32[]{:S(2)}, u32[]{:S(2)}) collective-permute-start(bf16[256,1024]{1,0:T(8,128)(2,1)S(1)} %add_convert_fusion.6), channel_id=1, source_target_pairs={{0,2},{1,3},{2,0},{3,1},{4,6},{5,7},{6,4},{7,5},{8,10},{9,11},{10,... | collective-permute-start | bytes 1572872 | tf_op jit(solution)/shard_map/ppermute | solution.py:66
  210.8 26.8 %collective-permute-start.32 = (bf16[256,1024]{1,0:T(8,128)(2,1)S(1)}, bf16[256,1024]{1,0:T(8,128)(2,1)S(1)}, u32[]{:S(2)}, u32[]{:S(2)}) collective-permute-start(bf16[256,1024]{1,0:T(8,128)(2,1)S(1)} %copy-done.44), channel_id=1, source_target_pairs={{0,1},{1,0},{2,3},{3,2},{4,5},{5,4},{6,7},{7,6},{8,9},{9,8},{10,11... | collective-permute-start | bytes 1572872 | tf_op jit(solution)/shard_map/ppermute | solution.py:66
  238.9 13.7 %collective-permute-start.29 = (bf16[256,1024]{1,0:T(8,128)(2,1)S(1)}, bf16[256,1024]{1,0:T(8,128)(2,1)S(1)}, u32[]{:S(2)}, u32[]{:S(2)}) collective-permute-start(bf16[256,1024]{1,0:T(8,128)(2,1)S(1)} %copy-done.40), channel_id=1, source_target_pairs={{0,1},{1,0},{2,3},{3,2},{4,5},{5,4},{6,7},{7,6},{8,9},{9,8},{10,11... | collective-permute-start | bytes 1572872 | tf_op jit(solution)/shard_map/ppermute | solution.py:66
  244.5 9.5 %collective-permute-start.33 = (bf16[256,256]{1,0:T(8,128)(2,1)}, bf16[256,256]{1,0:T(8,128)(2,1)S(1)}, u32[]{:S(2)}, u32[]{:S(2)}) collective-permute-start(bf16[256,256]{1,0:T(8,128)(2,1)} %get-tuple-element.155), channel_id=1, source_target_pairs={{0,1},{1,0},{2,3},{3,2},{4,5},{5,4},{6,7},{7,6},{8,9},{9,8},{10,11... | collective-permute-start | bytes 393224 | tf_op jit(solution)/shard_map/ppermute | solution.py:66
  246.3 9.7 %collective-permute-start.34 = (bf16[256,256]{1,0:T(8,128)(2,1)}, bf16[256,256]{1,0:T(8,128)(2,1)S(1)}, u32[]{:S(2)}, u32[]{:S(2)}) collective-permute-start(bf16[256,256]{1,0:T(8,128)(2,1)} %get-tuple-element.156), channel_id=1, source_target_pairs={{0,2},{1,3},{2,0},{3,1},{4,6},{5,7},{6,4},{7,5},{8,10},{9,11},{10,... | collective-permute-start | bytes 393224 | tf_op jit(solution)/shard_map/ppermute | solution.py:66
  247.0 9.0 %collective-permute-start.35 = (bf16[256,256]{1,0:T(8,128)(2,1)}, bf16[256,256]{1,0:T(8,128)(2,1)S(1)}, u32[]{:S(2)}, u32[]{:S(2)}) collective-permute-start(bf16[256,256]{1,0:T(8,128)(2,1)} %get-tuple-element.157), channel_id=1, source_target_pairs={{0,3},{1,2},{2,1},{3,0},{4,7},{5,6},{6,5},{7,4},{8,11},{9,10},{10,... | collective-permute-start | bytes 393224 | tf_op jit(solution)/shard_map/ppermute | solution.py:66
  256.0 3.2 collective-permute-start.36
  256.1 26.0 %collective-permute-start.31 = (bf16[256,1024]{1,0:T(8,128)(2,1)}, bf16[256,1024]{1,0:T(8,128)(2,1)}, u32[]{:S(2)}, u32[]{:S(2)}) collective-permute-start(bf16[256,1024]{1,0:T(8,128)(2,1)} %add_convert_fusion.5), channel_id=1, source_target_pairs={{0,2},{1,3},{2,0},{3,1},{4,6},{5,7},{6,4},{7,5},{8,10},{9,11},{10,... | collective-permute-start | bytes 1572872 | tf_op jit(solution)/shard_map/ppermute | solution.py:66
  259.2 23.8 %collective-permute-start.30 = (bf16[256,1024]{1,0:T(8,128)(2,1)}, bf16[256,1024]{1,0:T(8,128)(2,1)}, u32[]{:S(2)}, u32[]{:S(2)}) collective-permute-start(bf16[256,1024]{1,0:T(8,128)(2,1)} %get-tuple-element.146), channel_id=1, source_target_pairs={{0,1},{1,0},{2,3},{3,2},{4,5},{5,4},{6,7},{7,6},{8,9},{9,8},{10,11... | collective-permute-start | bytes 1572872 | tf_op jit(solution)/shard_map/ppermute | solution.py:66
  261.3 16.8 %collective-permute-start.37 = (bf16[2,1024,128]{2,1,0:T(8,128)(2,1)}, bf16[2,1024,128]{2,1,0:T(8,128)(2,1)}, u32[]{:S(2)}, u32[]{:S(2)}) collective-permute-start(bf16[2,1024,128]{2,1,0:T(8,128)(2,1)} %slice.171), channel_id=1, source_target_pairs={{0,8},{4,12},{8,0},{12,4},{16,24},{20,28},{24,16},{28,20},{1,9},{5... | collective-permute-start | bytes 1572872 | tf_op jit(solution)/shard_map/ppermute | solution.py:100
  263.2 14.9 %copy-start.5 = (bf16[4,1024,128]{2,1,0:T(8,128)(2,1)S(1)}, bf16[4,1024,128]{2,1,0:T(8,128)(2,1)}, u32[]{:S(2)}) copy-start(bf16[4,1024,128]{2,1,0:T(8,128)(2,1)} %copy-done.4) | copy-start | bytes 3145732
  283.0 15.0 %collective-permute-start.39 = (bf16[1,1024,128]{2,1,0:T(8,128)(2,1)S(1)}, bf16[1,1024,128]{2,1,0:T(8,128)(2,1)S(1)}, u32[]{:S(2)}, u32[]{:S(2)}) collective-permute-start(bf16[1,1024,128]{2,1,0:T(8,128)(2,1)S(1)} %slice.173), channel_id=1, source_target_pairs={{0,16},{4,20},{8,24},{12,28},{16,0},{20,4},{24,8},{28,12},{1,17},{... | collective-permute-start | bytes 786440 | tf_op jit(solution)/shard_map/ppermute | solution.py:100
  291.0 22.5 %collective-permute-start.38 = (bf16[256,1024]{1,0:T(8,128)(2,1)}, bf16[256,1024]{1,0:T(8,128)(2,1)S(1)}, u32[]{:S(2)}, u32[]{:S(2)}) collective-permute-start(bf16[256,1024]{1,0:T(8,128)(2,1)} %get-tuple-element.174), channel_id=1, source_target_pairs={{0,1},{1,0},{2,3},{3,2},{4,5},{5,4},{6,7},{7,6},{8,9},{9,8},{10,11... | collective-permute-start | bytes 1572872 | tf_op jit(solution)/shard_map/ppermute | solution.py:66
  294.6 11.6 %collective-permute-start.40 = (f32[8,1024]{1,0:T(8,128)}, f32[8,1024]{1,0:T(8,128)S(1)}, u32[]{:S(2)}, u32[]{:S(2)}) collective-permute-start(f32[8,1024]{1,0:T(8,128)} %get-tuple-element.177.refs_0_), channel_id=1, source_target_pairs={{0,1},{1,0},{2,3},{3,2},{4,5},{5,4},{6,7},{7,6},{8,9},{9,8},{10,11... | collective-permute-start | bytes 98312 | tf_op jit(solution)/shard_map/ppermute | solution.py:66
  294.6 12.5 %collective-permute-start.41 = (f32[8,1024]{1,0:T(8,128)}, f32[8,1024]{1,0:T(8,128)S(1)}, u32[]{:S(2)}, u32[]{:S(2)}) collective-permute-start(f32[8,1024]{1,0:T(8,128)} %get-tuple-element.177.refs_0_), channel_id=1, source_target_pairs={{0,2},{1,3},{2,0},{3,1},{4,6},{5,7},{6,4},{7,5},{8,10},{9,11},{10,... | collective-permute-start | bytes 98312 | tf_op jit(solution)/shard_map/ppermute | solution.py:66
  296.8 10.3 %collective-permute-start.42 = (f32[8,1024]{1,0:T(8,128)}, f32[8,1024]{1,0:T(8,128)S(1)}, u32[]{:S(2)}, u32[]{:S(2)}) collective-permute-start(f32[8,1024]{1,0:T(8,128)} %get-tuple-element.177.refs_0_), channel_id=1, source_target_pairs={{0,3},{1,2},{2,1},{3,0},{4,7},{5,6},{6,5},{7,4},{8,11},{9,10},{10,... | collective-permute-start | bytes 98312 | tf_op jit(solution)/shard_map/ppermute | solution.py:66
  298.1 15.4 %copy-start.10 = (bf16[256,1024]{1,0:T(8,128)(2,1)S(1)}, bf16[256,1024]{1,0:T(8,128)(2,1)}, u32[]{:S(2)}) copy-start(bf16[256,1024]{1,0:T(8,128)(2,1)} %get-tuple-element.173) | copy-start | bytes 1572868
  313.8 2.6 collective-permute-start.45
  313.8 29.9 %collective-permute-start.44 = (bf16[256,1024]{1,0:T(8,128)(2,1)S(1)}, bf16[256,1024]{1,0:T(8,128)(2,1)S(1)}, u32[]{:S(2)}, u32[]{:S(2)}) collective-permute-start(bf16[256,1024]{1,0:T(8,128)(2,1)S(1)} %add_convert_fusion.2), channel_id=1, source_target_pairs={{0,2},{1,3},{2,0},{3,1},{4,6},{5,7},{6,4},{7,5},{8,10},{9,11},{10,... | collective-permute-start | bytes 1572872 | tf_op jit(solution)/shard_map/ppermute | solution.py:66
  315.6 24.1 %collective-permute-start.43 = (bf16[256,1024]{1,0:T(8,128)(2,1)}, bf16[256,1024]{1,0:T(8,128)(2,1)S(1)}, u32[]{:S(2)}, u32[]{:S(2)}) collective-permute-start(bf16[256,1024]{1,0:T(8,128)(2,1)} %get-tuple-element.180), channel_id=1, source_target_pairs={{0,1},{1,0},{2,3},{3,2},{4,5},{5,4},{6,7},{7,6},{8,9},{9,8},{10,11... | collective-permute-start | bytes 1572872 | tf_op jit(solution)/shard_map/ppermute | solution.py:66
  317.8 30.4 %collective-permute-start.46 = (bf16[2,784,128]{2,1,0:T(8,128)(2,1)S(1)}, bf16[2,784,128]{2,1,0:T(8,128)(2,1)S(1)}, u32[]{:S(2)}, u32[]{:S(2)}) collective-permute-start(bf16[2,784,128]{2,1,0:T(8,128)(2,1)S(1)} %slice.175), channel_id=1, source_target_pairs={{0,8},{4,12},{8,0},{12,4},{16,24},{20,28},{24,16},{28,20},{1,9},{5... | collective-permute-start | bytes 1204232 | tf_op jit(solution)/shard_map/ppermute | solution.py:100
  339.7 8.6 %collective-permute-start.50 = (bf16[256,128]{1,0:T(8,128)(2,1)S(1)}, bf16[256,128]{1,0:T(8,128)(2,1)S(1)}, u32[]{:S(2)}, u32[]{:S(2)}) collective-permute-start(bf16[256,128]{1,0:T(8,128)(2,1)S(1)} %get-tuple-element.196), channel_id=1, source_target_pairs={{0,3},{1,2},{2,1},{3,0},{4,7},{5,6},{6,5},{7,4},{8,11},{9,10},{10,... | collective-permute-start | bytes 196616 | tf_op jit(solution)/shard_map/ppermute | solution.py:66
  341.0 7.3 %collective-permute-start.49 = (bf16[256,128]{1,0:T(8,128)(2,1)S(1)}, bf16[256,128]{1,0:T(8,128)(2,1)S(1)}, u32[]{:S(2)}, u32[]{:S(2)}) collective-permute-start(bf16[256,128]{1,0:T(8,128)(2,1)S(1)} %get-tuple-element.197), channel_id=1, source_target_pairs={{0,2},{1,3},{2,0},{3,1},{4,6},{5,7},{6,4},{7,5},{8,10},{9,11},{10,... | collective-permute-start | bytes 196616 | tf_op jit(solution)/shard_map/ppermute | solution.py:66
  342.3 6.0 %collective-permute-start.48 = (bf16[256,128]{1,0:T(8,128)(2,1)S(1)}, bf16[256,128]{1,0:T(8,128)(2,1)S(1)}, u32[]{:S(2)}, u32[]{:S(2)}) collective-permute-start(bf16[256,128]{1,0:T(8,128)(2,1)S(1)} %get-tuple-element.195), channel_id=1, source_target_pairs={{0,1},{1,0},{2,3},{3,2},{4,5},{5,4},{6,7},{7,6},{8,9},{9,8},{10,11... | collective-permute-start | bytes 196616 | tf_op jit(solution)/shard_map/ppermute | solution.py:66
  348.3 11.3 %collective-permute-start.47 = (bf16[1,784,128]{2,1,0:T(8,128)(2,1)S(1)}, bf16[1,784,128]{2,1,0:T(8,128)(2,1)S(1)}, u32[]{:S(2)}, u32[]{:S(2)}) collective-permute-start(bf16[1,784,128]{2,1,0:T(8,128)(2,1)S(1)} %slice.144), channel_id=1, source_target_pairs={{0,16},{4,20},{8,24},{12,28},{16,0},{20,4},{24,8},{28,12},{1,17},{... | collective-permute-start | bytes 602120 | tf_op jit(solution)/shard_map/ppermute | solution.py:100
  (40 other events, 183.9 us)
Sparse Core Ops, SparseCore 0:
  10.6 102.8 all-gather.2
  237.7 128.6 reduce-scatter.1

commit v5 on v4

--- a/solution.py
+++ b/solution.py
@@ -934,7 +934,7 @@
         BLOCK * np.arange(total // BLOCK + 1)[:, None] - (BLOCK * (total // BLOCK - 2) + 1) - np.arange(2 * BLOCK)[None, :]
     )
     table = jnp.einsum("hbt,btk->hk", diag, jnp.asarray(onehot_of(diag_at)), precision=PRECISE)
-    n1_passed = z_swap(proj[3], 1, z_size)
+    n1_passed = z_swap(after(proj[3], out_far), 1, z_size)
     if direct:
         table_rows = jnp.pad(table.reshape(1, -1), ((0, 7), (0, 0)))
         smalls = z_direct([proj[z_size]] * z_size, z_size)

time: 381 us -> 381 us (level)
  no operation moved by 1% of the time
where the time goes in v5:
time: 381 us; the launch traced here: 377 us
  Pallas kernels  150 us (39%)
  waiting for transfers between devices  118 us (31%)
  starting transfers between devices  56.9 us (15%)
  local copies, waits for them, and re-layouts  19.9 us (5%)
  other arithmetic  16.9 us (4%)
  between operations  14.9 us (4%)
    ppermute x33, waiting for transfers between devices, z_swap(): return lax.ppermute(x, 'tensor', [(i, i ^ mask) for i in range(size)])  99 us
    ppermute x33, starting transfers between devices, z_swap(): return lax.ppermute(x, 'tensor', [(i, i ^ mask) for i in range(size)])  44.3 us
    pallas_call x1, Pallas kernels, units_call(): pl.pallas_call(functools.partial(units_body, chunks, unit), grid=(ff // B...  32 us
    pallas_call x2, Pallas kernels, product_call(): pl.pallas_call(functools.partial(product_body, len(xs), chunks, bool(extr...  30.2 us
    pallas_call x1, Pallas kernels, wgrad_call(): pl.pallas_call(functools.partial(wgrad_body, count, chunks), grid=(ff //...  25 us
    pallas_call x1, Pallas kernels, attn_bwd(): pl.pallas_call(functools.partial(bwd_body, total, chunks), grid=(heads,),...  14.9 us
    pallas_call x1, Pallas kernels, attn_fwd(): pl.pallas_call(functools.partial(fwd_body, total, chunks), grid=(heads,),...  13.7 us
    unnamed x114, local copies, waits for them, and re-layouts  10.8 us
  transfers between devices with their start and end apart: 53, of which 24 were waited for; matrix products, arithmetic and copies ran while one was open for 6% of the time, Pallas kernels for 26%

profile of v5, /device:TPU:14, one launch (start us, length us, event | category | flops | bytes accessed | tf_op | source)
XLA Modules:
  0.0 377.0 jit_solution(4166266536863421377)
XLA Ops:
  7.2 3.1 pad_maximum_fusion
  11.9 2.6 collective-permute-start.1
  16.0 2.3 reduce-window.6
  19.1 1.6 fusion.2.refs_8_
  21.7 15.8 %collective-permute-done.1.refs_2_ = bf16[256,1024]{1,0:T(8,128)(2,1)S(1)} collective-permute-done((bf16[256,1024]{1,0:T(8,128)(2,1)S(1)}, bf16[256,1024]{1,0:T(8,128)(2,1)S(1)}, u32[]{:S(2)}, u32[]{:S(2)}) %collective-permute-start.1) | collective-permute-done | bytes 524320 | tf_op jit(solution)/shard_map/ppermute | solution.py:66
  37.9 3.5 collective-permute-start.6
  41.5 2.0 collective-permute-start.2
  44.6 1.2 collective-permute-done.6
  45.7 1.5 collective-permute-done.5
  48.5 4.3 %collective-permute-done.8 = bf16[1,4,128,128]{3,2,1,0:T(8,128)(2,1)S(1)} collective-permute-done((bf16[1,4,128,128]{3,2,1,0:T(8,128)(2,1)S(1)}, bf16[1,4,128,128]{3,2,1,0:T(8,128)(2,1)S(1)}, u32[]{:S(2)}, u32[]{:S(2)}) %collective-permute-start.8) | collective-permute-done | bytes 131104 | tf_op jit(solution)/shard_map/ppermute | solution.py:95
  52.9 1.5 collective-permute-done.9
  56.6 1.1 collective-permute-start.14
  57.7 1.4 collective-permute-start.15
  61.2 6.6 %norm_qkv.1 = (bf16[1024,1024]{1,0:T(8,128)(2,1)}, bf16[1024,256]{1,0:T(8,128)(2,1)}, bf16[1024,256]{1,0:T(8,128)(2,1)}, bf16[1024,256]{1,0:T(8,128)(2,1)}, bf16...) custom-call(s32[16]{0:T(128)} %pad_add_fusion.index_ref, ...), custom_call_target="tpu_custom_call" | custom-call | flops 1610612736 | bytes 8388608 | tf_op jit(solution)/shard_map/norm_qkv/pallas_call | solution.py:168
  67.8 1.5 collective-permute-start.20
  69.9 13.7 %attn_forward.1 = (bf16[4,1024,1024]{2,1,0:T(8,128)(2,1)}, f32[256,1024]{1,0:T(8,128)}, bf16[256,256]{1,0:T(8,128)(2,1)}, bf16[256,256]{1,0:T(8,128)(2,1)}, bf16...) custom-call(s32[1,2]{1,0:T(1,128)} %starts_ref.1, s32[4]{0:T(128)} %iota_xor_fusion.place_ref, ...), custom_call_target="tpu_custom_call" | custom-call | flops 4294967296 | bytes 10485760 | tf_op jit(solution)/shard_map/attn_forward/pallas_call | solution.py:261
  83.6 1.7 collective-permute-start.17
  85.8 4.6 %collective-permute-done.17.refs_1_ = bf16[256,256]{1,0:T(8,128)(2,1)S(1)} collective-permute-done((bf16[256,256]{1,0:T(8,128)(2,1)}, bf16[256,256]{1,0:T(8,128)(2,1)S(1)}, u32[]{:S(2)}, u32[]{:S(2)}) %collective-permute-start.17) | collective-permute-done | bytes 131104 | tf_op jit(solution)/shard_map/ppermute | solution.py:66
  91.0 1.3 collective-permute-start.18
  92.3 1.8 collective-permute-start.19
  94.1 8.5 %collective-permute-done.16.refs_7_.refs_10_ = bf16[256,1024]{1,0:T(8,128)(2,1)S(1)} collective-permute-done((bf16[256,1024]{1,0:T(8,128)(2,1)S(1)}, bf16[256,1024]{1,0:T(8,128)(2,1)S(1)}, u32[]{:S(2)}, u32[]{:S(2)}) %collective-permute-start.16) | collective-permute-done | bytes 524320 | tf_op jit(solution)/shard_map/ppermute | solution.py:66
  102.9 1.1 collective-permute-done.18.refs_2_
  104.0 2.2 collective-permute-done.19.refs_3_
  106.9 3.8 %out_projection_norm.1 = (f32[256,1024]{1,0:T(8,128)}, bf16[256,1024]{1,0:T(8,128)(2,1)}) custom-call(s32[16]{0:T(128)} %pad_add_fusion.index_ref, bf16[256,256]{1,0:T(8,128)(2,1)} %get-tuple-element.116.refs_0_, bf16[256,256]{1,0:T(8,128)(2,1)} %copy-done.22, bf16[256,256]{1,0:T(8,128)(2,1)} %copy-done.23, bf16[256,256]{1,0:T(8,128)(2,1)} %copy-done.24, ...), custom_call_target="tpu_custom_call" | custom-call | flops 536870912 | bytes 4194304 | tf_op jit(solution)/shard_map/out_projection_norm/pallas_call | solution.py:427
  112.1 19.3 %collective-permute-done.24.refs_1_.refs_4_ = bf16[256,1024]{1,0:T(8,128)(2,1)S(1)} collective-permute-done((bf16[256,1024]{1,0:T(8,128)(2,1)}, bf16[256,1024]{1,0:T(8,128)(2,1)S(1)}, u32[]{:S(2)}, u32[]{:S(2)}) %collective-permute-start.24) | collective-permute-done | bytes 524320 | tf_op jit(solution)/shard_map/ppermute | solution.py:66
  131.4 1.9 collective-permute-done.25.refs_2_.refs_5_
  133.3 2.4 collective-permute-start.26
  135.7 9.2 %collective-permute-done.26.refs_3_.refs_6_ = bf16[256,1024]{1,0:T(8,128)(2,1)S(1)} collective-permute-done((bf16[256,1024]{1,0:T(8,128)(2,1)S(1)}, bf16[256,1024]{1,0:T(8,128)(2,1)S(1)}, u32[]{:S(2)}, u32[]{:S(2)}) %collective-permute-start.26) | collective-permute-done | bytes 524320 | tf_op jit(solution)/shard_map/ppermute | solution.py:66
  145.7 32.0 %expert_units.1 = (bf16[1024,2816]{1,0:T(8,128)(2,1)}, bf16[1024,2816]{1,0:T(8,128)(2,1)}, bf16[1024,2816]{1,0:T(8,128)(2,1)}, f32[1024,128]{1,0:T(8,128)}, f32[8,1024]{1,0:T(8,128)}) custom-call(s32[4]{0:T(128)} %iota_xor_fusion.place_ref, bf16[256,1024]{1,0:T(8,128)(2,1)} %get-tuple-element.130.refs_0_.refs_3_, bf16[256,1024]{1,0:T(8,128)(2,1)} %copy-done.41, ...), custom_call_target="tpu_custom_call" | custom-call | flops 17716740096 | bytes 29884416 | tf_op jit(solution)/shard_map/expert_units/pallas_call | solution.py:530
  177.7 19.7 %normed_two_grads.1 = (bf16[256,1024]{1,0:T(8,128)(2,1)}, bf16[256,1024]{1,0:T(8,128)(2,1)}, bf16[256,1024]{1,0:T(8,128)(2,1)}, bf16[256,1024]{1,0:T(8,128)(2,1)}) custom-call(bf16[1024,2816]{1,0:T(8,128)(2,1)} %get-tuple-element.134.refs_0_.refs_1_, bf16[1024,2816]{1,0:T(8,128)(2,1)} %get-tuple-element.135.refs_1_.refs_2_, ...), custom_call_target="tpu_custom_call" | custom-call | flops 11811160064 | bytes 23068672 | tf_op jit(solution)/shard_map/normed_two_grads/pallas_call | solution.py:580
  197.4 2.1 collective-permute-start.27
  199.5 10.5 %expert_out.1 = (bf16[256,1024]{1,0:T(8,128)(2,1)}, bf16[256,1024]{1,0:T(8,128)(2,1)}, bf16[256,1024]{1,0:T(8,128)(2,1)}, bf16[256,1024]{1,0:T(8,128)(2,1)}) custom-call(bf16[1024,2816]{1,0:T(8,128)(2,1)} %get-tuple-element.148.refs_0_, bf16[8,3,2816,128]{3,2,1,0:T(8,128)(2,1)} %bitcast.81), custom_call_target="tpu_custom_call" | custom-call | flops 5905580032 | bytes 11534336 | tf_op jit(solution)/shard_map/expert_out/pallas_call | solution.py:580
  210.8 1.7 collective-permute-start.32
  212.6 25.0 %expert_weight_grads.1 = bf16[8,3,2816,128]{3,2,1,0:T(8,128)(2,1)} custom-call(bf16[1024,2816]{1,0:T(8,128)(2,1)} %get-tuple-element.148.refs_0_, bf16[1024,2816]{1,0:T(8,128)(2,1)} %get-tuple-element.134.refs_0_.refs_1_, bf16[1024,2816]{1,0:T(8,128)(2,1)} %get-tuple-element.135.refs_1_.refs_2_, bf16[256,1024]{1,0:T(8,128)(2,1)} %get-tuple-element.130.refs_0_.refs_3_, ...), custom_call_target="tpu_custom_call" | custom-call | flops 17716740096 | bytes 34603008 | tf_op jit(solution)/shard_map/expert_weight_grads/pallas_call | solution.py:620
  239.7 4.8 %resid_grad.1 = (f32[256,1024]{1,0:T(8,128)}, bf16[256,1024]{1,0:T(8,128)(2,1)}, f32[8,1024]{1,0:T(8,128)}, bf16[256,256]{1,0:T(8,128)(2,1)}, bf16[256,256]{1,0:...) custom-call(s32[16]{0:T(128)} %pad_add_fusion.index_ref, ...), custom_call_target="tpu_custom_call" | custom-call | flops 536870912 | bytes 4194304 | tf_op jit(solution)/shard_map/resid_grad/pallas_call | solution.py:661
  244.5 1.8 collective-permute-start.33
  247.0 1.1 collective-permute-start.35
  248.0 3.9 %w_output_grad.1 = (bf16[4,1024,128]{2,1,0:T(8,128)(2,1)}, bf16[4,1024,128]{2,1,0:T(8,128)(2,1)}) custom-call(s32[8]{0:T(128)} %fusion.17.slot_ref, bf16[256,256]{1,0:T(8,128)(2,1)} %get-tuple-element.116.refs_0_, bf16[256,256]{1,0:T(8,128)(2,1)} %copy-done.22, bf16[256,256]{1,0:T(8,128)(2,1)} %copy-done.23, bf16[256,256]{1,0:T(8,128)(2,1)} %copy-done.24, ...), custom_call_target="tpu_custom_call" | custom-call | flops 536870912 | bytes 4194304 | tf_op jit(solution)/shard_map/w_output_grad/pallas_call | solution.py:783
  252.6 1.0 add_convert_fusion.5
  254.0 1.9 collective-permute-done.34.refs_2_
  256.1 3.1 collective-permute-start.31
  261.3 1.8 collective-permute-start.37
  263.2 14.9 %attn_backward.1 = (bf16[1024,256]{1,0:T(8,128)(2,1)}, bf16[1024,256]{1,0:T(8,128)(2,1)}, bf16[1024,256]{1,0:T(8,128)(2,1)}, f32[4,5,512]{2,1,0:T(8,128)}) custom-call(s32[4]{0:T(128)} %iota_xor_fusion.place_ref, bf16[256,256]{1,0:T(8,128)(2,1)} %get-tuple-element.155.refs_0_, bf16[256,256]{1,0:T(8,128)(2,1)} %copy-done.45, bf16[256,256]{1,0:T(8,128)(2,1)} %copy-done.46, ...), custom_call_target="tpu_custom_call" | custom-call | flops 171798691840 | bytes 10485760 | tf_op jit(solution)/shard_map/attn_backward/pallas_call | solution.py:382
  278.1 1.2 add_convert_fusion.3
  279.4 2.7 collective-permute-done.31
  283.0 2.0 collective-permute-start.39
  285.1 5.9 %projection_grads.1 = (bf16[256,1024]{1,0:T(8,128)(2,1)}, bf16[256,1024]{1,0:T(8,128)(2,1)}, bf16[256,1024]{1,0:T(8,128)(2,1)}, bf16[256,1024]{1,0:T(8,128)(2,1)}, f32[8,1024]{1,0:T(8,128)}) custom-call(s32[16]{0:T(128)} %pad_add_fusion.index_ref, s32[4]{0:T(128)} %iota_xor_fusion.place_ref, bf16[1024,256]{1,0:T(8,128)(2,1)} %get-tuple-element.167.dq_ref, ...), custom_call_target="tpu_custom_call" | custom-call | flops 1610612736 | bytes 8388608 | tf_op jit(solution)/shard_map/projection_grads/pallas_call | solution.py:720
  291.0 2.5 collective-permute-start.38
  294.6 2.2 collective-permute-start.41
  296.8 1.3 collective-permute-start.42
  298.1 8.0 %collective-permute-done.40.refs_1_ = f32[8,1024]{1,0:T(8,128)S(1)} collective-permute-done((f32[8,1024]{1,0:T(8,128)}, f32[8,1024]{1,0:T(8,128)S(1)}, u32[]{:S(2)}, u32[]{:S(2)}) %collective-permute-start.40) | collective-permute-done | bytes 32800 | tf_op jit(solution)/shard_map/ppermute | solution.py:66
  308.3 5.3 %attn_weight_grads.1 = (bf16[4,784,128]{2,1,0:T(8,128)(2,1)}, bf16[4,784,128]{2,1,0:T(8,128)(2,1)}) custom-call(s32[8]{0:T(128)} %fusion.17.slot_ref, bf16[1024,1024]{1,0:T(8,128)(2,1)} %get-tuple-element.123.n1_ref, bf16[1024,256]{1,0:T(8,128)(2,1)} %get-tuple-element.167.dq_ref, bf16[1024,256]{1,0:T(8,128)(2,1)} %get-tuple-element.168.dk_ref, ...), custom_call_target="tpu_custom_call" | custom-call | flops 1610612736 | bytes 8388608 | tf_op jit(solution)/shard_map/attn_weight_grads/pallas_call | solution.py:756
  313.8 1.8 collective-permute-start.44
  316.3 1.4 add_convert_fusion.1
  317.8 2.0 collective-permute-start.46
  319.8 2.3 add_convert_fusion.4
  322.1 17.6 %collective-permute-done.43.refs_1_ = bf16[256,1024]{1,0:T(8,128)(2,1)S(1)} collective-permute-done((bf16[256,1024]{1,0:T(8,128)(2,1)}, bf16[256,1024]{1,0:T(8,128)(2,1)S(1)}, u32[]{:S(2)}, u32[]{:S(2)}) %collective-permute-start.43) | collective-permute-done | bytes 524320 | tf_op jit(solution)/shard_map/ppermute | solution.py:66
  339.7 1.3 collective-permute-start.50
  341.0 1.3 collective-permute-start.49
  342.3 1.4 collective-permute-start.48
  344.5 3.6 in_grad.1
  349.1 10.5 %collective-permute-done.47 = bf16[1,784,128]{2,1,0:T(8,128)(2,1)S(1)} collective-permute-done((bf16[1,784,128]{2,1,0:T(8,128)(2,1)S(1)}, bf16[1,784,128]{2,1,0:T(8,128)(2,1)S(1)}, u32[]{:S(2)}, u32[]{:S(2)}) %collective-permute-start.47) | collective-permute-done | bytes 200736 | tf_op jit(solution)/shard_map/ppermute | solution.py:100
  363.9 2.5 reduce-scatter.2.cloned.1.call-done
  366.5 3.7 fusion.19
  (243 shorter events, 34.8 us)
Async XLA Ops:
  7.2 13.6 %copy-start = (f32[4,32]{1,0:T(4,128)S(1)}, f32[4,32]{1,0:T(4,128)}, u32[]{:S(2)}) copy-start(f32[4,32]{1,0:T(4,128)} %param.24) | copy-start | bytes 1540
  7.2 137.7 %all-gather.3.cloned.1.call-start = ((), (), s32[]{:S(2)}) async-start(), calls=%async_computation.2 | async-start | bytes 19464192 | tf_op jit(solution)/shard_map/all_gather | solution.py:882
  10.4 27.0 %copy-start.28 = (bf16[256,128]{1,0:T(8,128)(2,1)S(1)}, bf16[256,128]{1,0:T(8,128)(2,1)}, u32[]{:S(2)}) copy-start(bf16[256,128]{1,0:T(8,128)(2,1)} %param.23) | copy-start | bytes 196612
  10.5 356.0 %reduce-scatter.2.cloned.1.call-start = ((), (), s32[]{:S(2)}) async-start(), calls=%async_computation.1 | async-start | bytes 19464192 | tf_op jit(solution)/shard_map/reduce_scatter | solution.py:914
  11.4 30.1 %collective-permute-start = (bf16[256,1024]{1,0:T(8,128)(2,1)S(1)}, bf16[256,1024]{1,0:T(8,128)(2,1)S(1)}, u32[]{:S(2)}, u32[]{:S(2)}) collective-permute-start(bf16[256,1024]{1,0:T(8,128)(2,1)S(1)} %copy-done.7), channel_id=1, source_target_pairs={{0,1},{1,0},{2,3},{3,2},{4,5},{5,4},{6,7},{7,6},{8,9},{9,8},{10,11... | collective-permute-start | bytes 1572872 | tf_op jit(solution)/shard_map/ppermute | solution.py:66
  11.9 25.6 %collective-permute-start.1 = (bf16[256,1024]{1,0:T(8,128)(2,1)S(1)}, bf16[256,1024]{1,0:T(8,128)(2,1)S(1)}, u32[]{:S(2)}, u32[]{:S(2)}) collective-permute-start(bf16[256,1024]{1,0:T(8,128)(2,1)S(1)} %copy-done.7), channel_id=1, source_target_pairs={{0,2},{1,3},{2,0},{3,1},{4,6},{5,7},{6,4},{7,5},{8,10},{9,11},{10,... | collective-permute-start | bytes 1572872 | tf_op jit(solution)/shard_map/ppermute | solution.py:66
  14.5 27.0 %collective-permute-start.3 = (bf16[1,80,768]{2,1,0:T(8,128)(2,1)S(1)}, bf16[1,80,768]{2,1,0:T(8,128)(2,1)S(1)}, u32[]{:S(2)}, u32[]{:S(2)}) collective-permute-start(bf16[1,80,768]{2,1,0:T(8,128)(2,1)S(1)} %slice_bitcast_fusion), channel_id=1, source_target_pairs={{0,8},{4,12},{8,0},{12,4},{16,24},{20,28},{24,16},{28,20},{1,9},{5... | collective-permute-start | bytes 368648 | tf_op jit(solution)/shard_map/ppermute | solution.py:95
  15.4 6.3 %collective-permute-start.11 = (bf16[1,64,768]{2,1,0:T(8,128)(2,1)S(1)}, bf16[1,64,768]{2,1,0:T(8,128)(2,1)S(1)}, u32[]{:S(2)}, u32[]{:S(2)}) collective-permute-start(bf16[1,64,768]{2,1,0:T(8,128)(2,1)S(1)} %maximum_bitcast_fusion.1), channel_id=1, source_target_pairs={{0,16},{4,20},{8,24},{12,28},{16,0},{20,4},{24,8},{28,12},{1,17},{... | collective-permute-start | bytes 294920 | tf_op jit(solution)/shard_map/ppermute | solution.py:95
  21.7 35.0 %copy-start.13 = (bf16[256,1024]{1,0:T(8,128)(2,1)S(1)}, bf16[256,1024]{1,0:T(8,128)(2,1)}, u32[]{:S(2)}) copy-start(bf16[256,1024]{1,0:T(8,128)(2,1)} %refs_4_.3) | copy-start | bytes 1572868
  37.4 17.1 %copy-start.35 = (bf16[256,1024]{1,0:T(8,128)(2,1)}, bf16[256,1024]{1,0:T(8,128)(2,1)S(1)}, u32[]{:S(2)}) copy-start(bf16[256,1024]{1,0:T(8,128)(2,1)S(1)} %collective-permute-done.1.refs_2_) | copy-start | bytes 1572868
  37.4 6.6 %collective-permute-start.7 = (bf16[256,128]{1,0:T(8,128)(2,1)S(1)}, bf16[256,128]{1,0:T(8,128)(2,1)S(1)}, u32[]{:S(2)}, u32[]{:S(2)}) collective-permute-start(bf16[256,128]{1,0:T(8,128)(2,1)S(1)} %copy-done.28), channel_id=1, source_target_pairs={{0,3},{1,2},{2,1},{3,0},{4,7},{5,6},{6,5},{7,4},{8,11},{9,10},{10,... | collective-permute-start | bytes 196616 | tf_op jit(solution)/shard_map/ppermute | solution.py:66
  37.9 7.9 %collective-permute-start.6 = (bf16[256,128]{1,0:T(8,128)(2,1)S(1)}, bf16[256,128]{1,0:T(8,128)(2,1)S(1)}, u32[]{:S(2)}, u32[]{:S(2)}) collective-permute-start(bf16[256,128]{1,0:T(8,128)(2,1)S(1)} %copy-done.28), channel_id=1, source_target_pairs={{0,2},{1,3},{2,0},{3,1},{4,6},{5,7},{6,4},{7,5},{8,10},{9,11},{10,... | collective-permute-start | bytes 196616 | tf_op jit(solution)/shard_map/ppermute | solution.py:66
  41.4 5.9 %collective-permute-start.5 = (bf16[256,128]{1,0:T(8,128)(2,1)S(1)}, bf16[256,128]{1,0:T(8,128)(2,1)S(1)}, u32[]{:S(2)}, u32[]{:S(2)}) collective-permute-start(bf16[256,128]{1,0:T(8,128)(2,1)S(1)} %copy-done.28), channel_id=1, source_target_pairs={{0,1},{1,0},{2,3},{3,2},{4,5},{5,4},{6,7},{7,6},{8,9},{9,8},{10,11... | collective-permute-start | bytes 196616 | tf_op jit(solution)/shard_map/ppermute | solution.py:66
  41.5 17.7 %copy-start.34 = (bf16[256,1024]{1,0:T(8,128)(2,1)}, bf16[256,1024]{1,0:T(8,128)(2,1)S(1)}, u32[]{:S(2)}) copy-start(bf16[256,1024]{1,0:T(8,128)(2,1)S(1)} %collective-permute-done.refs_1_) | copy-start | bytes 1572868
  41.5 13.5 %collective-permute-start.2 = (bf16[256,1024]{1,0:T(8,128)(2,1)S(1)}, bf16[256,1024]{1,0:T(8,128)(2,1)S(1)}, u32[]{:S(2)}, u32[]{:S(2)}) collective-permute-start(bf16[256,1024]{1,0:T(8,128)(2,1)S(1)} %collective-permute-done.1.refs_2_), channel_id=1, source_target_pairs={{0,1},{1,0},{2,3},{3,2},{4,5},{5,4},{6,7},{7,6},{8,9},{9,8},{10,11... | collective-permute-start | bytes 1572872 | tf_op jit(solution)/shard_map/ppermute | solution.py:66
  43.5 11.0 %collective-permute-start.4 = (bf16[2,80,768]{2,1,0:T(8,128)(2,1)S(1)}, bf16[2,80,768]{2,1,0:T(8,128)(2,1)S(1)}, u32[]{:S(2)}, u32[]{:S(2)}) collective-permute-start(bf16[2,80,768]{2,1,0:T(8,128)(2,1)S(1)} %pad_maximum_fusion.5), channel_id=1, source_target_pairs={{0,16},{4,20},{8,24},{12,28},{16,0},{20,4},{24,8},{28,12},{1,17},{... | collective-permute-start | bytes 737288 | tf_op jit(solution)/shard_map/ppermute | solution.py:95
  44.0 10.4 %collective-permute-start.12 = (bf16[2,64,768]{2,1,0:T(8,128)(2,1)S(1)}, bf16[2,64,768]{2,1,0:T(8,128)(2,1)S(1)}, u32[]{:S(2)}, u32[]{:S(2)}) collective-permute-start(bf16[2,64,768]{2,1,0:T(8,128)(2,1)S(1)} %pad_maximum_fusion.6), channel_id=1, source_target_pairs={{0,8},{4,12},{8,0},{12,4},{16,24},{20,28},{24,16},{28,20},{1,9},{5... | collective-permute-start | bytes 589832 | tf_op jit(solution)/shard_map/ppermute | solution.py:95
  47.3 5.5 %collective-permute-start.8 = (bf16[1,4,128,128]{3,2,1,0:T(8,128)(2,1)S(1)}, bf16[1,4,128,128]{3,2,1,0:T(8,128)(2,1)S(1)}, u32[]{:S(2)}, u32[]{:S(2)}) collective-permute-start(bf16[1,4,128,128]{3,2,1,0:T(8,128)(2,1)S(1)} %get-tuple-element.104), channel_id=1, source_target_pairs={{0,8},{4,12},{8,0},{12,4},{16,24},{20,28},{24,16},{28,20},{1,9},{5... | collective-permute-start | bytes 393224 | tf_op jit(solution)/shard_map/ppermute | solution.py:95
  47.9 6.5 %collective-permute-start.9 = (bf16[1,4,128,128]{3,2,1,0:T(8,128)(2,1)S(1)}, bf16[1,4,128,128]{3,2,1,0:T(8,128)(2,1)S(1)}, u32[]{:S(2)}, u32[]{:S(2)}) collective-permute-start(bf16[1,4,128,128]{3,2,1,0:T(8,128)(2,1)S(1)} %get-tuple-element.105), channel_id=1, source_target_pairs={{0,16},{4,20},{8,24},{12,28},{16,0},{20,4},{24,8},{28,12},{1,17},{... | collective-permute-start | bytes 393224 | tf_op jit(solution)/shard_map/ppermute | solution.py:95
  55.0 4.3 %collective-permute-start.10 = (bf16[4,80,768]{2,1,0:T(8,128)(2,1)S(1)}, bf16[4,80,768]{2,1,0:T(8,128)(2,1)S(1)}, u32[]{:S(2)}, u32[]{:S(2)}) collective-permute-start(bf16[4,80,768]{2,1,0:T(8,128)(2,1)S(1)} %pad_maximum_fusion.3), channel_id=1, source_target_pairs={{0,4},{4,0},{8,12},{12,8},{16,20},{20,16},{24,28},{28,24},{1,5},{5... | collective-permute-start | bytes 1474568 | tf_op jit(solution)/shard_map/ppermute | solution.py:95
  55.0 4.2 %collective-permute-start.13 = (bf16[4,64,768]{2,1,0:T(8,128)(2,1)S(1)}, bf16[4,64,768]{2,1,0:T(8,128)(2,1)S(1)}, u32[]{:S(2)}, u32[]{:S(2)}) collective-permute-start(bf16[4,64,768]{2,1,0:T(8,128)(2,1)S(1)} %pad_maximum_fusion.4), channel_id=1, source_target_pairs={{0,4},{4,0},{8,12},{12,8},{16,20},{20,16},{24,28},{28,24},{1,5},{5... | collective-permute-start | bytes 1179656 | tf_op jit(solution)/shard_map/ppermute | solution.py:95
  56.6 26.9 %collective-permute-start.14 = (bf16[256,1024]{1,0:T(8,128)(2,1)S(1)}, bf16[256,1024]{1,0:T(8,128)(2,1)S(1)}, u32[]{:S(2)}, u32[]{:S(2)}) collective-permute-start(bf16[256,1024]{1,0:T(8,128)(2,1)S(1)} %copy-done.13), channel_id=1, source_target_pairs={{0,1},{1,0},{2,3},{3,2},{4,5},{5,4},{6,7},{7,6},{8,9},{9,8},{10,11... | collective-permute-start | bytes 1572872 | tf_op jit(solution)/shard_map/ppermute | solution.py:66
  57.7 25.9 %collective-permute-start.15 = (bf16[256,1024]{1,0:T(8,128)(2,1)S(1)}, bf16[256,1024]{1,0:T(8,128)(2,1)S(1)}, u32[]{:S(2)}, u32[]{:S(2)}) collective-permute-start(bf16[256,1024]{1,0:T(8,128)(2,1)S(1)} %copy-done.13), channel_id=1, source_target_pairs={{0,2},{1,3},{2,0},{3,1},{4,6},{5,7},{6,4},{7,5},{8,10},{9,11},{10,... | collective-permute-start | bytes 1572872 | tf_op jit(solution)/shard_map/ppermute | solution.py:66
  67.8 17.9 %collective-permute-start.20 = (bf16[2,4,128,128]{3,2,1,0:T(8,128)(2,1)S(1)}, bf16[2,4,128,128]{3,2,1,0:T(8,128)(2,1)S(1)}, u32[]{:S(2)}, u32[]{:S(2)}) collective-permute-start(bf16[2,4,128,128]{3,2,1,0:T(8,128)(2,1)S(1)} %constant_dynamic-update-slice_fusion.3), channel_id=1, source_target_pairs={{0,16},{4,20},{8,24},{12,28},{16,0},{20,4},{24,8},{28,12},{1,17},{... | collective-permute-start | bytes 786440 | tf_op jit(solution)/shard_map/ppermute | solution.py:95
  69.3 21.1 %collective-permute-start.22 = (bf16[2,4,128,128]{3,2,1,0:T(8,128)(2,1)S(1)}, bf16[2,4,128,128]{3,2,1,0:T(8,128)(2,1)S(1)}, u32[]{:S(2)}, u32[]{:S(2)}) collective-permute-start(bf16[2,4,128,128]{3,2,1,0:T(8,128)(2,1)S(1)} %constant_dynamic-update-slice_fusion.5), channel_id=1, source_target_pairs={{0,8},{4,12},{8,0},{12,4},{16,24},{20,28},{24,16},{28,20},{1,9},{5... | collective-permute-start | bytes 786440 | tf_op jit(solution)/shard_map/ppermute | solution.py:95
  83.6 19.1 %copy-start.38 = (bf16[256,1024]{1,0:T(8,128)(2,1)}, bf16[256,1024]{1,0:T(8,128)(2,1)S(1)}, u32[]{:S(2)}) copy-start(bf16[256,1024]{1,0:T(8,128)(2,1)S(1)} %collective-permute-done.15.refs_6_.refs_9_) | copy-start | bytes 1572868
  83.6 6.7 %collective-permute-start.17 = (bf16[256,256]{1,0:T(8,128)(2,1)}, bf16[256,256]{1,0:T(8,128)(2,1)S(1)}, u32[]{:S(2)}, u32[]{:S(2)}) collective-permute-start(bf16[256,256]{1,0:T(8,128)(2,1)} %get-tuple-element.118), channel_id=1, source_target_pairs={{0,1},{1,0},{2,3},{3,2},{4,5},{5,4},{6,7},{7,6},{8,9},{9,8},{10,11... | collective-permute-start | bytes 393224 | tf_op jit(solution)/shard_map/ppermute | solution.py:66
  85.3 17.3 %collective-permute-start.16 = (bf16[256,1024]{1,0:T(8,128)(2,1)S(1)}, bf16[256,1024]{1,0:T(8,128)(2,1)S(1)}, u32[]{:S(2)}, u32[]{:S(2)}) collective-permute-start(bf16[256,1024]{1,0:T(8,128)(2,1)S(1)} %collective-permute-done.15.refs_6_.refs_9_), channel_id=1, source_target_pairs={{0,1},{1,0},{2,3},{3,2},{4,5},{5,4},{6,7},{7,6},{8,9},{9,8},{10,11... | collective-permute-start | bytes 1572872 | tf_op jit(solution)/shard_map/ppermute | solution.py:66
  90.3 12.3 %collective-permute-start.21 = (bf16[4,4,128,128]{3,2,1,0:T(8,128)(2,1)S(1)}, bf16[4,4,128,128]{3,2,1,0:T(8,128)(2,1)S(1)}, u32[]{:S(2)}, u32[]{:S(2)}) collective-permute-start(bf16[4,4,128,128]{3,2,1,0:T(8,128)(2,1)S(1)} %pad_maximum_fusion.1), channel_id=1, source_target_pairs={{0,4},{4,0},{8,12},{12,8},{16,20},{20,16},{24,28},{28,24},{1,5},{5... | collective-permute-start | bytes 1572872 | tf_op jit(solution)/shard_map/ppermute | solution.py:95
  90.4 12.4 %collective-permute-start.23 = (bf16[4,4,128,128]{3,2,1,0:T(8,128)(2,1)S(1)}, bf16[4,4,128,128]{3,2,1,0:T(8,128)(2,1)S(1)}, u32[]{:S(2)}, u32[]{:S(2)}) collective-permute-start(bf16[4,4,128,128]{3,2,1,0:T(8,128)(2,1)S(1)} %pad_maximum_fusion.2), channel_id=1, source_target_pairs={{0,4},{4,0},{8,12},{12,8},{16,20},{20,16},{24,28},{28,24},{1,5},{5... | collective-permute-start | bytes 1572872 | tf_op jit(solution)/shard_map/ppermute | solution.py:95
  91.0 13.0 %collective-permute-start.18 = (bf16[256,256]{1,0:T(8,128)(2,1)}, bf16[256,256]{1,0:T(8,128)(2,1)S(1)}, u32[]{:S(2)}, u32[]{:S(2)}) collective-permute-start(bf16[256,256]{1,0:T(8,128)(2,1)} %get-tuple-element.120), channel_id=1, source_target_pairs={{0,2},{1,3},{2,0},{3,1},{4,6},{5,7},{6,4},{7,5},{8,10},{9,11},{10,... | collective-permute-start | bytes 393224 | tf_op jit(solution)/shard_map/ppermute | solution.py:66
  92.3 13.9 %collective-permute-start.19 = (bf16[256,256]{1,0:T(8,128)(2,1)}, bf16[256,256]{1,0:T(8,128)(2,1)S(1)}, u32[]{:S(2)}, u32[]{:S(2)}) collective-permute-start(bf16[256,256]{1,0:T(8,128)(2,1)} %get-tuple-element.122), channel_id=1, source_target_pairs={{0,3},{1,2},{2,1},{3,0},{4,7},{5,6},{6,5},{7,4},{8,11},{9,10},{10,... | collective-permute-start | bytes 393224 | tf_op jit(solution)/shard_map/ppermute | solution.py:66
  110.7 20.7 %collective-permute-start.24 = (bf16[256,1024]{1,0:T(8,128)(2,1)}, bf16[256,1024]{1,0:T(8,128)(2,1)S(1)}, u32[]{:S(2)}, u32[]{:S(2)}) collective-permute-start(bf16[256,1024]{1,0:T(8,128)(2,1)} %get-tuple-element.130.refs_0_.refs_3_), channel_id=1, source_target_pairs={{0,1},{1,0},{2,3},{3,2},{4,5},{5,4},{6,7},{7,6},{8,9},{9,8},{10,11... | collective-permute-start | bytes 1572872 | tf_op jit(solution)/shard_map/ppermute | solution.py:66
  111.3 22.0 %collective-permute-start.25 = (bf16[256,1024]{1,0:T(8,128)(2,1)}, bf16[256,1024]{1,0:T(8,128)(2,1)S(1)}, u32[]{:S(2)}, u32[]{:S(2)}) collective-permute-start(bf16[256,1024]{1,0:T(8,128)(2,1)} %get-tuple-element.130.refs_0_.refs_3_), channel_id=1, source_target_pairs={{0,2},{1,3},{2,0},{3,1},{4,6},{5,7},{6,4},{7,5},{8,10},{9,11},{10,... | collective-permute-start | bytes 1572872 | tf_op jit(solution)/shard_map/ppermute | solution.py:66
  131.4 13.5 %copy-start.41 = (bf16[256,1024]{1,0:T(8,128)(2,1)}, bf16[256,1024]{1,0:T(8,128)(2,1)S(1)}, u32[]{:S(2)}) copy-start(bf16[256,1024]{1,0:T(8,128)(2,1)S(1)} %collective-permute-done.24.refs_1_.refs_4_) | copy-start | bytes 1572868
  133.3 11.6 %collective-permute-start.26 = (bf16[256,1024]{1,0:T(8,128)(2,1)S(1)}, bf16[256,1024]{1,0:T(8,128)(2,1)S(1)}, u32[]{:S(2)}, u32[]{:S(2)}) collective-permute-start(bf16[256,1024]{1,0:T(8,128)(2,1)S(1)} %collective-permute-done.25.refs_2_.refs_5_), channel_id=1, source_target_pairs={{0,1},{1,0},{2,3},{3,2},{4,5},{5,4},{6,7},{7,6},{8,9},{9,8},{10,11... | collective-permute-start | bytes 1572872 | tf_op jit(solution)/shard_map/ppermute | solution.py:66
  197.4 12.6 %copy-start.11 = (bf16[256,1024]{1,0:T(8,128)(2,1)S(1)}, bf16[256,1024]{1,0:T(8,128)(2,1)}, u32[]{:S(2)}) copy-start(bf16[256,1024]{1,0:T(8,128)(2,1)} %get-tuple-element.143) | copy-start | bytes 1572868
  197.4 13.4 %copy-start.44 = (bf16[256,1024]{1,0:T(8,128)(2,1)S(1)}, bf16[256,1024]{1,0:T(8,128)(2,1)}, u32[]{:S(2)}) copy-start(bf16[256,1024]{1,0:T(8,128)(2,1)} %get-tuple-element.151) | copy-start | bytes 1572868
  197.4 12.5 %collective-permute-start.27 = (bf16[256,1024]{1,0:T(8,128)(2,1)}, bf16[256,1024]{1,0:T(8,128)(2,1)S(1)}, u32[]{:S(2)}, u32[]{:S(2)}) collective-permute-start(bf16[256,1024]{1,0:T(8,128)(2,1)} %get-tuple-element.144), channel_id=1, source_target_pairs={{0,1},{1,0},{2,3},{3,2},{4,5},{5,4},{6,7},{7,6},{8,9},{9,8},{10,11... | collective-permute-start | bytes 1572872 | tf_op jit(solution)/shard_map/ppermute | solution.py:66
  210.2 27.4 %collective-permute-start.28 = (bf16[256,1024]{1,0:T(8,128)(2,1)S(1)}, bf16[256,1024]{1,0:T(8,128)(2,1)S(1)}, u32[]{:S(2)}, u32[]{:S(2)}) collective-permute-start(bf16[256,1024]{1,0:T(8,128)(2,1)S(1)} %add_convert_fusion.6), channel_id=1, source_target_pairs={{0,2},{1,3},{2,0},{3,1},{4,6},{5,7},{6,4},{7,5},{8,10},{9,11},{10,... | collective-permute-start | bytes 1572872 | tf_op jit(solution)/shard_map/ppermute | solution.py:66
  210.8 26.8 %collective-permute-start.32 = (bf16[256,1024]{1,0:T(8,128)(2,1)S(1)}, bf16[256,1024]{1,0:T(8,128)(2,1)S(1)}, u32[]{:S(2)}, u32[]{:S(2)}) collective-permute-start(bf16[256,1024]{1,0:T(8,128)(2,1)S(1)} %copy-done.44), channel_id=1, source_target_pairs={{0,1},{1,0},{2,3},{3,2},{4,5},{5,4},{6,7},{7,6},{8,9},{9,8},{10,11... | collective-permute-start | bytes 1572872 | tf_op jit(solution)/shard_map/ppermute | solution.py:66
  238.9 13.7 %collective-permute-start.29 = (bf16[256,1024]{1,0:T(8,128)(2,1)S(1)}, bf16[256,1024]{1,0:T(8,128)(2,1)S(1)}, u32[]{:S(2)}, u32[]{:S(2)}) collective-permute-start(bf16[256,1024]{1,0:T(8,128)(2,1)S(1)} %copy-done.40), channel_id=1, source_target_pairs={{0,1},{1,0},{2,3},{3,2},{4,5},{5,4},{6,7},{7,6},{8,9},{9,8},{10,11... | collective-permute-start | bytes 1572872 | tf_op jit(solution)/shard_map/ppermute | solution.py:66
  244.5 9.5 %collective-permute-start.33 = (bf16[256,256]{1,0:T(8,128)(2,1)}, bf16[256,256]{1,0:T(8,128)(2,1)S(1)}, u32[]{:S(2)}, u32[]{:S(2)}) collective-permute-start(bf16[256,256]{1,0:T(8,128)(2,1)} %get-tuple-element.156), channel_id=1, source_target_pairs={{0,1},{1,0},{2,3},{3,2},{4,5},{5,4},{6,7},{7,6},{8,9},{9,8},{10,11... | collective-permute-start | bytes 393224 | tf_op jit(solution)/shard_map/ppermute | solution.py:66
  246.3 9.7 %collective-permute-start.34 = (bf16[256,256]{1,0:T(8,128)(2,1)}, bf16[256,256]{1,0:T(8,128)(2,1)S(1)}, u32[]{:S(2)}, u32[]{:S(2)}) collective-permute-start(bf16[256,256]{1,0:T(8,128)(2,1)} %get-tuple-element.157), channel_id=1, source_target_pairs={{0,2},{1,3},{2,0},{3,1},{4,6},{5,7},{6,4},{7,5},{8,10},{9,11},{10,... | collective-permute-start | bytes 393224 | tf_op jit(solution)/shard_map/ppermute | solution.py:66
  247.0 9.0 %collective-permute-start.35 = (bf16[256,256]{1,0:T(8,128)(2,1)}, bf16[256,256]{1,0:T(8,128)(2,1)S(1)}, u32[]{:S(2)}, u32[]{:S(2)}) collective-permute-start(bf16[256,256]{1,0:T(8,128)(2,1)} %get-tuple-element.158), channel_id=1, source_target_pairs={{0,3},{1,2},{2,1},{3,0},{4,7},{5,6},{6,5},{7,4},{8,11},{9,10},{10,... | collective-permute-start | bytes 393224 | tf_op jit(solution)/shard_map/ppermute | solution.py:66
  256.0 3.2 collective-permute-start.36
  256.1 26.0 %collective-permute-start.31 = (bf16[256,1024]{1,0:T(8,128)(2,1)}, bf16[256,1024]{1,0:T(8,128)(2,1)}, u32[]{:S(2)}, u32[]{:S(2)}) collective-permute-start(bf16[256,1024]{1,0:T(8,128)(2,1)} %add_convert_fusion.5), channel_id=1, source_target_pairs={{0,2},{1,3},{2,0},{3,1},{4,6},{5,7},{6,4},{7,5},{8,10},{9,11},{10,... | collective-permute-start | bytes 1572872 | tf_op jit(solution)/shard_map/ppermute | solution.py:66
  259.2 23.8 %collective-permute-start.30 = (bf16[256,1024]{1,0:T(8,128)(2,1)}, bf16[256,1024]{1,0:T(8,128)(2,1)}, u32[]{:S(2)}, u32[]{:S(2)}) collective-permute-start(bf16[256,1024]{1,0:T(8,128)(2,1)} %get-tuple-element.147), channel_id=1, source_target_pairs={{0,1},{1,0},{2,3},{3,2},{4,5},{5,4},{6,7},{7,6},{8,9},{9,8},{10,11... | collective-permute-start | bytes 1572872 | tf_op jit(solution)/shard_map/ppermute | solution.py:66
  261.3 16.8 %collective-permute-start.37 = (bf16[2,1024,128]{2,1,0:T(8,128)(2,1)}, bf16[2,1024,128]{2,1,0:T(8,128)(2,1)}, u32[]{:S(2)}, u32[]{:S(2)}) collective-permute-start(bf16[2,1024,128]{2,1,0:T(8,128)(2,1)} %slice.171), channel_id=1, source_target_pairs={{0,8},{4,12},{8,0},{12,4},{16,24},{20,28},{24,16},{28,20},{1,9},{5... | collective-permute-start | bytes 1572872 | tf_op jit(solution)/shard_map/ppermute | solution.py:100
  263.2 14.9 %copy-start.5 = (bf16[4,1024,128]{2,1,0:T(8,128)(2,1)S(1)}, bf16[4,1024,128]{2,1,0:T(8,128)(2,1)}, u32[]{:S(2)}) copy-start(bf16[4,1024,128]{2,1,0:T(8,128)(2,1)} %copy-done.4) | copy-start | bytes 3145732
  283.0 15.0 %collective-permute-start.39 = (bf16[1,1024,128]{2,1,0:T(8,128)(2,1)S(1)}, bf16[1,1024,128]{2,1,0:T(8,128)(2,1)S(1)}, u32[]{:S(2)}, u32[]{:S(2)}) collective-permute-start(bf16[1,1024,128]{2,1,0:T(8,128)(2,1)S(1)} %slice.173), channel_id=1, source_target_pairs={{0,16},{4,20},{8,24},{12,28},{16,0},{20,4},{24,8},{28,12},{1,17},{... | collective-permute-start | bytes 786440 | tf_op jit(solution)/shard_map/ppermute | solution.py:100
  291.0 22.5 %collective-permute-start.38 = (bf16[256,1024]{1,0:T(8,128)(2,1)}, bf16[256,1024]{1,0:T(8,128)(2,1)S(1)}, u32[]{:S(2)}, u32[]{:S(2)}) collective-permute-start(bf16[256,1024]{1,0:T(8,128)(2,1)} %get-tuple-element.176), channel_id=1, source_target_pairs={{0,1},{1,0},{2,3},{3,2},{4,5},{5,4},{6,7},{7,6},{8,9},{9,8},{10,11... | collective-permute-start | bytes 1572872 | tf_op jit(solution)/shard_map/ppermute | solution.py:66
  294.6 11.6 %collective-permute-start.40 = (f32[8,1024]{1,0:T(8,128)}, f32[8,1024]{1,0:T(8,128)S(1)}, u32[]{:S(2)}, u32[]{:S(2)}) collective-permute-start(f32[8,1024]{1,0:T(8,128)} %get-tuple-element.179.refs_0_), channel_id=1, source_target_pairs={{0,1},{1,0},{2,3},{3,2},{4,5},{5,4},{6,7},{7,6},{8,9},{9,8},{10,11... | collective-permute-start | bytes 98312 | tf_op jit(solution)/shard_map/ppermute | solution.py:66
  294.6 12.5 %collective-permute-start.41 = (f32[8,1024]{1,0:T(8,128)}, f32[8,1024]{1,0:T(8,128)S(1)}, u32[]{:S(2)}, u32[]{:S(2)}) collective-permute-start(f32[8,1024]{1,0:T(8,128)} %get-tuple-element.179.refs_0_), channel_id=1, source_target_pairs={{0,2},{1,3},{2,0},{3,1},{4,6},{5,7},{6,4},{7,5},{8,10},{9,11},{10,... | collective-permute-start | bytes 98312 | tf_op jit(solution)/shard_map/ppermute | solution.py:66
  296.8 10.3 %collective-permute-start.42 = (f32[8,1024]{1,0:T(8,128)}, f32[8,1024]{1,0:T(8,128)S(1)}, u32[]{:S(2)}, u32[]{:S(2)}) collective-permute-start(f32[8,1024]{1,0:T(8,128)} %get-tuple-element.179.refs_0_), channel_id=1, source_target_pairs={{0,3},{1,2},{2,1},{3,0},{4,7},{5,6},{6,5},{7,4},{8,11},{9,10},{10,... | collective-permute-start | bytes 98312 | tf_op jit(solution)/shard_map/ppermute | solution.py:66
  298.1 15.4 %copy-start.10 = (bf16[256,1024]{1,0:T(8,128)(2,1)S(1)}, bf16[256,1024]{1,0:T(8,128)(2,1)}, u32[]{:S(2)}) copy-start(bf16[256,1024]{1,0:T(8,128)(2,1)} %get-tuple-element.174) | copy-start | bytes 1572868
  313.8 2.6 collective-permute-start.45
  313.8 29.9 %collective-permute-start.44 = (bf16[256,1024]{1,0:T(8,128)(2,1)S(1)}, bf16[256,1024]{1,0:T(8,128)(2,1)S(1)}, u32[]{:S(2)}, u32[]{:S(2)}) collective-permute-start(bf16[256,1024]{1,0:T(8,128)(2,1)S(1)} %add_convert_fusion.2), channel_id=1, source_target_pairs={{0,2},{1,3},{2,0},{3,1},{4,6},{5,7},{6,4},{7,5},{8,10},{9,11},{10,... | collective-permute-start | bytes 1572872 | tf_op jit(solution)/shard_map/ppermute | solution.py:66
  315.6 24.1 %collective-permute-start.43 = (bf16[256,1024]{1,0:T(8,128)(2,1)}, bf16[256,1024]{1,0:T(8,128)(2,1)S(1)}, u32[]{:S(2)}, u32[]{:S(2)}) collective-permute-start(bf16[256,1024]{1,0:T(8,128)(2,1)} %get-tuple-element.182), channel_id=1, source_target_pairs={{0,1},{1,0},{2,3},{3,2},{4,5},{5,4},{6,7},{7,6},{8,9},{9,8},{10,11... | collective-permute-start | bytes 1572872 | tf_op jit(solution)/shard_map/ppermute | solution.py:66
  317.8 30.4 %collective-permute-start.46 = (bf16[2,784,128]{2,1,0:T(8,128)(2,1)S(1)}, bf16[2,784,128]{2,1,0:T(8,128)(2,1)S(1)}, u32[]{:S(2)}, u32[]{:S(2)}) collective-permute-start(bf16[2,784,128]{2,1,0:T(8,128)(2,1)S(1)} %slice.175), channel_id=1, source_target_pairs={{0,8},{4,12},{8,0},{12,4},{16,24},{20,28},{24,16},{28,20},{1,9},{5... | collective-permute-start | bytes 1204232 | tf_op jit(solution)/shard_map/ppermute | solution.py:100
  339.7 8.6 %collective-permute-start.50 = (bf16[256,128]{1,0:T(8,128)(2,1)S(1)}, bf16[256,128]{1,0:T(8,128)(2,1)S(1)}, u32[]{:S(2)}, u32[]{:S(2)}) collective-permute-start(bf16[256,128]{1,0:T(8,128)(2,1)S(1)} %get-tuple-element.198), channel_id=1, source_target_pairs={{0,3},{1,2},{2,1},{3,0},{4,7},{5,6},{6,5},{7,4},{8,11},{9,10},{10,... | collective-permute-start | bytes 196616 | tf_op jit(solution)/shard_map/ppermute | solution.py:66
  341.0 7.3 %collective-permute-start.49 = (bf16[256,128]{1,0:T(8,128)(2,1)S(1)}, bf16[256,128]{1,0:T(8,128)(2,1)S(1)}, u32[]{:S(2)}, u32[]{:S(2)}) collective-permute-start(bf16[256,128]{1,0:T(8,128)(2,1)S(1)} %get-tuple-element.199), channel_id=1, source_target_pairs={{0,2},{1,3},{2,0},{3,1},{4,6},{5,7},{6,4},{7,5},{8,10},{9,11},{10,... | collective-permute-start | bytes 196616 | tf_op jit(solution)/shard_map/ppermute | solution.py:66
  342.3 6.0 %collective-permute-start.48 = (bf16[256,128]{1,0:T(8,128)(2,1)S(1)}, bf16[256,128]{1,0:T(8,128)(2,1)S(1)}, u32[]{:S(2)}, u32[]{:S(2)}) collective-permute-start(bf16[256,128]{1,0:T(8,128)(2,1)S(1)} %get-tuple-element.197), channel_id=1, source_target_pairs={{0,1},{1,0},{2,3},{3,2},{4,5},{5,4},{6,7},{7,6},{8,9},{9,8},{10,11... | collective-permute-start | bytes 196616 | tf_op jit(solution)/shard_map/ppermute | solution.py:66
  348.3 11.3 %collective-permute-start.47 = (bf16[1,784,128]{2,1,0:T(8,128)(2,1)S(1)}, bf16[1,784,128]{2,1,0:T(8,128)(2,1)S(1)}, u32[]{:S(2)}, u32[]{:S(2)}) collective-permute-start(bf16[1,784,128]{2,1,0:T(8,128)(2,1)S(1)} %slice.144), channel_id=1, source_target_pairs={{0,16},{4,20},{8,24},{12,28},{16,0},{20,4},{24,8},{28,12},{1,17},{... | collective-permute-start | bytes 602120 | tf_op jit(solution)/shard_map/ppermute | solution.py:100
  (40 other events, 183.9 us)
Sparse Core Ops, SparseCore 0:
  10.6 102.8 all-gather.2
  237.7 128.6 reduce-scatter.1
